TPU v7x, 32 devices: a whole 2x2x4 slice. The times are simulated.
32 devices in a mesh: inp: 4 (over z), wt: 4 (over x, core), dep: 2 (over y).
Axes of the slice: x: 2, y: 2, z: 4, core: 2. Of those that a mesh axis runs over, the one named last changes fastest.
Arguments:
- x_saved: bfloat16 [1024, 8192], P(('wt', 'dep'), 'inp'), may hold values from -6 to 6
- out_grad: bfloat16 [1024, 8192], P(('wt', 'dep'), 'inp'), may hold values from -6 to 6
- gate_pre: bfloat16 [1024, 29568], P('inp', ('wt', 'dep')), may hold values from -6 to 6
- up_pre: bfloat16 [1024, 29568], P('inp', ('wt', 'dep')), may hold values from -6 to 6
- w_gate: bfloat16 [8192, 29568], P('inp', ('wt', 'dep')), may hold values from -0.0625 to 0.0625
- w_up: bfloat16 [8192, 29568], P('inp', ('wt', 'dep')), may hold values from -0.0625 to 0.0625
- w_down: bfloat16 [29568, 8192], P(('wt', 'dep'), 'inp'), may hold values from -0.03125 to 0.03125
Outputs:
- input_grad: bfloat16 [1024, 8192], P(('wt', 'dep'), 'inp')
- gate_wgrad: bfloat16 [8192, 29568], P('inp', ('wt', 'dep'))
- up_wgrad: bfloat16 [8192, 29568], P('inp', ('wt', 'dep'))
- down_wgrad: bfloat16 [29568, 8192], P(('wt', 'dep'), 'inp')
All inputs are finite; a program needn't handle non-finite values.
Results may differ from a plain program's by a relative error of at most 0.005.
Values may be sent and summed in bfloat16 or wider, within the bound.
No kernel may reach another device: no remote copies, remote signals or barrier semaphores. Data moves between devices by JAX's collectives and lax.ppermute only.
A program may use at most 192 MiB of HBM per device.

v0:
```python
import jax
import jax.numpy as jnp
from jax import lax
from jax.sharding import PartitionSpec as P


def contract_rows(left, right):
    return lax.dot_general(
        left, right, (((0,), (0,)), ((), ())), preferred_element_type=jnp.float32
    )


def contract_cols(left, right):
    return lax.dot_general(
        left, right, (((1,), (1,)), ((), ())), preferred_element_type=jnp.float32
    )


def gated_step(hidden_grad, gate_pre, up_pre):
    gate = gate_pre.astype(jnp.float32)
    upper = up_pre.astype(jnp.float32)
    sigma = jax.nn.sigmoid(gate)
    active = gate * sigma
    hidden = (active * upper).astype(jnp.bfloat16)
    up_act_grad = (hidden_grad * active).astype(jnp.bfloat16)
    gate_act_grad = (hidden_grad * upper * sigma * (1.0 + gate * (1.0 - sigma))).astype(
        jnp.bfloat16
    )
    return (hidden, gate_act_grad, up_act_grad)


def per_device(x_saved, out_grad, gate_pre, up_pre, w_gate, w_up, w_down):
    x_whole, grad_whole = (
        lax.all_gather(x_saved, ("wt", "dep"), axis=0, tiled=True),
        lax.all_gather(out_grad, ("wt", "dep"), axis=0, tiled=True),
    )
    hidden_share = lax.psum_scatter(
        contract_cols(grad_whole, w_down), "inp", scatter_dimension=0, tiled=True
    )
    hidden_part, gate_part, up_part = gated_step(hidden_share, gate_pre, up_pre)
    hidden, gate_act_grad, up_act_grad = (
        lax.all_gather(hidden_part, "inp", axis=0, tiled=True),
        lax.all_gather(gate_part, "inp", axis=0, tiled=True),
        lax.all_gather(up_part, "inp", axis=0, tiled=True),
    )
    down_wgrad = contract_rows(hidden, grad_whole).astype(jnp.bfloat16)
    gate_wgrad = contract_rows(x_whole, gate_act_grad).astype(jnp.bfloat16)
    up_wgrad = contract_rows(x_whole, up_act_grad).astype(jnp.bfloat16)
    input_grad = lax.psum_scatter(
        contract_cols(gate_act_grad, w_gate) + contract_cols(up_act_grad, w_up),
        ("wt", "dep"),
        scatter_dimension=0,
        tiled=True,
    )
    return (input_grad.astype(jnp.bfloat16), gate_wgrad, up_wgrad, down_wgrad)


def solution(mesh):
    placed = (
        P(("wt", "dep"), "inp"),
        P(("wt", "dep"), "inp"),
        P("inp", ("wt", "dep")),
        P("inp", ("wt", "dep")),
        P("inp", ("wt", "dep")),
        P("inp", ("wt", "dep")),
        P(("wt", "dep"), "inp"),
    )
    return jax.shard_map(
        per_device,
        mesh=mesh,
        in_specs=placed,
        out_specs=(
            P(("wt", "dep"), "inp"),
            P("inp", ("wt", "dep")),
            P("inp", ("wt", "dep")),
            P(("wt", "dep"), "inp"),
        ),
        check_vma=False,
    )
```

profile of v0, /device:TPU:1, one launch (start us, length us, event | category | flops | bytes accessed | tf_op | source)
XLA Modules:
  0.0 859.5 jit_solution(13552907768000546049)
XLA Ops:
  7.2 0.0 all-gather.6.cloned.1.call-start
  7.2 0.7 all-gather.6.cloned.1.call-update
  7.9 0.0 reduce-scatter.3.cloned.1.call-start
  7.9 41.2 %all-gather.6.cloned.1.call-done = bf16[1024,2048]{1,0:T(8,128)(2,1)} async-done(((bf16[128,2048]{1,0:T(8,128)(2,1)}), bf16[1024,2048]{1,0:T(8,128)(2,1)}) %all-gather.6.cloned.1.call-update) | async-done | bytes 4194320 | tf_op jit(solution)/shard_map/all_gather | solution.py:35
  49.1 21.7 %fusion.8 = f32[1024,3696]{0,1:T(8,128)} fusion(bf16[1024,2048]{1,0:T(8,128)(2,1)} %all-gather.6.cloned.1.call-done, bf16[3696,2048]{1,0:T(8,128)(2,1)} %param.13), kind=kOutput, calls=%fused_computation.18 | convolution fusion | flops 15502147584 | bytes 34471936 | tf_op jit(solution)/shard_map/dot_general | solution.py:14
  70.9 0.0 copy-start
  70.9 0.0 reduce-scatter.3.cloned.1.call-update
  70.9 0.0 all-gather.8.cloned.1.call-start
  71.0 252.8 %reduce-scatter.3.cloned.1.call-done = f32[256,3696]{0,1:T(8,128)} async-done(((f32[1024,3696]{0,1:T(8,128)}), f32[256,3696]{0,1:T(8,128)}) %reduce-scatter.3.cloned.1.call-update) | async-done | bytes 3784720 | tf_op jit(solution)/shard_map/reduce_scatter | solution.py:37
  323.8 0.0 copy-done
  323.8 6.3 multiply_convert_fusion
  330.1 0.0 all-gather.8.cloned.1.call-update
  330.2 0.0 all-gather.10.cloned.1.call-start
  330.2 0.5 all-gather.10.cloned.1.call-update
  330.7 0.0 all-gather.12.cloned.1.call-start
  330.8 0.5 all-gather.12.cloned.1.call-update
  331.3 0.0 all-gather.14.cloned.1.call-start
  331.4 0.5 all-gather.14.cloned.1.call-update
  331.9 0.2 reduce-scatter.5.cloned.1.call-start
  332.1 135.0 %all-gather.8.cloned.1.call-done = bf16[1024,3696]{0,1:T(8,128)(2,1)} async-done(((bf16[256,3696]{0,1:T(8,128)(2,1)}), bf16[1024,3696]{0,1:T(8,128)(2,1)}) %all-gather.8.cloned.1.call-update) | async-done | bytes 7569424 | tf_op jit(solution)/shard_map/all_gather | solution.py:43
  467.2 22.7 %fusion.9 = f32[1024,2048]{1,0:T(8,128)} fusion(bf16[1024,3696]{0,1:T(8,128)(2,1)} %all-gather.8.cloned.1.call-done, bf16[2048,3696]{0,1:T(8,128)(2,1)} %param.11), kind=kOutput, calls=%fused_computation.19 | convolution fusion | flops 15502147584 | bytes 31096832 | tf_op jit(solution)/shard_map/dot_general | solution.py:14
  489.9 113.3 %all-gather.10.cloned.1.call-done = bf16[1024,3696]{0,1:T(8,128)(2,1)} async-done(((bf16[256,3696]{0,1:T(8,128)(2,1)}), bf16[1024,3696]{0,1:T(8,128)(2,1)}) %all-gather.10.cloned.1.call-update) | async-done | bytes 7569424 | tf_op jit(solution)/shard_map/all_gather | solution.py:44
  603.2 23.4 %convolution_add_fusion = f32[1024,2048]{1,0:T(8,128)} fusion(f32[1024,2048]{1,0:T(8,128)} %fusion.9, bf16[1024,3696]{0,1:T(8,128)(2,1)} %all-gather.10.cloned.1.call-done, bf16[2048,3696]{0,1:T(8,128)(2,1)} %param.12), kind=kOutput, calls=%fused_computation.8 | convolution fusion | flops 15504244736 | bytes 39485440 | tf_op jit(solution)/shard_map/dot_general | solution.py:14
  626.6 0.0 reduce-scatter.5.cloned.1.call-update
  626.6 13.7 %all-gather.12.cloned.1.call-done = bf16[1024,2048]{1,0:T(8,128)(2,1)} async-done(((bf16[128,2048]{1,0:T(8,128)(2,1)}), bf16[1024,2048]{1,0:T(8,128)(2,1)}) %all-gather.12.cloned.1.call-update) | async-done | bytes 4194320 | tf_op jit(solution)/shard_map/all_gather | solution.py:34
  640.3 0.0 copy-start.1
  640.3 22.0 %convert_bitcast_fusion = bf16[2048,3696]{0,1:T(8,128)(2,1)} fusion(bf16[1024,3696]{0,1:T(8,128)(2,1)} %all-gather.10.cloned.1.call-done, bf16[1024,2048]{1,0:T(8,128)(2,1)} %all-gather.12.cloned.1.call-done), kind=kOutput, calls=%fused_computation | convolution fusion | flops 15509716992 | bytes 26902528 | tf_op jit(solution)/shard_map/dot_general | solution.py:8
  662.3 0.0 copy-done.1
  662.3 21.5 %convert_bitcast_fusion.1 = bf16[2048,3696]{0,1:T(8,128)(2,1)} fusion(bf16[1024,3696]{0,1:T(8,128)(2,1)} %all-gather.8.cloned.1.call-done, bf16[1024,2048]{1,0:T(8,128)(2,1)S(1)} %copy-done.1), kind=kOutput, calls=%fused_computation.1 | convolution fusion | flops 15509716992 | bytes 26902528 | tf_op jit(solution)/shard_map/dot_general | solution.py:8
  683.9 93.4 %all-gather.14.cloned.1.call-done = bf16[1024,3696]{0,1:T(8,128)(2,1)} async-done(((bf16[256,3696]{0,1:T(8,128)(2,1)}), bf16[1024,3696]{0,1:T(8,128)(2,1)}) %all-gather.14.cloned.1.call-update) | async-done | bytes 7569424 | tf_op jit(solution)/shard_map/all_gather | solution.py:42
  777.3 21.5 %convolution_convert_fusion = bf16[3696,2048]{1,0:T(8,128)(2,1)} fusion(bf16[1024,3696]{0,1:T(8,128)(2,1)} %all-gather.14.cloned.1.call-done, bf16[1024,2048]{1,0:T(8,128)(2,1)} %all-gather.6.cloned.1.call-done), kind=kOutput, calls=%fused_computation.2 | convolution fusion | flops 15509716992 | bytes 26902528 | tf_op jit(solution)/shard_map/dot_general | solution.py:8
  798.8 51.8 %reduce-scatter.5.cloned.1.call-done = f32[128,2048]{1,0:T(8,128)} async-done(((f32[1024,2048]{1,0:T(8,128)}), f32[128,2048]{1,0:T(8,128)}) %reduce-scatter.5.cloned.1.call-update) | async-done | bytes 1048592 | tf_op jit(solution)/shard_map/reduce_scatter | solution.py:49
  850.5 2.1 convert_element_type.37
Async XLA Ops:
  7.2 42.0 %all-gather.6.cloned.1.call-start = ((), (), s32[]{:S(2)}) async-start(), calls=%async_computation.2 | async-start | bytes 4718592 | tf_op jit(solution)/shard_map/all_gather | solution.py:35
  7.9 315.9 %reduce-scatter.3.cloned.1.call-start = ((), (), s32[]{:S(2)}) async-start(), calls=%async_computation.3 | async-start | bytes 18923520 | tf_op jit(solution)/shard_map/reduce_scatter | solution.py:37
  70.9 252.9 %copy-start = (bf16[256,3696]{0,1:T(8,128)(2,1)S(1)}, bf16[256,3696]{0,1:T(8,128)(2,1)}, u32[]{:S(2)}) copy-start(bf16[256,3696]{0,1:T(8,128)(2,1)} %param.9) | copy-start | bytes 5677060
  70.9 396.3 %all-gather.8.cloned.1.call-start = ((), (), s32[]{:S(2)}) async-start(), calls=%async_computation.4 | async-start | bytes 9461760 | tf_op jit(solution)/shard_map/all_gather | solution.py:43
  330.2 273.0 %all-gather.10.cloned.1.call-start = ((), (), s32[]{:S(2)}) async-start(), calls=%async_computation.5 | async-start | bytes 9461760 | tf_op jit(solution)/shard_map/all_gather | solution.py:44
  330.7 309.6 %all-gather.12.cloned.1.call-start = ((), (), s32[]{:S(2)}) async-start(), calls=%async_computation.7 | async-start | bytes 4718592 | tf_op jit(solution)/shard_map/all_gather | solution.py:34
  331.3 446.0 %all-gather.14.cloned.1.call-start = ((), (), s32[]{:S(2)}) async-start(), calls=%async_computation.8 | async-start | bytes 9461760 | tf_op jit(solution)/shard_map/all_gather | solution.py:42
  331.9 518.6 %reduce-scatter.5.cloned.1.call-start = ((), (), s32[]{:S(2)}) async-start(), calls=%async_computation.6 | async-start | bytes 9437184 | tf_op jit(solution)/shard_map/reduce_scatter | solution.py:49
  640.3 22.0 %copy-start.1 = (bf16[1024,2048]{1,0:T(8,128)(2,1)S(1)}, bf16[1024,2048]{1,0:T(8,128)(2,1)}, u32[]{:S(2)}) copy-start(bf16[1024,2048]{1,0:T(8,128)(2,1)} %all-gather.12.cloned.1.call-done) | copy-start | bytes 12582916
Sparse Core Ops, SparseCore 0:
  9.9 39.2 all-gather.5
  71.0 252.7 reduce-scatter.2
  330.3 136.8 all-gather.7
  469.2 133.9 all-gather.9
  605.1 35.1 all-gather.11
  641.8 135.4 all-gather.13
  781.1 69.3 reduce-scatter.4
where the time goes:
time: 860 us; the launch traced here: 859 us
  waiting for transfers between devices  704 us (82%)
  matrix products  133 us (15%)
  between operations  14.1 us (2%)
    reduce_scatter x1, waiting for transfers between devices, per_device(): lax.psum_scatter(contract_cols(grad_whole, w_down), 'inp', scatter_dimens...  253 us
    all_gather x1, waiting for transfers between devices, per_device(): lax.all_gather(gate_part, 'inp', axis=0, tiled=True)  135 us
    all_gather x1, waiting for transfers between devices, per_device(): lax.all_gather(up_part, 'inp', axis=0, tiled=True)  113 us
    all_gather x1, waiting for transfers between devices, per_device(): lax.all_gather(hidden_part, 'inp', axis=0, tiled=True)  93.4 us
    dot_general x3, matrix products, contract_cols(): lax.dot_general(left, right, (((1,), (1,)), ((), ())), preferred_element_...  67.8 us
    dot_general x3, matrix products, contract_rows(): lax.dot_general(left, right, (((0,), (0,)), ((), ())), preferred_element_...  65 us
    reduce_scatter x1, waiting for transfers between devices, per_device(): lax.psum_scatter(contract_cols(gate_act_grad, w_gate) + contract_cols(up_...  51.8 us
    all_gather x1, waiting for transfers between devices, per_device(): lax.all_gather(out_grad, ('wt', 'dep'), axis=0, tiled=True)  41.2 us
  transfers between devices with their start and end apart: 7, of which 7 were waited for; matrix products, arithmetic and copies ran while one was open for 13% of the time, Pallas kernels for 0%

commit v1 on v0

v1 whole, which is shorter than its diff:
```python
import functools

import jax
import jax.numpy as jnp
from jax import lax
from jax.experimental import pallas as pl
from jax.experimental.pallas import tpu as pltpu
from jax.sharding import PartitionSpec as P

GROUPS = 4
VMEM_LIMIT = 60 * 1024 * 1024

SWAP = [(0, 1), (1, 0), (2, 3), (3, 2)]
MIDDLE = [(1, 2), (2, 1)]
TO_ENDS = [(1, 0), (2, 3)]


def send(value, pairs):
    return lax.ppermute(value, "inp", pairs)


def block_rows(rows):
    units = rows // 16
    return 16 * max(n for n in range(1, 33) if units % n == 0)


def sum_kernel(w_ref, grad_ref, out_ref):
    count, _, width = out_ref.shape
    for j in range(count):
        out_ref[j] = lax.dot_general(
            w_ref[...],
            grad_ref[j * width : (j + 1) * width, :],
            (((1,), (1,)), ((), ())),
            preferred_element_type=jnp.float32,
        )


def slot_value(end, refs, slot):
    if slot == 0:
        return refs[0][...].astype(jnp.float32)
    if slot == 1:
        return refs[1][...].astype(jnp.float32)
    at_end, at_middle = refs[2:4] if slot == 2 else refs[4:6]
    return jnp.where(end, at_end[...], at_middle[...]).astype(jnp.float32)


def place(k_ref, slot):
    return k_ref[0] ^ slot


def columns(index, width):
    return pl.ds(pl.multiple_of(index * width, width), width)


def valid_rows(value, rows, block):
    at = lax.broadcasted_iota(jnp.int32, value.shape, 0) + pl.program_id(0) * block
    return jnp.where(at < rows, value, jnp.zeros_like(value))


def down_kernel(k_ref, *refs):
    gates, uppers = refs[:6], refs[6:12]
    grad_ref, out_ref, hidden = refs[12], refs[-2], refs[-1]
    width = gates[0].shape[1]
    end = k_ref[1] == 1
    for slot in range(4):
        gate, upper = slot_value(end, gates, slot), slot_value(end, uppers, slot)
        value = gate * jax.nn.sigmoid(gate) * upper
        hidden[:, columns(place(k_ref, slot), width)] = value.astype(jnp.bfloat16)
    features = grad_ref.shape[1]
    step = min(features, 512)
    for c in range(0, features, step):
        cols = slice(c, c + step)
        out_ref[:, cols] = jnp.dot(
            hidden[...], grad_ref[:, cols], preferred_element_type=jnp.float32
        ).astype(jnp.bfloat16)


def main_kernel(rows, has_acc, k_ref, *refs):
    gates, uppers = refs[:6], refs[6:12]
    part, r1, r2, r3, x_ref, wg_ref, wu_ref = refs[12:19]
    acc_in = refs[19] if has_acc else None
    acc, gate_out, up_out, gate_grad, up_grad = refs[-5:]
    block, width = gates[0].shape
    ragged = rows % block != 0
    end = k_ref[1] == 1
    for slot in range(4):
        gate, upper = slot_value(end, gates, slot), slot_value(end, uppers, slot)
        j = place(k_ref, slot)
        at = columns(j, width)
        hidden_grad = (
            part[j]
            + r2[j].astype(jnp.float32)
            + jnp.where(end, r3[j], r1[j]).astype(jnp.float32)
        )
        sigma = jax.nn.sigmoid(gate)
        up_value = (hidden_grad * (gate * sigma)).astype(jnp.bfloat16)
        gate_value = (
            hidden_grad * upper * sigma * (1.0 + gate * (1.0 - sigma))
        ).astype(jnp.bfloat16)
        if ragged:
            up_value = valid_rows(up_value, rows, block)
            gate_value = valid_rows(gate_value, rows, block)
        up_grad[:, at] = up_value
        gate_grad[:, at] = gate_value

    @pl.when(pl.program_id(0) == 0)
    def _():
        if has_acc:
            acc[...] = acc_in[...]
        else:
            acc[...] = jnp.zeros_like(acc)

    features = x_ref.shape[1]
    step = min(features, 512)
    for c in range(0, features, step):
        cols = slice(c, c + step)
        gate_out[:, cols] = jnp.dot(
            gate_grad[...], x_ref[:, cols], preferred_element_type=jnp.float32
        ).astype(jnp.bfloat16)
        up_out[:, cols] = jnp.dot(
            up_grad[...], x_ref[:, cols], preferred_element_type=jnp.float32
        ).astype(jnp.bfloat16)
        wg, wu = wg_ref[:, cols], wu_ref[:, cols]
        if ragged:
            wg, wu = valid_rows(wg, rows, block), valid_rows(wu, rows, block)
        dims = (((0,), (0,)), ((), ()))
        acc[:, cols] += lax.dot_general(
            gate_grad[...], wg, dims, preferred_element_type=jnp.float32
        ) + lax.dot_general(
            up_grad[...], wu, dims, preferred_element_type=jnp.float32
        )


def once(shape):
    return pl.BlockSpec(shape, lambda i, *k: (0, 0), pipeline_mode=pl.Buffered(1))


def sum_group(w_down, grad_whole, a, size, count):
    tokens, features = grad_whole.shape
    block = block_rows(size)
    blocks = size // block
    width = tokens // count
    return pl.pallas_call(
        sum_kernel,
        grid=(blocks,),
        in_specs=[
            pl.BlockSpec((block, features), lambda i: (a * blocks + i, 0)),
            once((tokens, features)),
        ],
        out_specs=pl.BlockSpec((count, block, width), lambda i: (0, i, 0)),
        out_shape=jax.ShapeDtypeStruct((count, size, width), jnp.float32),
        compiler_params=pltpu.CompilerParams(vmem_limit_bytes=VMEM_LIMIT),
        cost_estimate=pl.CostEstimate(
            flops=2 * size * tokens * features,
            bytes_accessed=size * (features * 2 + tokens * 4),
            transcendentals=0,
        ),
    )(w_down, grad_whole)


def slot_specs(a, block, width):
    gate = pl.BlockSpec((None, block, width), lambda i, k: (a % 2, i, 0))
    upper = pl.BlockSpec((None, block, width), lambda i, k: (2 + a % 2, i, 0))
    return [gate] * 6 + [upper] * 6


def down_group(k, slots, grad_whole, out, a, size, total):
    tokens, features = grad_whole.shape
    width = slots[0].shape[2]
    block = block_rows(size)
    blocks = size // block
    specs = slot_specs(a, block, width) + [once((tokens, features))]
    args = list(slots) * 2 + [grad_whole]
    aliases = {}
    if out is not None:
        aliases[1 + len(args)] = 0
        args.append(out)
        specs.append(pl.BlockSpec(memory_space=pl.ANY))
    return pl.pallas_call(
        down_kernel,
        grid_spec=pltpu.PrefetchScalarGridSpec(
            num_scalar_prefetch=1,
            grid=(blocks,),
            in_specs=specs,
            out_specs=pl.BlockSpec(
                (block, features), lambda i, k: (a * blocks + i, 0)
            ),
            scratch_shapes=[pltpu.VMEM((block, tokens), jnp.bfloat16)],
        ),
        out_shape=jax.ShapeDtypeStruct((total, features), jnp.bfloat16),
        input_output_aliases=aliases,
        compiler_params=pltpu.CompilerParams(vmem_limit_bytes=VMEM_LIMIT),
        cost_estimate=pl.CostEstimate(
            flops=2 * size * tokens * features,
            bytes_accessed=size * (features * 2 + tokens * 4),
            transcendentals=size * tokens,
        ),
    )(k, *args)


def main_group(k, slots, sums, x_whole, wg, wu, acc, outs, a, size, total):
    tokens, features = x_whole.shape
    count, _, width = slots[0].shape
    block = block_rows(size)
    blocks = size // block
    wide = pl.BlockSpec((count, block, width), lambda i, k: (0, i, 0))
    weight = pl.BlockSpec((block, features), lambda i, k: (a * blocks + i, 0))
    specs = (
        slot_specs(a, block, width)
        + [wide] * 4
        + [once((tokens, features)), weight, weight]
    )
    args = list(slots) * 2 + list(sums) + [x_whole, wg, wu]
    aliases = {}
    if acc is not None:
        aliases[1 + len(args)] = 0
        args.append(acc)
        specs.append(once((tokens, features)))
        for i, out in enumerate(outs):
            aliases[1 + len(args)] = 1 + i
            args.append(out)
            specs.append(pl.BlockSpec(memory_space=pl.ANY))
    wgrad = jax.ShapeDtypeStruct((total, features), jnp.bfloat16)
    rows = min(size, total - a * size)
    return pl.pallas_call(
        functools.partial(main_kernel, rows, acc is not None),
        grid_spec=pltpu.PrefetchScalarGridSpec(
            num_scalar_prefetch=1,
            grid=(blocks,),
            in_specs=specs,
            out_specs=(once((tokens, features)), weight, weight),
            scratch_shapes=[pltpu.VMEM((block, tokens), jnp.bfloat16)] * 2,
        ),
        out_shape=(
            jax.ShapeDtypeStruct((tokens, features), jnp.float32),
            wgrad,
            wgrad,
        ),
        input_output_aliases=aliases,
        compiler_params=pltpu.CompilerParams(vmem_limit_bytes=VMEM_LIMIT),
        cost_estimate=pl.CostEstimate(
            flops=8 * size * tokens * features,
            bytes_accessed=size * (features * 8 + tokens * 14),
            transcendentals=size * tokens,
        ),
    )(k, *args)


def scatter_axis(value, axis, name, size):
    me = lax.axis_index(name)
    bit = 1
    while bit < size:
        shape = value.shape
        high = size // (2 * bit)
        view = value.reshape(shape[:axis] + (high, 2) + shape[axis + 1 :])
        mine = (me // bit) % 2
        pairs = [(i, i ^ bit) for i in range(size)]
        away = lax.dynamic_index_in_dim(view, 1 - mine, axis + 1, keepdims=False)
        kept = lax.dynamic_index_in_dim(view, mine, axis + 1, keepdims=False)
        got = lax.ppermute(away.astype(jnp.bfloat16), name, pairs)
        value = kept.astype(jnp.float32) + got.astype(jnp.float32)
        bit *= 2
    return value.reshape(value.shape[:axis] + value.shape[axis + 1 :])


def own_half(gate, upper, half, size):
    first, last = 2 * half * size, 2 * (half + 1) * size
    parts = []
    for whole in (gate, upper):
        part = whole[first : min(last, whole.shape[0])]
        part = jnp.pad(part, ((0, last - first - part.shape[0]), (0, 0)))
        parts.append(part.reshape(2, size, -1))
    return jnp.concatenate(parts, axis=0)


def per_device(n_wt, n_dep, x_saved, out_grad, gate_pre, up_pre, w_gate, w_up, w_down):
    index = lax.axis_index("inp")
    end = (index == 0) | (index == 3)
    k = jnp.stack([index, end]).astype(jnp.int32)
    total = w_down.shape[0]
    size = 16 * -(-total // (16 * GROUPS))
    gate, upper = gate_pre.T, up_pre.T
    wg, wu = w_gate.T, w_up.T

    def rounded(part, got):
        return (part + got.astype(jnp.float32)).astype(jnp.bfloat16)

    own = [own_half(gate, upper, half, size) for half in range(2)]
    swap, middle = [], []
    for step in range(2):
        swap.append(send(own[step], SWAP))
        middle.append(send(own[step], MIDDLE))
    x_whole, grad_whole = (
        lax.all_gather(x_saved, ("wt", "dep"), axis=0, tiled=True),
        lax.all_gather(out_grad, ("wt", "dep"), axis=0, tiled=True),
    )
    part = [sum_group(w_down, grad_whole, a, size, 4) for a in range(GROUPS)]
    for step in range(2, 10):
        if step < 6:
            outward = part[step - 2].astype(jnp.bfloat16)
            payload = jnp.where(end, outward, middle[step - 2])
            swap.append(send(payload, SWAP))
        else:
            swap.append(send(rounded(part[step - 6], middle[step - 2]), TO_ENDS))
        if step < 4:
            middle.append(send(swap[step - 2], MIDDLE))
        elif step < 8:
            middle.append(send(rounded(part[step - 4], swap[step - 2]), MIDDLE))

    down = None
    acc, wgrads = None, (None, None)
    for a in range(GROUPS):
        h = a // 2
        slots = [own[h], swap[h], swap[2 + h], middle[2 + h], swap[4 + h], middle[h]]
        down = down_group(k, slots, grad_whole, down, a, size, total)
        sums = [part[a], swap[2 + a], middle[4 + a], swap[6 + a]]
        acc, *wgrads = main_group(
            k, slots, sums, x_whole, wg, wu, acc, wgrads, a, size, total
        )
    gate_wgrad, up_wgrad = wgrads

    tokens, features = acc.shape
    view = acc.reshape(n_wt, n_dep, tokens // (n_wt * n_dep), features)
    input_grad = scatter_axis(view, 0, "wt", n_wt)
    input_grad = scatter_axis(input_grad, 0, "dep", n_dep)
    return (input_grad.astype(jnp.bfloat16), gate_wgrad.T, up_wgrad.T, down)


def solution(mesh):
    placed = (
        P(("wt", "dep"), "inp"),
        P(("wt", "dep"), "inp"),
        P("inp", ("wt", "dep")),
        P("inp", ("wt", "dep")),
        P("inp", ("wt", "dep")),
        P("inp", ("wt", "dep")),
        P(("wt", "dep"), "inp"),
    )
    return jax.shard_map(
        functools.partial(per_device, mesh.shape["wt"], mesh.shape["dep"]),
        mesh=mesh,
        in_specs=placed,
        out_specs=(
            P(("wt", "dep"), "inp"),
            P("inp", ("wt", "dep")),
            P("inp", ("wt", "dep")),
            P(("wt", "dep"), "inp"),
        ),
        check_vma=False,
    )
```

time: 860 us -> 598 us (0.70); the launches traced: 859 us -> 587 us
  waiting for transfers between devices: 704 us -> 237 us
  Pallas kernels: 0 us -> 211 us
  matrix products: 133 us -> 0 us
  starting transfers between devices: 0.45 us -> 74.8 us
  other arithmetic: 8.41 us -> 41 us
  local copies, waits for them, and re-layouts: 0.01 us -> 9.15 us
    all_gather x3 -> x0, waiting for transfers between devices: 342 us -> none  [the longest x1 135 us: per_device(): lax.all_gather(gate_part, 'inp', axis=0, tiled=True)]
    reduce_scatter x2 -> x0, waiting for transfers between devices: 305 us -> none  [the longest x1 253 us: per_device(): lax.psum_scatter(contract_cols(grad_whole, w_down), 'inp', scatter_dimens...]
    ppermute x0 -> x21, waiting for transfers between devices: none -> 236 us  [the longest x18 232 us: send(): return lax.ppermute(value, 'inp', pairs)]
    pallas_call x0 -> x12, Pallas kernels: none -> 211 us  [the longest x4 133 us: main_group(): pl.pallas_call(functools.partial(main_kernel, rows, acc is not None), gri...]
    dot_general x6 -> x0, matrix products: 133 us -> none  [the longest x3 67.8 us: contract_cols(): lax.dot_general(left, right, (((1,), (1,)), ((), ())), preferred_element_...]
    ppermute x0 -> x21, starting transfers between devices: none -> 74.7 us  [the longest x18 68.7 us: send(): return lax.ppermute(value, 'inp', pairs)]
    all_gather x1, waiting for transfers between devices: 41.2 us -> 0.01 us  [per_device(): lax.all_gather(out_grad, ('wt', 'dep'), axis=0, tiled=True)]
    all_gather x1, waiting for transfers between devices: 13.7 us -> 0.02 us  [per_device(): lax.all_gather(x_saved, ('wt', 'dep'), axis=0, tiled=True)]
  transfers between devices with their start and end apart: 7 -> 23, of which waited for: 7 -> 10; matrix products, arithmetic and copies ran while one was open for 13% -> 6% of each run, Pallas kernels for 0% -> 30%
where the time goes in v1:
time: 598 us; the launch traced here: 587 us
  waiting for transfers between devices  237 us (40%)
  Pallas kernels  211 us (35%)
  starting transfers between devices  74.8 us (13%)
  other arithmetic  41 us (7%)
  between operations  14.8 us (2%)
  local copies, waits for them, and re-layouts  9.15 us (2%)
    ppermute x18, waiting for transfers between devices, send(): return lax.ppermute(value, 'inp', pairs)  232 us
    pallas_call x4, Pallas kernels, main_group(): pl.pallas_call(functools.partial(main_kernel, rows, acc is not None), gri...  133 us
    ppermute x18, starting transfers between devices, send(): return lax.ppermute(value, 'inp', pairs)  68.7 us
    pallas_call x4, Pallas kernels, down_group(): pl.pallas_call(down_kernel, grid_spec=pltpu.PrefetchScalarGridSpec(num_sc...  44.3 us
    pallas_call x4, Pallas kernels, sum_group(): pl.pallas_call(sum_kernel, grid=(blocks,), in_specs=[pl.BlockSpec((block,...  33.6 us
    convert_element_type x8, other arithmetic, rounded(): return (part + got.astype(jnp.float32)).astype(jnp.bfloat16)  20.5 us
  transfers between devices with their start and end apart: 23, of which 10 were waited for; matrix products, arithmetic and copies ran while one was open for 6% of the time, Pallas kernels for 30%

profile of v1, /device:TPU:1, one launch (start us, length us, event | category | flops | bytes accessed | tf_op | source)
XLA Modules:
  0.0 587.3 jit_solution(13131854652196166893)
XLA Ops:
  10.8 2.2 collective-permute-start
  14.9 2.1 collective-permute-start.7
  17.0 1.9 collective-permute-start.12
  18.9 2.0 collective-permute-start.1
  21.0 33.3 %collective-permute-done.refs_1_.refs_7_ = bf16[4,928,256]{2,1,0:T(8,128)(2,1)} collective-permute-done((bf16[4,928,256]{2,1,0:T(8,128)(2,1)S(1)}, bf16[4,928,256]{2,1,0:T(8,128)(2,1)}, u32[]{:S(2)}, u32[]{:S(2)}) %collective-permute-start) | collective-permute-done | bytes 1900576 | tf_op jit(solution)/shard_map/ppermute | solution.py:19
  54.2 1.9 collective-permute-start.3
  56.1 38.8 %collective-permute-done.7.refs_1_.refs_7_ = bf16[4,928,256]{2,1,0:T(8,128)(2,1)} collective-permute-done((bf16[4,928,256]{2,1,0:T(8,128)(2,1)}, bf16[4,928,256]{2,1,0:T(8,128)(2,1)}, u32[]{:S(2)}, u32[]{:S(2)}) %collective-permute-start.7) | collective-permute-done | bytes 1900576 | tf_op jit(solution)/shard_map/ppermute | solution.py:19
  95.0 1.9 collective-permute-start.8
  96.9 8.4 %shard_map.105.refs_12_ = f32[4,928,256]{2,1,0:T(8,128)} custom-call(bf16[3696,2048]{1,0:T(8,128)(2,1)} %w_ref.7, bf16[1024,2048]{1,0:T(8,128)(2,1)} %all-gather.3.cloned.1.call-done.grad_ref.refs_12_), custom_call_target="tpu_custom_call" | custom-call | flops 3892314112 | bytes 7602176 | tf_op jit(solution)/shard_map/pallas_call | solution.py:143
  105.3 3.6 convert_select_fusion
  108.9 3.0 collective-permute-start.13
  111.9 8.4 %shard_map.102.refs_12_ = f32[4,928,256]{2,1,0:T(8,128)} custom-call(bf16[3696,2048]{1,0:T(8,128)(2,1)} %w_ref.7, bf16[1024,2048]{1,0:T(8,128)(2,1)} %all-gather.3.cloned.1.call-done.grad_ref.refs_12_), custom_call_target="tpu_custom_call" | custom-call | flops 3892314112 | bytes 7602176 | tf_op jit(solution)/shard_map/pallas_call | solution.py:143
  120.3 2.3 convert_select_fusion.3
  123.3 8.4 %shard_map.103.refs_12_ = f32[4,928,256]{2,1,0:T(8,128)} custom-call(bf16[3696,2048]{1,0:T(8,128)(2,1)} %w_ref.7, bf16[1024,2048]{1,0:T(8,128)(2,1)} %all-gather.3.cloned.1.call-done.grad_ref.refs_12_), custom_call_target="tpu_custom_call" | custom-call | flops 3892314112 | bytes 7602176 | tf_op jit(solution)/shard_map/pallas_call | solution.py:143
  131.7 3.6 convert_select_fusion.2
  135.3 13.0 %collective-permute-start.4 = (bf16[4,928,256]{2,1,0:T(8,128)(2,1)}, bf16[4,928,256]{2,1,0:T(8,128)(2,1)}, u32[]{:S(2)}, u32[]{:S(2)}) collective-permute-start(bf16[4,928,256]{2,1,0:T(8,128)(2,1)} %convert_select_fusion.2), channel_id=1, source_target_pairs={{0,8},{8,0},{16,24},{24,16},{1,9},{9,1},{17,25},{25,17},{2,10},{10... | collective-permute-start | bytes 5701640 | tf_op jit(solution)/shard_map/ppermute | solution.py:19
  148.3 8.4 %shard_map.104.refs_12_ = f32[4,928,256]{2,1,0:T(8,128)} custom-call(bf16[3696,2048]{1,0:T(8,128)(2,1)} %w_ref.7, bf16[1024,2048]{1,0:T(8,128)(2,1)} %all-gather.3.cloned.1.call-done.grad_ref.refs_12_), custom_call_target="tpu_custom_call" | custom-call | flops 3892314112 | bytes 7602176 | tf_op jit(solution)/shard_map/pallas_call | solution.py:143
  156.6 2.5 convert_select_fusion.1
  159.1 28.7 %collective-permute-start.9 = (bf16[4,928,256]{2,1,0:T(8,128)(2,1)S(1)}, bf16[4,928,256]{2,1,0:T(8,128)(2,1)S(1)}, u32[]{:S(2)}, u32[]{:S(2)}) collective-permute-start(bf16[4,928,256]{2,1,0:T(8,128)(2,1)S(1)} %convert_select_fusion.1), channel_id=1, source_target_pairs={{0,8},{8,0},{16,24},{24,16},{1,9},{9,1},{17,25},{25,17},{2,10},{10... | collective-permute-start | bytes 5701640 | tf_op jit(solution)/shard_map/ppermute | solution.py:19
  187.8 2.0 add_convert_fusion.1
  190.7 2.0 collective-permute-done.2.refs_13_.refs_2_.refs_8_
  192.8 1.9 add_convert_fusion.3
  194.6 2.1 collective-permute-start.14
  196.7 36.9 %collective-permute-done.4.refs_4_.refs_10_.refs_13_ = bf16[4,928,256]{2,1,0:T(8,128)(2,1)} collective-permute-done((bf16[4,928,256]{2,1,0:T(8,128)(2,1)}, bf16[4,928,256]{2,1,0:T(8,128)(2,1)}, u32[]{:S(2)}, u32[]{:S(2)}) %collective-permute-start.4) | collective-permute-done | bytes 1900576 | tf_op jit(solution)/shard_map/ppermute | solution.py:19
  233.6 3.2 add_convert_fusion.7
  237.8 36.4 %collective-permute-done.9.refs_4_.refs_10_.refs_13_ = bf16[4,928,256]{2,1,0:T(8,128)(2,1)S(1)} collective-permute-done((bf16[4,928,256]{2,1,0:T(8,128)(2,1)S(1)}, bf16[4,928,256]{2,1,0:T(8,128)(2,1)S(1)}, u32[]{:S(2)}, u32[]{:S(2)}) %collective-permute-start.9) | collective-permute-done | bytes 1900576 | tf_op jit(solution)/shard_map/ppermute | solution.py:19
  274.2 1.9 add_convert_fusion.5
  276.1 1.9 collective-permute-start.10
  278.0 1.9 add_convert_fusion
  281.9 4.5 add_convert_fusion.2
  291.2 3.3 add_convert_fusion.4
  295.7 26.9 %collective-permute-done.17.refs_15_ = bf16[4,928,256]{2,1,0:T(8,128)(2,1)} collective-permute-done((bf16[4,928,256]{2,1,0:T(8,128)(2,1)}, bf16[4,928,256]{2,1,0:T(8,128)(2,1)}, u32[]{:S(2)}, u32[]{:S(2)}) %collective-permute-start.17) | collective-permute-done | bytes 1900576 | tf_op jit(solution)/shard_map/ppermute | solution.py:19
  322.6 31.0 %shard_map.106 = (f32[1024,2048]{1,0:T(8,128)}, bf16[3696,2048]{1,0:T(8,128)(2,1)}, bf16[3696,2048]{1,0:T(8,128)(2,1)}) custom-call(s32[2]{0:T(128)} %pad_add_fusion.k_ref, bf16[4,928,256]{2,1,0:T(8,128)(2,1)} %pad_maximum_fusion.1.refs_0_.refs_6_, bf16[4,928,256]{2,1,0:T(8,128)(2,1)} %collective-permute-done.7.refs_1_.refs_7_, ...), custom_call_target="tpu_custom_call" | custom-call | flops 15569256448 | bytes 28508160 | tf_op jit(solution)/shard_map/pallas_call | solution.py:225
  353.7 9.7 %collective-permute-done.15.refs_15_ = bf16[4,928,256]{2,1,0:T(8,128)(2,1)} collective-permute-done((bf16[4,928,256]{2,1,0:T(8,128)(2,1)}, bf16[4,928,256]{2,1,0:T(8,128)(2,1)}, u32[]{:S(2)}, u32[]{:S(2)}) %collective-permute-start.15) | collective-permute-done | bytes 1900576 | tf_op jit(solution)/shard_map/ppermute | solution.py:19
  363.4 33.8 %shard_map.107 = (f32[1024,2048]{1,0:T(8,128)}, bf16[3696,2048]{1,0:T(8,128)(2,1)}, bf16[3696,2048]{1,0:T(8,128)(2,1)}) custom-call(s32[2]{0:T(128)} %pad_add_fusion.k_ref, bf16[4,928,256]{2,1,0:T(8,128)(2,1)} %pad_maximum_fusion.1.refs_0_.refs_6_, ...), custom_call_target="tpu_custom_call", output_to_operand_aliasing={{0}: (20, {}), {1}: (21, {}), {2}: (22, {})} | custom-call | flops 15569256448 | bytes 28508160 | tf_op jit(solution)/shard_map/pallas_call | solution.py:225
  397.2 47.5 %collective-permute-done.11.refs_15_ = bf16[4,928,256]{2,1,0:T(8,128)(2,1)S(1)} collective-permute-done((bf16[4,928,256]{2,1,0:T(8,128)(2,1)}, bf16[4,928,256]{2,1,0:T(8,128)(2,1)S(1)}, u32[]{:S(2)}, u32[]{:S(2)}) %collective-permute-start.11) | collective-permute-done | bytes 1900576 | tf_op jit(solution)/shard_map/ppermute | solution.py:19
  446.0 33.6 %shard_map.108 = (f32[1024,2048]{1,0:T(8,128)}, bf16[3696,2048]{1,0:T(8,128)(2,1)}, bf16[3696,2048]{1,0:T(8,128)(2,1)}) custom-call(s32[2]{0:T(128)} %pad_add_fusion.k_ref, bf16[4,928,256]{2,1,0:T(8,128)(2,1)} %copy-done.2, bf16[4,928,256]{2,1,0:T(8,128)(2,1)} %collective-permute-done.refs_1_.refs_7_, ...), custom_call_target="tpu_custom_call", output_to_operand_aliasing={{0}: (20, {}), {1}: (21, {}), {2}: (22, {})} | custom-call | flops 15569256448 | bytes 28508160 | tf_op jit(solution)/shard_map/pallas_call | solution.py:225
  479.6 34.2 %shard_map.109 = (f32[1024,2048]{1,0:T(8,128)}, bf16[3696,2048]{1,0:T(8,128)(2,1)}, bf16[3696,2048]{1,0:T(8,128)(2,1)}) custom-call(s32[2]{0:T(128)} %pad_add_fusion.k_ref, bf16[4,928,256]{2,1,0:T(8,128)(2,1)} %copy-done.2, bf16[4,928,256]{2,1,0:T(8,128)(2,1)} %collective-permute-done.refs_1_.refs_7_, ...), custom_call_target="tpu_custom_call", output_to_operand_aliasing={{0}: (20, {}), {1}: (21, {}), {2}: (22, {})} | custom-call | flops 15569256448 | bytes 28508160 | tf_op jit(solution)/shard_map/pallas_call | solution.py:225
  513.8 2.5 fusion
  516.4 3.5 collective-permute-start.18
  519.8 3.9 collective-permute-done.18
  523.7 3.4 bitcast_add_fusion
  527.2 2.0 copy-done.9
  530.6 11.4 %shard_map.110.refs_13_ = bf16[3696,2048]{1,0:T(8,128)(2,1)} custom-call(s32[2]{0:T(128)} %pad_add_fusion.k_ref, bf16[4,928,256]{2,1,0:T(8,128)(2,1)} %pad_maximum_fusion.1.refs_0_.refs_6_, bf16[4,928,256]{2,1,0:T(8,128)(2,1)} %collective-permute-done.7.refs_1_.refs_7_, bf16[4,928,256]{2,1,0:T(8,128)(2,1)} %collective-permute-done.13.refs_2_.refs_8_.refs_13_, ...), custom_call_target="tpu_custom_call" | custom-call | flops 3892314112 | bytes 7602176 | tf_op jit(solution)/shard_map/pallas_call | solution.py:179
  542.0 10.8 %shard_map.111.refs_13_ = bf16[3696,2048]{1,0:T(8,128)(2,1)} custom-call(s32[2]{0:T(128)} %pad_add_fusion.k_ref, bf16[4,928,256]{2,1,0:T(8,128)(2,1)} %pad_maximum_fusion.1.refs_0_.refs_6_, bf16[4,928,256]{2,1,0:T(8,128)(2,1)} %collective-permute-done.7.refs_1_.refs_7_, ...), custom_call_target="tpu_custom_call", output_to_operand_aliasing={{}: (14, {})} | custom-call | flops 3892314112 | bytes 7602176 | tf_op jit(solution)/shard_map/pallas_call | solution.py:179
  553.8 1.9 convert_add_fusion
  557.1 11.2 %shard_map.112.refs_13_ = bf16[3696,2048]{1,0:T(8,128)(2,1)} custom-call(s32[2]{0:T(128)} %pad_add_fusion.k_ref, bf16[4,928,256]{2,1,0:T(8,128)(2,1)} %copy-done.2, bf16[4,928,256]{2,1,0:T(8,128)(2,1)} %collective-permute-done.refs_1_.refs_7_, bf16[4,928,256]{2,1,0:T(8,128)(2,1)} %copy-done, ...), custom_call_target="tpu_custom_call", output_to_operand_aliasing={{}: (14, {})} | custom-call | flops 3892314112 | bytes 7602176 | tf_op jit(solution)/shard_map/pallas_call | solution.py:179
  568.3 10.8 %shard_map.113 = bf16[3696,2048]{1,0:T(8,128)(2,1)} custom-call(s32[2]{0:T(128)} %pad_add_fusion.k_ref, bf16[4,928,256]{2,1,0:T(8,128)(2,1)} %copy-done.2, bf16[4,928,256]{2,1,0:T(8,128)(2,1)} %collective-permute-done.refs_1_.refs_7_, bf16[4,928,256]{2,1,0:T(8,128)(2,1)} %copy-done, ...), custom_call_target="tpu_custom_call", output_to_operand_aliasing={{}: (14, {})} | custom-call | flops 3892314112 | bytes 7602176 | tf_op jit(solution)/shard_map/pallas_call | solution.py:179
  (69 shorter events, 21.8 us)
Async XLA Ops:
  7.2 89.7 %all-gather.3.cloned.1.call-start = ((), (), s32[]{:S(2)}) async-start(), calls=%async_computation | async-start | bytes 4718592 | tf_op jit(solution)/shard_map/all_gather | solution.py:295
  7.9 287.8 %all-gather.5.cloned.1.call-start = ((), (), s32[]{:S(2)}) async-start(), calls=%async_computation.1 | async-start | bytes 4718592 | tf_op jit(solution)/shard_map/all_gather | solution.py:294
  10.6 2.4 copy-start.13
  10.6 2.8 copy-start.14
  10.8 8.1 %copy-start.2 = (bf16[4,928,256]{2,1,0:T(8,128)(2,1)}, bf16[4,928,256]{2,1,0:T(8,128)(2,1)S(1)}, u32[]{:S(2)}) copy-start(bf16[4,928,256]{2,1,0:T(8,128)(2,1)S(1)} %pad_maximum_fusion.refs_0_.refs_6_) | copy-start | bytes 5701636
  10.8 43.4 %collective-permute-start = (bf16[4,928,256]{2,1,0:T(8,128)(2,1)S(1)}, bf16[4,928,256]{2,1,0:T(8,128)(2,1)}, u32[]{:S(2)}, u32[]{:S(2)}) collective-permute-start(bf16[4,928,256]{2,1,0:T(8,128)(2,1)S(1)} %pad_maximum_fusion.refs_0_.refs_6_), channel_id=1, source_target_pairs={{0,8},{8,0},{16,24},{24,16},{1,9},{9,1},{17,25},{25,17},{2,10},{10... | collective-permute-start | bytes 5701640 | tf_op jit(solution)/shard_map/ppermute | solution.py:19
  14.9 80.1 %collective-permute-start.7 = (bf16[4,928,256]{2,1,0:T(8,128)(2,1)}, bf16[4,928,256]{2,1,0:T(8,128)(2,1)}, u32[]{:S(2)}, u32[]{:S(2)}) collective-permute-start(bf16[4,928,256]{2,1,0:T(8,128)(2,1)} %pad_maximum_fusion.1.refs_0_.refs_6_), channel_id=1, source_target_pairs={{0,8},{8,0},{16,24},{24,16},{1,9},{9,1},{17,25},{25,17},{2,10},{10... | collective-permute-start | bytes 5701640 | tf_op jit(solution)/shard_map/ppermute | solution.py:19
  17.0 88.3 %collective-permute-start.12 = (bf16[4,928,256]{2,1,0:T(8,128)(2,1)}, bf16[4,928,256]{2,1,0:T(8,128)(2,1)}, u32[]{:S(2)}, u32[]{:S(2)}) collective-permute-start(bf16[4,928,256]{2,1,0:T(8,128)(2,1)} %pad_maximum_fusion.1.refs_0_.refs_6_), channel_id=1, source_target_pairs={{8,16},{16,8},{9,17},{17,9},{10,18},{18,10},{11,19},{19,11},{12,20... | collective-permute-start | bytes 5701640 | tf_op jit(solution)/shard_map/ppermute | solution.py:19
  18.9 101.4 %collective-permute-start.1 = (bf16[4,928,256]{2,1,0:T(8,128)(2,1)S(1)}, bf16[4,928,256]{2,1,0:T(8,128)(2,1)}, u32[]{:S(2)}, u32[]{:S(2)}) collective-permute-start(bf16[4,928,256]{2,1,0:T(8,128)(2,1)S(1)} %pad_maximum_fusion.refs_0_.refs_6_), channel_id=1, source_target_pairs={{8,16},{16,8},{9,17},{17,9},{10,18},{18,10},{11,19},{19,11},{12,20... | collective-permute-start | bytes 5701640 | tf_op jit(solution)/shard_map/ppermute | solution.py:19
  54.2 77.5 %collective-permute-start.3 = (bf16[4,928,256]{2,1,0:T(8,128)(2,1)}, bf16[4,928,256]{2,1,0:T(8,128)(2,1)}, u32[]{:S(2)}, u32[]{:S(2)}) collective-permute-start(bf16[4,928,256]{2,1,0:T(8,128)(2,1)} %collective-permute-done.refs_1_.refs_7_), channel_id=1, source_target_pairs={{8,16},{16,8},{9,17},{17,9},{10,18},{18,10},{11,19},{19,11},{12,20... | collective-permute-start | bytes 5701640 | tf_op jit(solution)/shard_map/ppermute | solution.py:19
  95.0 61.7 %collective-permute-start.8 = (bf16[4,928,256]{2,1,0:T(8,128)(2,1)}, bf16[4,928,256]{2,1,0:T(8,128)(2,1)}, u32[]{:S(2)}, u32[]{:S(2)}) collective-permute-start(bf16[4,928,256]{2,1,0:T(8,128)(2,1)} %collective-permute-done.7.refs_1_.refs_7_), channel_id=1, source_target_pairs={{8,16},{16,8},{9,17},{17,9},{10,18},{18,10},{11,19},{19,11},{12,20... | collective-permute-start | bytes 5701640 | tf_op jit(solution)/shard_map/ppermute | solution.py:19
  108.9 79.0 %collective-permute-start.13 = (bf16[4,928,256]{2,1,0:T(8,128)(2,1)}, bf16[4,928,256]{2,1,0:T(8,128)(2,1)}, u32[]{:S(2)}, u32[]{:S(2)}) collective-permute-start(bf16[4,928,256]{2,1,0:T(8,128)(2,1)} %convert_select_fusion), channel_id=1, source_target_pairs={{0,8},{8,0},{16,24},{24,16},{1,9},{9,1},{17,25},{25,17},{2,10},{10... | collective-permute-start | bytes 5701640 | tf_op jit(solution)/shard_map/ppermute | solution.py:19
  122.7 70.1 %collective-permute-start.2 = (bf16[4,928,256]{2,1,0:T(8,128)(2,1)S(1)}, bf16[4,928,256]{2,1,0:T(8,128)(2,1)S(1)}, u32[]{:S(2)}, u32[]{:S(2)}) collective-permute-start(bf16[4,928,256]{2,1,0:T(8,128)(2,1)S(1)} %convert_select_fusion.3), channel_id=1, source_target_pairs={{0,8},{8,0},{16,24},{24,16},{1,9},{9,1},{17,25},{25,17},{2,10},{10... | collective-permute-start | bytes 5701640 | tf_op jit(solution)/shard_map/ppermute | solution.py:19
  135.3 98.3 %collective-permute-start.4 = (bf16[4,928,256]{2,1,0:T(8,128)(2,1)}, bf16[4,928,256]{2,1,0:T(8,128)(2,1)}, u32[]{:S(2)}, u32[]{:S(2)}) collective-permute-start(bf16[4,928,256]{2,1,0:T(8,128)(2,1)} %convert_select_fusion.2), channel_id=1, source_target_pairs={{0,8},{8,0},{16,24},{24,16},{1,9},{9,1},{17,25},{25,17},{2,10},{10... | collective-permute-start | bytes 5701640 | tf_op jit(solution)/shard_map/ppermute | solution.py:19
  156.6 31.2 %copy-start.6 = (f32[4,928,256]{2,1,0:T(8,128)S(1)}, f32[4,928,256]{2,1,0:T(8,128)}, u32[]{:S(2)}) copy-start(f32[4,928,256]{2,1,0:T(8,128)} %shard_map.105.refs_12_) | copy-start | bytes 11403268
  159.1 33.6 %copy-start.5 = (f32[4,928,256]{2,1,0:T(8,128)S(1)}, f32[4,928,256]{2,1,0:T(8,128)}, u32[]{:S(2)}) copy-start(f32[4,928,256]{2,1,0:T(8,128)} %shard_map.102.refs_12_) | copy-start | bytes 11403268
  159.1 115.1 %collective-permute-start.9 = (bf16[4,928,256]{2,1,0:T(8,128)(2,1)S(1)}, bf16[4,928,256]{2,1,0:T(8,128)(2,1)S(1)}, u32[]{:S(2)}, u32[]{:S(2)}) collective-permute-start(bf16[4,928,256]{2,1,0:T(8,128)(2,1)S(1)} %convert_select_fusion.1), channel_id=1, source_target_pairs={{0,8},{8,0},{16,24},{24,16},{1,9},{9,1},{17,25},{25,17},{2,10},{10... | collective-permute-start | bytes 5701640 | tf_op jit(solution)/shard_map/ppermute | solution.py:19
  189.8 43.8 %copy-start.3 = (f32[4,928,256]{2,1,0:T(8,128)S(1)}, f32[4,928,256]{2,1,0:T(8,128)}, u32[]{:S(2)}) copy-start(f32[4,928,256]{2,1,0:T(8,128)} %shard_map.103.refs_12_) | copy-start | bytes 11403268
  189.8 88.2 %collective-permute-start.16 = (bf16[4,928,256]{2,1,0:T(8,128)(2,1)S(1)}, bf16[4,928,256]{2,1,0:T(8,128)(2,1)S(1)}, u32[]{:S(2)}, u32[]{:S(2)}) collective-permute-start(bf16[4,928,256]{2,1,0:T(8,128)(2,1)S(1)} %add_convert_fusion.1), channel_id=1, source_target_pairs={{8,16},{16,8},{9,17},{17,9},{10,18},{18,10},{11,19},{19,11},{12,20... | collective-permute-start | bytes 5701640 | tf_op jit(solution)/shard_map/ppermute | solution.py:19
  192.8 1.9 copy-start
  194.6 79.6 %copy-start.7 = (f32[4,928,256]{2,1,0:T(8,128)S(1)}, f32[4,928,256]{2,1,0:T(8,128)}, u32[]{:S(2)}) copy-start(f32[4,928,256]{2,1,0:T(8,128)} %shard_map.104.refs_12_) | copy-start | bytes 11403268
  194.6 87.3 %collective-permute-start.14 = (bf16[4,928,256]{2,1,0:T(8,128)(2,1)}, bf16[4,928,256]{2,1,0:T(8,128)(2,1)}, u32[]{:S(2)}, u32[]{:S(2)}) collective-permute-start(bf16[4,928,256]{2,1,0:T(8,128)(2,1)} %add_convert_fusion.3), channel_id=1, source_target_pairs={{8,16},{16,8},{9,17},{17,9},{10,18},{18,10},{11,19},{19,11},{12,20... | collective-permute-start | bytes 5701640 | tf_op jit(solution)/shard_map/ppermute | solution.py:19
  236.8 51.2 %collective-permute-start.5 = (bf16[4,928,256]{2,1,0:T(8,128)(2,1)}, bf16[4,928,256]{2,1,0:T(8,128)(2,1)S(1)}, u32[]{:S(2)}, u32[]{:S(2)}) collective-permute-start(bf16[4,928,256]{2,1,0:T(8,128)(2,1)} %add_convert_fusion.7), channel_id=1, source_target_pairs={{8,16},{16,8},{9,17},{17,9},{10,18},{18,10},{11,19},{19,11},{12,20... | collective-permute-start | bytes 5701640 | tf_op jit(solution)/shard_map/ppermute | solution.py:19
  274.2 1.9 copy-start.1
  276.1 15.1 %collective-permute-start.10 = (bf16[4,928,256]{2,1,0:T(8,128)(2,1)}, bf16[4,928,256]{2,1,0:T(8,128)(2,1)}, u32[]{:S(2)}, u32[]{:S(2)}) collective-permute-start(bf16[4,928,256]{2,1,0:T(8,128)(2,1)} %add_convert_fusion.5), channel_id=1, source_target_pairs={{8,16},{16,8},{9,17},{17,9},{10,18},{18,10},{11,19},{19,11},{12,20... | collective-permute-start | bytes 5701640 | tf_op jit(solution)/shard_map/ppermute | solution.py:19
  278.0 1.9 copy-start.11
  280.0 42.6 %collective-permute-start.17 = (bf16[4,928,256]{2,1,0:T(8,128)(2,1)}, bf16[4,928,256]{2,1,0:T(8,128)(2,1)}, u32[]{:S(2)}, u32[]{:S(2)}) collective-permute-start(bf16[4,928,256]{2,1,0:T(8,128)(2,1)} %add_convert_fusion), channel_id=1, source_target_pairs={{8,0},{16,24},{9,1},{17,25},{10,2},{18,26},{11,3},{19,27},{12,4},{... | collective-permute-start | bytes 5701640 | tf_op jit(solution)/shard_map/ppermute | solution.py:19
  281.9 6.1 %copy-start.4 = (f32[4,928,256]{2,1,0:T(8,128)S(1)}, f32[4,928,256]{2,1,0:T(8,128)}, u32[]{:S(2)}) copy-start(f32[4,928,256]{2,1,0:T(8,128)} %shard_map.103.refs_12_) | copy-start | bytes 11403268
  286.5 4.7 copy-start.8
  286.5 76.9 %collective-permute-start.15 = (bf16[4,928,256]{2,1,0:T(8,128)(2,1)}, bf16[4,928,256]{2,1,0:T(8,128)(2,1)}, u32[]{:S(2)}, u32[]{:S(2)}) collective-permute-start(bf16[4,928,256]{2,1,0:T(8,128)(2,1)} %add_convert_fusion.2), channel_id=1, source_target_pairs={{8,0},{16,24},{9,1},{17,25},{10,2},{18,26},{11,3},{19,27},{12,4},{... | collective-permute-start | bytes 5701640 | tf_op jit(solution)/shard_map/ppermute | solution.py:19
  288.0 1.8 copy-start.10
  289.9 189.8 %collective-permute-start.6 = (bf16[4,928,256]{2,1,0:T(8,128)(2,1)}, bf16[4,928,256]{2,1,0:T(8,128)(2,1)}, u32[]{:S(2)}, u32[]{:S(2)}) collective-permute-start(bf16[4,928,256]{2,1,0:T(8,128)(2,1)} %add_convert_fusion.6), channel_id=1, source_target_pairs={{8,0},{16,24},{9,1},{17,25},{10,2},{18,26},{11,3},{19,27},{12,4},{... | collective-permute-start | bytes 5701640 | tf_op jit(solution)/shard_map/ppermute | solution.py:19
  294.4 150.3 %collective-permute-start.11 = (bf16[4,928,256]{2,1,0:T(8,128)(2,1)}, bf16[4,928,256]{2,1,0:T(8,128)(2,1)S(1)}, u32[]{:S(2)}, u32[]{:S(2)}) collective-permute-start(bf16[4,928,256]{2,1,0:T(8,128)(2,1)} %add_convert_fusion.4), channel_id=1, source_target_pairs={{8,0},{16,24},{9,1},{17,25},{10,2},{18,26},{11,3},{19,27},{12,4},{... | collective-permute-start | bytes 5701640 | tf_op jit(solution)/shard_map/ppermute | solution.py:19
  444.7 1.3 copy-start.12
  516.4 7.4 %collective-permute-start.18 = (bf16[2,2,128,2048]{3,2,1,0:T(8,128)(2,1)S(1)}, bf16[2,2,128,2048]{3,2,1,0:T(8,128)(2,1)}, u32[]{:S(2)}, u32[]{:S(2)}) collective-permute-start(bf16[2,2,128,2048]{3,2,1,0:T(8,128)(2,1)S(1)} %fusion), channel_id=1, source_target_pairs={{0,2},{2,0},{4,6},{6,4},{1,3},{3,1},{5,7},{7,5},{8,10},{10,8},{12,... | collective-permute-start | bytes 6291464 | tf_op jit(solution)/shard_map/ppermute | solution.py:260
  527.1 2.0 copy-start.9
  529.3 24.4 %collective-permute-start.19 = (bf16[1,2,128,2048]{3,2,1,0:T(8,128)(2,1)S(1)}, bf16[1,2,128,2048]{3,2,1,0:T(8,128)(2,1)S(1)}, u32[]{:S(2)}, u32[]{:S(2)}) collective-permute-start(bf16[1,2,128,2048]{3,2,1,0:T(8,128)(2,1)S(1)} %dynamic-slice_convert_fusion), channel_id=1, source_target_pairs={{0,4},{2,6},{4,0},{6,2},{1,5},{3,7},{5,1},{7,3},{8,12},{10,14},{12... | collective-permute-start | bytes 3145736 | tf_op jit(solution)/shard_map/ppermute | solution.py:260
  555.8 23.4 %collective-permute-start.20 = (bf16[1,128,2048]{2,1,0:T(8,128)(2,1)S(1)}, bf16[1,128,2048]{2,1,0:T(8,128)(2,1)S(1)}, u32[]{:S(2)}, u32[]{:S(2)}) collective-permute-start(bf16[1,128,2048]{2,1,0:T(8,128)(2,1)S(1)} %fusion.2), channel_id=1, source_target_pairs={{0,1},{1,0},{2,3},{3,2},{4,5},{5,4},{6,7},{7,6},{8,9},{9,8},{10,11... | collective-permute-start | bytes 1572872 | tf_op jit(solution)/shard_map/ppermute | solution.py:260
Sparse Core Ops, SparseCore 0:
  9.9 39.2 all-gather.2
  51.0 36.7 all-gather.4

commit v2 on v1

--- a/solution.py
+++ b/solution.py
@@ -13,6 +13,16 @@
 SWAP = [(0, 1), (1, 0), (2, 3), (3, 2)]
 MIDDLE = [(1, 2), (2, 1)]
 TO_ENDS = [(1, 0), (2, 3)]
+
+
+def tie(value, *after):
+    return pl.pallas_call(
+        lambda *refs: None,
+        in_specs=[pl.BlockSpec(memory_space=pl.ANY)] * (1 + len(after)),
+        out_specs=pl.BlockSpec(memory_space=pl.ANY),
+        out_shape=jax.ShapeDtypeStruct(value.shape, value.dtype),
+        input_output_aliases={0: 0},
+    )(value, *after)
 
 
 def send(value, pairs):
@@ -35,6 +45,10 @@
         )
 
 
+def sigmoid(value):
+    return 0.5 + 0.5 * jnp.tanh(0.5 * value)
+
+
 def slot_value(end, refs, slot):
     if slot == 0:
         return refs[0][...].astype(jnp.float32)
@@ -57,15 +71,21 @@
     return jnp.where(at < rows, value, jnp.zeros_like(value))
 
 
-def down_kernel(k_ref, *refs):
+def down_kernel(factors, k_ref, *refs):
     gates, uppers = refs[:6], refs[6:12]
-    grad_ref, out_ref, hidden = refs[12], refs[-2], refs[-1]
+    grad_ref, hidden = refs[12], refs[-1]
+    out_ref = refs[-4] if factors else refs[-2]
     width = gates[0].shape[1]
     end = k_ref[1] == 1
     for slot in range(4):
         gate, upper = slot_value(end, gates, slot), slot_value(end, uppers, slot)
-        value = gate * jax.nn.sigmoid(gate) * upper
-        hidden[:, columns(place(k_ref, slot), width)] = value.astype(jnp.bfloat16)
+        j = place(k_ref, slot)
+        sigma = sigmoid(gate)
+        active = gate * sigma
+        hidden[:, columns(j, width)] = (active * upper).astype(jnp.bfloat16)
+        if factors:
+            refs[-3][j] = active
+            refs[-2][j] = upper * sigma * (1.0 + gate * (1.0 - sigma))
     features = grad_ref.shape[1]
     step = min(features, 512)
     for c in range(0, features, step):
@@ -92,7 +112,7 @@
             + r2[j].astype(jnp.float32)
             + jnp.where(end, r3[j], r1[j]).astype(jnp.float32)
         )
-        sigma = jax.nn.sigmoid(gate)
+        sigma = sigmoid(gate)
         up_value = (hidden_grad * (gate * sigma)).astype(jnp.bfloat16)
         gate_value = (
             hidden_grad * upper * sigma * (1.0 + gate * (1.0 - sigma))
@@ -129,6 +149,68 @@
         ) + lax.dot_general(
             up_grad[...], wu, dims, preferred_element_type=jnp.float32
         )
+
+
+def token_kernel(rows, block, *refs):
+    up_factor, gate_factor, part, r1, r2, r3, wg_ref, wu_ref, acc_in = refs[1:10]
+    k_ref, (gate_out, up_out, acc, rounded, gate_grad, up_grad) = refs[0], refs[10:]
+    count, _, width = part.shape
+    ragged = rows % block != 0
+    end = k_ref[1] == 1
+    for j in range(count):
+        hidden_grad = (
+            part[j]
+            + r2[j].astype(jnp.float32)
+            + jnp.where(end, r3[j], r1[j]).astype(jnp.float32)
+        )
+        up_value = (hidden_grad * up_factor[j]).astype(jnp.bfloat16)
+        gate_value = (hidden_grad * gate_factor[j]).astype(jnp.bfloat16)
+        if ragged:
+            up_value = valid_rows(up_value, rows, block)
+            gate_value = valid_rows(gate_value, rows, block)
+        up_out[j] = up_value
+        gate_out[j] = gate_value
+        up_grad[:, j * width : (j + 1) * width] = up_value
+        gate_grad[:, j * width : (j + 1) * width] = gate_value
+
+    @pl.when(pl.program_id(0) == 0)
+    def _():
+        acc[...] = acc_in[...]
+
+    features = wg_ref.shape[1]
+    step = min(features, 512)
+    for c in range(0, features, step):
+        cols = slice(c, c + step)
+        wg, wu = wg_ref[:, cols], wu_ref[:, cols]
+        if ragged:
+            wg, wu = valid_rows(wg, rows, block), valid_rows(wu, rows, block)
+        dims = (((0,), (0,)), ((), ()))
+        more = lax.dot_general(
+            gate_grad[...], wg, dims, preferred_element_type=jnp.float32
+        ) + lax.dot_general(
+            up_grad[...], wu, dims, preferred_element_type=jnp.float32
+        )
+        acc[:, :, cols] += more.reshape(count, width, step)
+
+    @pl.when(pl.program_id(0) == pl.num_programs(0) - 1)
+    def _():
+        rounded[...] = acc[...].astype(jnp.bfloat16)
+
+
+def weight_kernel(parts, *refs):
+    x_ref, out_ref, grad = refs[parts], refs[-2], refs[-1]
+    count, _, width = refs[0].shape
+    for q in range(parts):
+        for j in range(count):
+            at = (j * parts + q) * width
+            grad[:, at : at + width] = refs[q][j]
+    features = x_ref.shape[1]
+    step = min(features, 512)
+    for c in range(0, features, step):
+        cols = slice(c, c + step)
+        out_ref[:, cols] = jnp.dot(
+            grad[...], x_ref[:, cols], preferred_element_type=jnp.float32
+        ).astype(jnp.bfloat16)
 
 
 def once(shape):
@@ -164,7 +246,7 @@
     return [gate] * 6 + [upper] * 6
 
 
-def down_group(k, slots, grad_whole, out, a, size, total):
+def down_group(k, slots, grad_whole, out, a, size, total, factors):
     tokens, features = grad_whole.shape
     width = slots[0].shape[2]
     block = block_rows(size)
@@ -176,18 +258,23 @@
         aliases[1 + len(args)] = 0
         args.append(out)
         specs.append(pl.BlockSpec(memory_space=pl.ANY))
+    count = slots[0].shape[0]
+    wide = pl.BlockSpec((count, block, width), lambda i, k: (0, i, 0))
+    factor = jax.ShapeDtypeStruct((count, size, width), jnp.float32)
     return pl.pallas_call(
-        down_kernel,
+        functools.partial(down_kernel, factors),
         grid_spec=pltpu.PrefetchScalarGridSpec(
             num_scalar_prefetch=1,
             grid=(blocks,),
             in_specs=specs,
-            out_specs=pl.BlockSpec(
-                (block, features), lambda i, k: (a * blocks + i, 0)
-            ),
+            out_specs=[
+                pl.BlockSpec((block, features), lambda i, k: (a * blocks + i, 0))
+            ]
+            + [wide] * (2 * factors),
             scratch_shapes=[pltpu.VMEM((block, tokens), jnp.bfloat16)],
         ),
-        out_shape=jax.ShapeDtypeStruct((total, features), jnp.bfloat16),
+        out_shape=[jax.ShapeDtypeStruct((total, features), jnp.bfloat16)]
+        + [factor] * (2 * factors),
         input_output_aliases=aliases,
         compiler_params=pltpu.CompilerParams(vmem_limit_bytes=VMEM_LIMIT),
         cost_estimate=pl.CostEstimate(
@@ -246,21 +333,144 @@
     )(k, *args)
 
 
-def scatter_axis(value, axis, name, size):
-    me = lax.axis_index(name)
-    bit = 1
-    while bit < size:
-        shape = value.shape
-        high = size // (2 * bit)
-        view = value.reshape(shape[:axis] + (high, 2) + shape[axis + 1 :])
-        mine = (me // bit) % 2
-        pairs = [(i, i ^ bit) for i in range(size)]
-        away = lax.dynamic_index_in_dim(view, 1 - mine, axis + 1, keepdims=False)
-        kept = lax.dynamic_index_in_dim(view, mine, axis + 1, keepdims=False)
-        got = lax.ppermute(away.astype(jnp.bfloat16), name, pairs)
-        value = kept.astype(jnp.float32) + got.astype(jnp.float32)
-        bit *= 2
-    return value.reshape(value.shape[:axis] + value.shape[axis + 1 :])
+def token_group(k, factors, sums, r3, wg, wu, acc, q, a, size, total):
+    tokens, features = acc.shape
+    count, _, width = r3.shape
+    block = block_rows(size)
+    blocks = size // block
+    parts = tokens // (count * width)
+
+    def split(value):
+        return value.reshape((count, parts) + value.shape[1:])
+
+    some = pl.BlockSpec((count, None, block, width), lambda i, k: (0, q, i, 0))
+    wide = pl.BlockSpec((count, block, width), lambda i, k: (0, i, 0))
+    weight = pl.BlockSpec((block, features), lambda i, k: (a * blocks + i, 0))
+    rows = min(size, total - a * size)
+    grad = jax.ShapeDtypeStruct((count, size, width), jnp.bfloat16)
+    whole = pl.BlockSpec(
+        (count, width, features),
+        lambda i, k: (0, 0, 0),
+        pipeline_mode=pl.Buffered(1),
+    )
+    return pl.pallas_call(
+        functools.partial(token_kernel, rows, block),
+        grid_spec=pltpu.PrefetchScalarGridSpec(
+            num_scalar_prefetch=1,
+            grid=(blocks,),
+            in_specs=[some] * 5
+            + [wide, weight, weight]
+            + [
+                pl.BlockSpec(
+                    (count, None, width, features),
+                    lambda i, k: (0, q, 0, 0),
+                    pipeline_mode=pl.Buffered(1),
+                )
+            ],
+            out_specs=[wide, wide, whole, whole],
+            scratch_shapes=[pltpu.VMEM((block, count * width), jnp.bfloat16)] * 2,
+        ),
+        out_shape=[
+            grad,
+            grad,
+            jax.ShapeDtypeStruct((count, width, features), jnp.float32),
+            jax.ShapeDtypeStruct((count, width, features), jnp.bfloat16),
+        ],
+        compiler_params=pltpu.CompilerParams(vmem_limit_bytes=VMEM_LIMIT),
+        cost_estimate=pl.CostEstimate(
+            flops=4 * size * count * width * features,
+            bytes_accessed=size * (features * 4 + count * width * 22),
+            transcendentals=0,
+        ),
+    )(
+        k,
+        *[split(f) for f in factors],
+        *[split(s) for s in sums],
+        r3,
+        wg,
+        wu,
+        acc.reshape(count, parts, width, features),
+    )
+
+
+def weight_group(grads, x_whole, out, a, size):
+    tokens, features = x_whole.shape
+    count, _, width = grads[0].shape
+    block = block_rows(size)
+    blocks = size // block
+    wide = pl.BlockSpec((count, block, width), lambda i: (0, i, 0))
+    return pl.pallas_call(
+        functools.partial(weight_kernel, len(grads)),
+        grid=(blocks,),
+        in_specs=[wide] * len(grads)
+        + [once((tokens, features)), pl.BlockSpec(memory_space=pl.ANY)],
+        out_specs=pl.BlockSpec((block, features), lambda i: (a * blocks + i, 0)),
+        scratch_shapes=[pltpu.VMEM((block, tokens), jnp.bfloat16)],
+        out_shape=jax.ShapeDtypeStruct(out.shape, out.dtype),
+        input_output_aliases={len(grads) + 1: 0},
+        compiler_params=pltpu.CompilerParams(vmem_limit_bytes=VMEM_LIMIT),
+        cost_estimate=pl.CostEstimate(
+            flops=2 * size * tokens * features,
+            bytes_accessed=size * (features * 2 + tokens * 2),
+            transcendentals=0,
+        ),
+    )(*grads, x_whole, out)
+
+
+def halve(value, axis, bit, mine, pairs):
+    size = value.shape[axis]
+    shape = value.shape
+    view = value.reshape(shape[:axis] + (size // (2 * bit), 2, bit) + shape[axis + 1 :])
+    away = lax.dynamic_index_in_dim(view, 1 - mine, axis + 1, keepdims=False)
+    kept = lax.dynamic_index_in_dim(view, mine, axis + 1, keepdims=False)
+    rest = shape[:axis] + (size // 2,) + shape[axis + 1 :]
+    got = lax.ppermute(away.reshape(rest).astype(jnp.bfloat16), ("wt", "dep"), pairs)
+    return kept.reshape(rest) + got.astype(jnp.float32)
+
+
+def scatter_half(value, rounded, q, n_wt, n_dep):
+    at_wt, at_dep = lax.axis_index("wt"), lax.axis_index("dep")
+
+    def pairs(bit_wt, bit_dep):
+        return [
+            (w * n_dep + d, (w ^ bit_wt) * n_dep + (d ^ bit_dep))
+            for w in range(n_wt)
+            for d in range(n_dep)
+            if w % 2 == q
+        ]
+
+    inward = [
+        (w * n_dep + d, (w ^ 1) * n_dep + d)
+        for w in range(n_wt)
+        for d in range(n_dep)
+        if w % 2 != q
+    ]
+    features = value.shape[-1]
+    blocks = (n_wt // 2, n_dep, -1, features)
+    value = value.reshape(blocks)
+    got = lax.ppermute(rounded, ("wt", "dep"), inward).reshape(blocks)
+
+    def over_wt(part):
+        bit = 2
+        while bit < n_wt:
+            mine = (at_wt // bit) % 2
+            part = halve(part, 0, 1, mine, pairs(bit, 0))
+            bit *= 2
+        return part
+
+    def over_dep(part):
+        bit = 1
+        while bit < n_dep:
+            mine = (at_dep // bit) % 2
+            part = halve(part, 1, 1, mine, pairs(0, bit))
+            bit *= 2
+        return part
+
+    half = features // 2
+    one = value[..., :half] + got[..., :half].astype(jnp.float32)
+    two = value[..., half:] + got[..., half:].astype(jnp.float32)
+    one, two = over_dep(over_wt(one)), over_wt(over_dep(two))
+    return jnp.concatenate([one[0, 0], two[0, 0]], axis=-1)
 
 
 def own_half(gate, upper, half, size):
@@ -295,34 +505,69 @@
         lax.all_gather(out_grad, ("wt", "dep"), axis=0, tiled=True),
     )
     part = [sum_group(w_down, grad_whole, a, size, 4) for a in range(GROUPS)]
+    down = None
+    acc, wgrads = None, (None, None)
+    last = GROUPS - 1
+    factors = None
+
+    def slots_of(a):
+        h = a // 2
+        return [own[h], swap[h], swap[2 + h], middle[2 + h], swap[4 + h], middle[h]]
+
     for step in range(2, 10):
+        if step < 4:
+            swap[step - 2] = tie(swap[step - 2], part[step - 2])
+            middle.append(send(swap[step - 2], MIDDLE))
         if step < 6:
             outward = part[step - 2].astype(jnp.bfloat16)
             payload = jnp.where(end, outward, middle[step - 2])
             swap.append(send(payload, SWAP))
-        else:
-            swap.append(send(rounded(part[step - 6], middle[step - 2]), TO_ENDS))
-        if step < 4:
-            middle.append(send(swap[step - 2], MIDDLE))
-        elif step < 8:
+        elif step < 9:
+            payload = rounded(part[step - 6], middle[step - 2])
+            if step == 8:
+                payload = tie(payload, swap[6], down)
+            swap.append(send(payload, TO_ENDS))
+        if 4 <= step < 8:
             middle.append(send(rounded(part[step - 4], swap[step - 2]), MIDDLE))
-
-    down = None
-    acc, wgrads = None, (None, None)
-    for a in range(GROUPS):
-        h = a // 2
-        slots = [own[h], swap[h], swap[2 + h], middle[2 + h], swap[4 + h], middle[h]]
-        down = down_group(k, slots, grad_whole, down, a, size, total)
+        if step == 6 or step == 7:
+            for a in (2 * step - 12, 2 * step - 11):
+                down, *factors = down_group(
+                    k, slots_of(a), grad_whole, down, a, size, total, a == last
+                )
+
+    def main(a, acc, wgrads):
         sums = [part[a], swap[2 + a], middle[4 + a], swap[6 + a]]
         acc, *wgrads = main_group(
-            k, slots, sums, x_whole, wg, wu, acc, wgrads, a, size, total
-        )
-    gate_wgrad, up_wgrad = wgrads
-
-    tokens, features = acc.shape
-    view = acc.reshape(n_wt, n_dep, tokens // (n_wt * n_dep), features)
-    input_grad = scatter_axis(view, 0, "wt", n_wt)
-    input_grad = scatter_axis(input_grad, 0, "dep", n_dep)
+            k, slots_of(a), sums, x_whole, wg, wu, acc, wgrads, a, size, total
+        )
+        return acc, wgrads
+
+    def pieces(value):
+        return value.reshape((2, 2) + value.shape[1:])
+
+    final = []
+    for q in range(2):
+        payload = rounded(pieces(part[last])[:, q], pieces(middle[4 + last])[:, q])
+        if q == 0:
+            payload = tie(payload, swap[7])
+        else:
+            acc, wgrads = main(0, acc, wgrads)
+            payload = tie(payload, acc)
+        final.append(send(payload, TO_ENDS))
+    for a in range(1, last):
+        acc, wgrads = main(a, acc, wgrads)
+    sums = [part[last], swap[2 + last], middle[4 + last]]
+    gate_grads, up_grads, shares = [], [], []
+    for q in range(2):
+        gate_part, up_part, value, small = token_group(
+            k, factors, sums, final[q], wg, wu, acc, q, last, size, total
+        )
+        gate_grads.append(gate_part)
+        up_grads.append(up_part)
+        shares.append(scatter_half(value, small, q, n_wt, n_dep))
+    gate_wgrad = weight_group(gate_grads, x_whole, wgrads[0], last, size)
+    up_wgrad = weight_group(up_grads, x_whole, wgrads[1], last, size)
+    input_grad = jnp.where(lax.axis_index("wt") % 2 == 0, *shares)
     return (input_grad.astype(jnp.bfloat16), gate_wgrad.T, up_wgrad.T, down)
 
 

time: 598 us -> 535 us (0.89)
  the two profiles are of different devices: /device:TPU:1 before, /device:TPU:8 now
where the time goes in v2:
time: 535 us; the launch traced here: 526 us
  Pallas kernels  226 us (42%)
  waiting for transfers between devices  168 us (31%)
  starting transfers between devices  57.9 us (11%)
  other arithmetic  51.7 us (10%)
  between operations  15.2 us (3%)
  local copies, waits for them, and re-layouts  7.67 us (1%)
    ppermute x19, waiting for transfers between devices, send(): return lax.ppermute(value, 'inp', pairs)  131 us
    pallas_call x3, Pallas kernels, main_group(): pl.pallas_call(functools.partial(main_kernel, rows, acc is not None), gri...  98.6 us
    pallas_call x4, Pallas kernels, down_group(): pl.pallas_call(functools.partial(down_kernel, factors), grid_spec=pltpu.P...  48.4 us
    ppermute x19, starting transfers between devices, send(): return lax.ppermute(value, 'inp', pairs)  39.4 us
    pallas_call x4, Pallas kernels, sum_group(): pl.pallas_call(sum_kernel, grid=(blocks,), in_specs=[pl.BlockSpec((block,...  33.6 us
    pallas_call x2, Pallas kernels, token_group(): pl.pallas_call(functools.partial(token_kernel, rows, block), grid_spec=pl...  28.9 us
    convert_element_type x8, other arithmetic, rounded(): return (part + got.astype(jnp.float32)).astype(jnp.bfloat16)  26.9 us
    all_gather x1, waiting for transfers between devices, per_device(): lax.all_gather(out_grad, ('wt', 'dep'), axis=0, tiled=True)  25 us
  transfers between devices with their start and end apart: 31, of which 11 were waited for; matrix products, arithmetic and copies ran while one was open for 10% of the time, Pallas kernels for 43%

profile of v2, /device:TPU:8, one launch (start us, length us, event | category | flops | bytes accessed | tf_op | source)
XLA Modules:
  0.0 525.7 jit_solution(12124548813252282460)
XLA Ops:
  10.7 3.5 collective-permute-start.6
  22.8 25.0 %all-gather.3.cloned.1.call-done.grad_ref.refs_12_ = bf16[1024,2048]{1,0:T(8,128)(2,1)} async-done(((bf16[128,2048]{1,0:T(8,128)(2,1)}), bf16[1024,2048]{1,0:T(8,128)(2,1)}) %all-gather.3.cloned.1.call-update) | async-done | bytes 4194320 | tf_op jit(solution)/shard_map/all_gather | solution.py:505
  47.8 8.4 %shard_map.105.refs_1_.refs_12_ = f32[4,928,256]{2,1,0:T(8,128)} custom-call(bf16[3696,2048]{1,0:T(8,128)(2,1)} %w_ref.7, bf16[1024,2048]{1,0:T(8,128)(2,1)} %all-gather.3.cloned.1.call-done.grad_ref.refs_12_), custom_call_target="tpu_custom_call" | custom-call | flops 3892314112 | bytes 7602176 | tf_op jit(solution)/shard_map/pallas_call | solution.py:225
  58.4 3.6 convert_select_fusion.1
  62.0 4.0 collective-permute-start.8
  66.0 8.4 %shard_map.102.refs_1_.refs_12_ = f32[4,928,256]{2,1,0:T(8,128)} custom-call(bf16[3696,2048]{1,0:T(8,128)(2,1)} %w_ref.7, bf16[1024,2048]{1,0:T(8,128)(2,1)} %all-gather.3.cloned.1.call-done.grad_ref.refs_12_), custom_call_target="tpu_custom_call" | custom-call | flops 3892314112 | bytes 7602176 | tf_op jit(solution)/shard_map/pallas_call | solution.py:225
  74.4 25.2 %collective-permute-done.refs_0_ = bf16[4,928,256]{2,1,0:T(8,128)(2,1)} collective-permute-done((bf16[4,928,256]{2,1,0:T(8,128)(2,1)}, bf16[4,928,256]{2,1,0:T(8,128)(2,1)}, u32[]{:S(2)}, u32[]{:S(2)}) %collective-permute-start) | collective-permute-done | bytes 1900576 | tf_op jit(solution)/shard_map/ppermute | solution.py:29
  102.0 4.2 convert_select_fusion.3
  106.2 8.4 %shard_map.107.refs_12_ = f32[4,928,256]{2,1,0:T(8,128)} custom-call(bf16[3696,2048]{1,0:T(8,128)(2,1)} %w_ref.7, bf16[1024,2048]{1,0:T(8,128)(2,1)} %all-gather.3.cloned.1.call-done.grad_ref.refs_12_), custom_call_target="tpu_custom_call" | custom-call | flops 3892314112 | bytes 7602176 | tf_op jit(solution)/shard_map/pallas_call | solution.py:225
  114.6 8.4 %shard_map.104 = f32[4,928,256]{2,1,0:T(8,128)} custom-call(bf16[3696,2048]{1,0:T(8,128)(2,1)} %w_ref.7, bf16[1024,2048]{1,0:T(8,128)(2,1)} %all-gather.3.cloned.1.call-done.grad_ref.refs_12_), custom_call_target="tpu_custom_call" | custom-call | flops 3892314112 | bytes 7602176 | tf_op jit(solution)/shard_map/pallas_call | solution.py:225
  123.0 17.3 %collective-permute-done.7.refs_2_.refs_8_.refs_13_ = bf16[4,928,256]{2,1,0:T(8,128)(2,1)S(1)} collective-permute-done((bf16[4,928,256]{2,1,0:T(8,128)(2,1)}, bf16[4,928,256]{2,1,0:T(8,128)(2,1)S(1)}, u32[]{:S(2)}, u32[]{:S(2)}) %collective-permute-start.7) | collective-permute-done | bytes 1900576 | tf_op jit(solution)/shard_map/ppermute | solution.py:29
  140.3 4.5 add_convert_fusion.1
  144.8 2.6 collective-permute-start.15
  147.5 3.0 convert_select_fusion
  150.5 28.9 %collective-permute-done.3.refs_3_.refs_9_ = bf16[4,928,256]{2,1,0:T(8,128)(2,1)} collective-permute-done((bf16[4,928,256]{2,1,0:T(8,128)(2,1)}, bf16[4,928,256]{2,1,0:T(8,128)(2,1)}, u32[]{:S(2)}, u32[]{:S(2)}) %collective-permute-start.3) | collective-permute-done | bytes 1900576 | tf_op jit(solution)/shard_map/ppermute | solution.py:29
  179.4 3.0 convert_select_fusion.2
  182.5 3.2 add_convert_fusion.5
  185.7 3.5 collective-permute-start.11
  189.8 30.3 %collective-permute-done.15.refs_14_ = bf16[4,928,256]{2,1,0:T(8,128)(2,1)} collective-permute-done((bf16[4,928,256]{2,1,0:T(8,128)(2,1)}, bf16[4,928,256]{2,1,0:T(8,128)(2,1)}, u32[]{:S(2)}, u32[]{:S(2)}) %collective-permute-start.15) | collective-permute-done | bytes 1900576 | tf_op jit(solution)/shard_map/ppermute | solution.py:29
  220.1 4.4 add_convert_fusion
  224.5 3.0 collective-permute-start.16
  229.5 3.7 collective-permute-start.14
  233.2 27.9 %collective-permute-done.4.refs_4_.refs_10_ = bf16[4,928,256]{2,1,0:T(8,128)(2,1)} collective-permute-done((bf16[4,928,256]{2,1,0:T(8,128)(2,1)}, bf16[4,928,256]{2,1,0:T(8,128)(2,1)}, u32[]{:S(2)}, u32[]{:S(2)}) %collective-permute-start.4) | collective-permute-done | bytes 1900576 | tf_op jit(solution)/shard_map/ppermute | solution.py:29
  261.1 3.2 add_convert_fusion.6
  266.7 3.3 add_convert_fusion.4
  270.0 4.2 collective-permute-start.12
  274.2 11.6 %shard_map.108.refs_13_ = bf16[3696,2048]{1,0:T(8,128)(2,1)} custom-call(s32[2]{0:T(128)} %pad_add_fusion.k_ref.refs_0_, bf16[4,928,256]{2,1,0:T(8,128)(2,1)} %pad_maximum_fusion.1.refs_0_.refs_6_, bf16[4,928,256]{2,1,0:T(8,128)(2,1)} %shard_map.106.refs_1_.refs_7_, bf16[4,928,256]{2,1,0:T(8,128)(2,1)} %copy-done.1, ...), custom_call_target="tpu_custom_call" | custom-call | flops 3892314112 | bytes 7602176 | tf_op jit(solution)/shard_map/pallas_call | solution.py:264
  285.7 11.2 %shard_map.109.refs_13_ = bf16[3696,2048]{1,0:T(8,128)(2,1)} custom-call(s32[2]{0:T(128)} %pad_add_fusion.k_ref.refs_0_, bf16[4,928,256]{2,1,0:T(8,128)(2,1)} %pad_maximum_fusion.1.refs_0_.refs_6_, bf16[4,928,256]{2,1,0:T(8,128)(2,1)} %shard_map.106.refs_1_.refs_7_, bf16[4,928,256]{2,1,0:T(8,128)(2,1)} %copy-done.1, ...), custom_call_target="tpu_custom_call", output_to_operand_aliasing={{}: (14, {})} | custom-call | flops 3892314112 | bytes 7602176 | tf_op jit(solution)/shard_map/pallas_call | solution.py:264
  296.9 11.6 %shard_map.110.refs_13_ = bf16[3696,2048]{1,0:T(8,128)(2,1)} custom-call(s32[2]{0:T(128)} %pad_add_fusion.k_ref.refs_0_, bf16[4,928,256]{2,1,0:T(8,128)(2,1)} %pad_maximum_fusion.refs_0_.refs_6_, bf16[4,928,256]{2,1,0:T(8,128)(2,1)} %shard_map.103.refs_1_.refs_7_, ...), custom_call_target="tpu_custom_call", output_to_operand_aliasing={{}: (14, {})} | custom-call | flops 3892314112 | bytes 7602176 | tf_op jit(solution)/shard_map/pallas_call | solution.py:264
  308.6 14.0 %shard_map.111 = (bf16[3696,2048]{1,0:T(8,128)(2,1)}, f32[4,928,256]{2,1,0:T(8,128)}, f32[4,928,256]{2,1,0:T(8,128)}) custom-call(s32[2]{0:T(128)} %pad_add_fusion.k_ref.refs_0_, bf16[4,928,256]{2,1,0:T(8,128)(2,1)} %pad_maximum_fusion.refs_0_.refs_6_, bf16[4,928,256]{2,1,0:T(8,128)(2,1)} %shard_map.103.refs_1_.refs_7_, ...), custom_call_target="tpu_custom_call", output_to_operand_aliasing={{0}: (14, {})} | custom-call | flops 3892314112 | bytes 7602176 | tf_op jit(solution)/shard_map/pallas_call | solution.py:264
  322.6 3.3 add_convert_fusion.2.refs_0_
  325.8 2.9 collective-permute-start.17
  328.8 31.4 %shard_map.114 = (f32[1024,2048]{1,0:T(8,128)}, bf16[3696,2048]{1,0:T(8,128)(2,1)}, bf16[3696,2048]{1,0:T(8,128)(2,1)}) custom-call(s32[2]{0:T(128)} %pad_add_fusion.k_ref.refs_0_, bf16[4,928,256]{2,1,0:T(8,128)(2,1)} %pad_maximum_fusion.1.refs_0_.refs_6_, bf16[4,928,256]{2,1,0:T(8,128)(2,1)} %shard_map.106.refs_1_.refs_7_, bf16[4,928,256]{2,1,0:T(8,128)(2,1)} %copy-done.1, ...), custom_call_target="tpu_custom_call" | custom-call | flops 15569256448 | bytes 28508160 | tf_op jit(solution)/shard_map/pallas_call | solution.py:312
  360.2 3.2 fusion.4
  366.3 33.5 %shard_map.115 = (f32[1024,2048]{1,0:T(8,128)}, bf16[3696,2048]{1,0:T(8,128)(2,1)}, bf16[3696,2048]{1,0:T(8,128)(2,1)}) custom-call(s32[2]{0:T(128)} %pad_add_fusion.k_ref.refs_0_, bf16[4,928,256]{2,1,0:T(8,128)(2,1)} %pad_maximum_fusion.1.refs_0_.refs_6_, ...), custom_call_target="tpu_custom_call", output_to_operand_aliasing={{0}: (20, {}), {1}: (21, {}), {2}: (22, {})} | custom-call | flops 15569256448 | bytes 28508160 | tf_op jit(solution)/shard_map/pallas_call | solution.py:312
  399.8 33.7 %shard_map.116 = (f32[1024,2048]{1,0:T(8,128)}, bf16[3696,2048]{1,0:T(8,128)(2,1)}, bf16[3696,2048]{1,0:T(8,128)(2,1)}) custom-call(s32[2]{0:T(128)} %pad_add_fusion.k_ref.refs_0_, bf16[4,928,256]{2,1,0:T(8,128)(2,1)} %pad_maximum_fusion.refs_0_.refs_6_, ...), custom_call_target="tpu_custom_call", output_to_operand_aliasing={{0}: (20, {}), {1}: (21, {}), {2}: (22, {})} | custom-call | flops 15569256448 | bytes 28508160 | tf_op jit(solution)/shard_map/pallas_call | solution.py:312
  434.5 14.3 %shard_map.119 = (bf16[2,928,256]{2,1,0:T(8,128)(2,1)}, bf16[2,928,256]{2,1,0:T(8,128)(2,1)}, f32[2,256,2048]{2,1,0:T(8,128)}, bf16[2,256,2048]{2,1,0:T(8,128)(2,1)}) custom-call(s32[2]{0:T(128)} %pad_add_fusion.k_ref.refs_0_, f32[2,2,928,256]{3,2,1,0:T(8,128)} %bitcast.51, f32[2,2,928,256]{3,2,1,0:T(8,128)} %bitcast.53, f32[2,2,928,256]{3,2,1,0:T(8,128)} %bitcast.46, ...), custom_call_target="tpu_custom_call" | custom-call | flops 3892314112 | bytes 18055168 | tf_op jit(solution)/shard_map/pallas_call | solution.py:356
  451.3 14.5 %shard_map.117 = (bf16[2,928,256]{2,1,0:T(8,128)(2,1)}, bf16[2,928,256]{2,1,0:T(8,128)(2,1)}, f32[2,256,2048]{2,1,0:T(8,128)}, bf16[2,256,2048]{2,1,0:T(8,128)(2,1)}) custom-call(s32[2]{0:T(128)} %pad_add_fusion.k_ref.refs_0_, f32[2,2,928,256]{3,2,1,0:T(8,128)} %bitcast.52, f32[2,2,928,256]{3,2,1,0:T(8,128)} %bitcast.54, f32[2,2,928,256]{3,2,1,0:T(8,128)} %bitcast.47, ...), custom_call_target="tpu_custom_call" | custom-call | flops 3892314112 | bytes 18055168 | tf_op jit(solution)/shard_map/pallas_call | solution.py:356
  467.2 8.1 %shard_map.121 = bf16[3696,2048]{1,0:T(8,128)(2,1)} custom-call(bf16[2,928,256]{2,1,0:T(8,128)(2,1)} %get-tuple-element.41.refs_0_, bf16[2,928,256]{2,1,0:T(8,128)(2,1)} %get-tuple-element.42.refs_1_, bf16[1024,2048]{1,0:T(8,128)(2,1)} %all-gather.5.cloned.1.call-done.refs_16_.refs_2_, ...), custom_call_target="tpu_custom_call", output_to_operand_aliasing={{}: (3, {})} | custom-call | flops 3892314112 | bytes 5701632 | tf_op jit(solution)/shard_map/pallas_call | solution.py:402
  475.2 8.0 %shard_map.120 = bf16[3696,2048]{1,0:T(8,128)(2,1)} custom-call(bf16[2,928,256]{2,1,0:T(8,128)(2,1)} %get-tuple-element.38.refs_0_, bf16[2,928,256]{2,1,0:T(8,128)(2,1)} %get-tuple-element.39.refs_1_, bf16[1024,2048]{1,0:T(8,128)(2,1)} %all-gather.5.cloned.1.call-done.refs_16_.refs_2_, ...), custom_call_target="tpu_custom_call", output_to_operand_aliasing={{}: (3, {})} | custom-call | flops 3892314112 | bytes 5701632 | tf_op jit(solution)/shard_map/pallas_call | solution.py:402
  483.2 3.1 slice_add_fusion.1
  487.9 2.6 slice_add_fusion.3
  490.6 3.4 collective-permute-start.19
  494.1 3.4 collective-permute-start.21
  499.3 5.2 collective-permute-done.19
  504.7 3.4 collective-permute-start.20
  509.1 2.7 collective-permute-start.22
  513.4 4.0 collective-permute-done.22
  (106 shorter events, 36.2 us)
Async XLA Ops:
  7.2 2.1 copy-start.12
  7.2 40.6 %all-gather.3.cloned.1.call-start = ((), (), s32[]{:S(2)}) async-start(), calls=%async_computation | async-start | bytes 4718592 | tf_op jit(solution)/shard_map/all_gather | solution.py:505
  7.9 320.9 %all-gather.5.cloned.1.call-start = ((), (), s32[]{:S(2)}) async-start(), calls=%async_computation.1 | async-start | bytes 4718592 | tf_op jit(solution)/shard_map/all_gather | solution.py:504
  10.7 46.4 %collective-permute-start.6 = (bf16[4,928,256]{2,1,0:T(8,128)(2,1)}, bf16[4,928,256]{2,1,0:T(8,128)(2,1)S(1)}, u32[]{:S(2)}, u32[]{:S(2)}) collective-permute-start(bf16[4,928,256]{2,1,0:T(8,128)(2,1)} %pad_maximum_fusion.1.refs_0_.refs_6_), channel_id=1, source_target_pairs={{8,16},{16,8},{9,17},{17,9},{10,18},{18,10},{11,19},{19,11},{12,20... | collective-permute-start | bytes 5701640 | tf_op jit(solution)/shard_map/ppermute | solution.py:29
  14.2 47.8 %collective-permute-start.5 = (bf16[4,928,256]{2,1,0:T(8,128)(2,1)}, bf16[4,928,256]{2,1,0:T(8,128)(2,1)}, u32[]{:S(2)}, u32[]{:S(2)}) collective-permute-start(bf16[4,928,256]{2,1,0:T(8,128)(2,1)} %pad_maximum_fusion.1.refs_0_.refs_6_), channel_id=1, source_target_pairs={{0,8},{8,0},{16,24},{24,16},{1,9},{9,1},{17,25},{25,17},{2,10},{10... | collective-permute-start | bytes 5701640 | tf_op jit(solution)/shard_map/ppermute | solution.py:29
  18.4 81.3 %collective-permute-start = (bf16[4,928,256]{2,1,0:T(8,128)(2,1)}, bf16[4,928,256]{2,1,0:T(8,128)(2,1)}, u32[]{:S(2)}, u32[]{:S(2)}) collective-permute-start(bf16[4,928,256]{2,1,0:T(8,128)(2,1)} %pad_maximum_fusion.refs_0_.refs_6_), channel_id=1, source_target_pairs={{0,8},{8,0},{16,24},{24,16},{1,9},{9,1},{17,25},{25,17},{2,10},{10... | collective-permute-start | bytes 5701640 | tf_op jit(solution)/shard_map/ppermute | solution.py:29
  20.5 81.6 %collective-permute-start.1 = (bf16[4,928,256]{2,1,0:T(8,128)(2,1)}, bf16[4,928,256]{2,1,0:T(8,128)(2,1)}, u32[]{:S(2)}, u32[]{:S(2)}) collective-permute-start(bf16[4,928,256]{2,1,0:T(8,128)(2,1)} %pad_maximum_fusion.refs_0_.refs_6_), channel_id=1, source_target_pairs={{8,16},{16,8},{9,17},{17,9},{10,18},{18,10},{11,19},{19,11},{12,20... | collective-permute-start | bytes 5701640 | tf_op jit(solution)/shard_map/ppermute | solution.py:29
  57.1 1.3 copy-start.2
  62.0 78.3 %collective-permute-start.7 = (bf16[4,928,256]{2,1,0:T(8,128)(2,1)}, bf16[4,928,256]{2,1,0:T(8,128)(2,1)S(1)}, u32[]{:S(2)}, u32[]{:S(2)}) collective-permute-start(bf16[4,928,256]{2,1,0:T(8,128)(2,1)} %convert_select_fusion.1), channel_id=1, source_target_pairs={{0,8},{8,0},{16,24},{24,16},{1,9},{9,1},{17,25},{25,17},{2,10},{10... | collective-permute-start | bytes 5701640 | tf_op jit(solution)/shard_map/ppermute | solution.py:29
  62.0 85.4 %collective-permute-start.8 = (bf16[4,928,256]{2,1,0:T(8,128)(2,1)}, bf16[4,928,256]{2,1,0:T(8,128)(2,1)}, u32[]{:S(2)}, u32[]{:S(2)}) collective-permute-start(bf16[4,928,256]{2,1,0:T(8,128)(2,1)} %shard_map.106.refs_1_.refs_7_), channel_id=1, source_target_pairs={{8,16},{16,8},{9,17},{17,9},{10,18},{18,10},{11,19},{19,11},{12,20... | collective-permute-start | bytes 5701640 | tf_op jit(solution)/shard_map/ppermute | solution.py:29
  99.7 79.8 %collective-permute-start.3 = (bf16[4,928,256]{2,1,0:T(8,128)(2,1)}, bf16[4,928,256]{2,1,0:T(8,128)(2,1)}, u32[]{:S(2)}, u32[]{:S(2)}) collective-permute-start(bf16[4,928,256]{2,1,0:T(8,128)(2,1)} %shard_map.103.refs_1_.refs_7_), channel_id=1, source_target_pairs={{8,16},{16,8},{9,17},{17,9},{10,18},{18,10},{11,19},{19,11},{12,20... | collective-permute-start | bytes 5701640 | tf_op jit(solution)/shard_map/ppermute | solution.py:29
  106.2 76.3 %collective-permute-start.2 = (bf16[4,928,256]{2,1,0:T(8,128)(2,1)}, bf16[4,928,256]{2,1,0:T(8,128)(2,1)}, u32[]{:S(2)}, u32[]{:S(2)}) collective-permute-start(bf16[4,928,256]{2,1,0:T(8,128)(2,1)} %convert_select_fusion.3), channel_id=1, source_target_pairs={{0,8},{8,0},{16,24},{24,16},{1,9},{9,1},{17,25},{25,17},{2,10},{10... | collective-permute-start | bytes 5701640 | tf_op jit(solution)/shard_map/ppermute | solution.py:29
  123.0 24.5 %copy-start.8 = (f32[4,928,256]{2,1,0:T(8,128)S(1)}, f32[4,928,256]{2,1,0:T(8,128)}, u32[]{:S(2)}) copy-start(f32[4,928,256]{2,1,0:T(8,128)} %shard_map.107.refs_12_) | copy-start | bytes 11403268
  140.3 4.5 copy-start.1
  144.8 34.6 %copy-start.3 = (f32[4,928,256]{2,1,0:T(8,128)S(1)}, f32[4,928,256]{2,1,0:T(8,128)}, u32[]{:S(2)}) copy-start(f32[4,928,256]{2,1,0:T(8,128)} %shard_map.104) | copy-start | bytes 11403268
  144.8 75.3 %collective-permute-start.15 = (bf16[4,928,256]{2,1,0:T(8,128)(2,1)}, bf16[4,928,256]{2,1,0:T(8,128)(2,1)}, u32[]{:S(2)}, u32[]{:S(2)}) collective-permute-start(bf16[4,928,256]{2,1,0:T(8,128)(2,1)} %add_convert_fusion.1), channel_id=1, source_target_pairs={{8,16},{16,8},{9,17},{17,9},{10,18},{18,10},{11,19},{19,11},{12,20... | collective-permute-start | bytes 5701640 | tf_op jit(solution)/shard_map/ppermute | solution.py:29
  150.5 32.0 %copy-start.6 = (f32[4,928,256]{2,1,0:T(8,128)S(1)}, f32[4,928,256]{2,1,0:T(8,128)}, u32[]{:S(2)}) copy-start(f32[4,928,256]{2,1,0:T(8,128)} %shard_map.102.refs_1_.refs_12_) | copy-start | bytes 11403268
  150.5 77.1 %collective-permute-start.9 = (bf16[4,928,256]{2,1,0:T(8,128)(2,1)}, bf16[4,928,256]{2,1,0:T(8,128)(2,1)S(1)}, u32[]{:S(2)}, u32[]{:S(2)}) collective-permute-start(bf16[4,928,256]{2,1,0:T(8,128)(2,1)} %convert_select_fusion), channel_id=1, source_target_pairs={{0,8},{8,0},{16,24},{24,16},{1,9},{9,1},{17,25},{25,17},{2,10},{10... | collective-permute-start | bytes 5701640 | tf_op jit(solution)/shard_map/ppermute | solution.py:29
  182.4 78.7 %collective-permute-start.4 = (bf16[4,928,256]{2,1,0:T(8,128)(2,1)}, bf16[4,928,256]{2,1,0:T(8,128)(2,1)}, u32[]{:S(2)}, u32[]{:S(2)}) collective-permute-start(bf16[4,928,256]{2,1,0:T(8,128)(2,1)} %convert_select_fusion.2), channel_id=1, source_target_pairs={{0,8},{8,0},{16,24},{24,16},{1,9},{9,1},{17,25},{25,17},{2,10},{10... | collective-permute-start | bytes 5701640 | tf_op jit(solution)/shard_map/ppermute | solution.py:29
  185.7 81.0 %collective-permute-start.11 = (bf16[4,928,256]{2,1,0:T(8,128)(2,1)}, bf16[4,928,256]{2,1,0:T(8,128)(2,1)}, u32[]{:S(2)}, u32[]{:S(2)}) collective-permute-start(bf16[4,928,256]{2,1,0:T(8,128)(2,1)} %add_convert_fusion.5), channel_id=1, source_target_pairs={{8,16},{16,8},{9,17},{17,9},{10,18},{18,10},{11,19},{19,11},{12,20... | collective-permute-start | bytes 5701640 | tf_op jit(solution)/shard_map/ppermute | solution.py:29
  189.8 37.8 %copy-start.9 = (f32[4,928,256]{2,1,0:T(8,128)S(1)}, f32[4,928,256]{2,1,0:T(8,128)}, u32[]{:S(2)}) copy-start(f32[4,928,256]{2,1,0:T(8,128)} %shard_map.107.refs_12_) | copy-start | bytes 11403268
  224.5 36.6 %copy-start.4 = (f32[4,928,256]{2,1,0:T(8,128)S(1)}, f32[4,928,256]{2,1,0:T(8,128)}, u32[]{:S(2)}) copy-start(f32[4,928,256]{2,1,0:T(8,128)} %shard_map.104) | copy-start | bytes 11403268
  224.5 101.3 %collective-permute-start.16 = (bf16[4,928,256]{2,1,0:T(8,128)(2,1)}, bf16[4,928,256]{2,1,0:T(8,128)(2,1)}, u32[]{:S(2)}, u32[]{:S(2)}) collective-permute-start(bf16[4,928,256]{2,1,0:T(8,128)(2,1)} %add_convert_fusion), channel_id=1, source_target_pairs={{8,0},{16,24},{9,1},{17,25},{10,2},{18,26},{11,3},{19,27},{12,4},{... | collective-permute-start | bytes 5701640 | tf_op jit(solution)/shard_map/ppermute | solution.py:29
  227.6 1.9 copy-start
  229.5 37.3 %copy-start.7 = (f32[4,928,256]{2,1,0:T(8,128)S(1)}, f32[4,928,256]{2,1,0:T(8,128)}, u32[]{:S(2)}) copy-start(f32[4,928,256]{2,1,0:T(8,128)} %shard_map.102.refs_1_.refs_12_) | copy-start | bytes 11403268
  229.5 93.1 %collective-permute-start.14 = (bf16[4,928,256]{2,1,0:T(8,128)(2,1)}, bf16[4,928,256]{2,1,0:T(8,128)(2,1)}, u32[]{:S(2)}, u32[]{:S(2)}) collective-permute-start(bf16[4,928,256]{2,1,0:T(8,128)(2,1)} %add_convert_fusion.3), channel_id=1, source_target_pairs={{8,16},{16,8},{9,17},{17,9},{10,18},{18,10},{11,19},{19,11},{12,20... | collective-permute-start | bytes 5701640 | tf_op jit(solution)/shard_map/ppermute | solution.py:29
  264.3 95.9 %collective-permute-start.10 = (bf16[4,928,256]{2,1,0:T(8,128)(2,1)}, bf16[4,928,256]{2,1,0:T(8,128)(2,1)}, u32[]{:S(2)}, u32[]{:S(2)}) collective-permute-start(bf16[4,928,256]{2,1,0:T(8,128)(2,1)} %add_convert_fusion.6), channel_id=1, source_target_pairs={{8,16},{16,8},{9,17},{17,9},{10,18},{18,10},{11,19},{19,11},{12,20... | collective-permute-start | bytes 5701640 | tf_op jit(solution)/shard_map/ppermute | solution.py:29
  270.0 94.8 %collective-permute-start.12 = (bf16[4,928,256]{2,1,0:T(8,128)(2,1)}, bf16[4,928,256]{2,1,0:T(8,128)(2,1)}, u32[]{:S(2)}, u32[]{:S(2)}) collective-permute-start(bf16[4,928,256]{2,1,0:T(8,128)(2,1)} %add_convert_fusion.4), channel_id=1, source_target_pairs={{8,0},{16,24},{9,1},{17,25},{10,2},{18,26},{11,3},{19,27},{12,4},{... | collective-permute-start | bytes 5701640 | tf_op jit(solution)/shard_map/ppermute | solution.py:29
  308.6 14.0 %copy-start.10 = (f32[4,928,256]{2,1,0:T(8,128)S(1)}, f32[4,928,256]{2,1,0:T(8,128)}, u32[]{:S(2)}) copy-start(f32[4,928,256]{2,1,0:T(8,128)} %shard_map.107.refs_12_) | copy-start | bytes 11403268
  325.8 74.0 %collective-permute-start.17 = (bf16[4,928,256]{2,1,0:T(8,128)(2,1)}, bf16[4,928,256]{2,1,0:T(8,128)(2,1)}, u32[]{:S(2)}, u32[]{:S(2)}) collective-permute-start(bf16[4,928,256]{2,1,0:T(8,128)(2,1)} %shard_map.113), channel_id=1, source_target_pairs={{8,0},{16,24},{9,1},{17,25},{10,2},{18,26},{11,3},{19,27},{12,4},{... | collective-permute-start | bytes 5701640 | tf_op jit(solution)/shard_map/ppermute | solution.py:29
  328.8 31.5 %copy-start.5 = (f32[4,928,256]{2,1,0:T(8,128)S(1)}, f32[4,928,256]{2,1,0:T(8,128)}, u32[]{:S(2)}) copy-start(f32[4,928,256]{2,1,0:T(8,128)} %shard_map.104) | copy-start | bytes 11403268
  363.4 70.1 %collective-permute-start.23 = (bf16[2,928,256]{2,1,0:T(8,128)(2,1)}, bf16[2,928,256]{2,1,0:T(8,128)(2,1)S(1)}, u32[]{:S(2)}, u32[]{:S(2)}) collective-permute-start(bf16[2,928,256]{2,1,0:T(8,128)(2,1)} %shard_map.118), channel_id=1, source_target_pairs={{8,0},{16,24},{9,1},{17,25},{10,2},{18,26},{11,3},{19,27},{12,4},{... | collective-permute-start | bytes 2850824 | tf_op jit(solution)/shard_map/ppermute | solution.py:29
  364.8 85.5 %collective-permute-start.13 = (bf16[2,928,256]{2,1,0:T(8,128)(2,1)}, bf16[2,928,256]{2,1,0:T(8,128)(2,1)S(1)}, u32[]{:S(2)}, u32[]{:S(2)}) collective-permute-start(bf16[2,928,256]{2,1,0:T(8,128)(2,1)} %shard_map.112), channel_id=1, source_target_pairs={{8,0},{16,24},{9,1},{17,25},{10,2},{18,26},{11,3},{19,27},{12,4},{... | collective-permute-start | bytes 2850824 | tf_op jit(solution)/shard_map/ppermute | solution.py:29
  433.5 1.0 copy-start.14
  448.8 34.4 %collective-permute-start.24 = (bf16[2,256,2048]{2,1,0:T(8,128)(2,1)}, bf16[2,256,2048]{2,1,0:T(8,128)(2,1)S(1)}, u32[]{:S(2)}, u32[]{:S(2)}) collective-permute-start(bf16[2,256,2048]{2,1,0:T(8,128)(2,1)} %get-tuple-element.37), channel_id=1, source_target_pairs={{0,2},{1,3},{4,6},{5,7},{8,10},{9,11},{12,14},{13,15},{16,18},{17,... | collective-permute-start | bytes 6291464 | tf_op jit(solution)/shard_map/ppermute | solution.py:451
  450.3 1.0 copy-start.13
  465.8 22.1 %collective-permute-start.18 = (bf16[2,256,2048]{2,1,0:T(8,128)(2,1)}, bf16[2,256,2048]{2,1,0:T(8,128)(2,1)}, u32[]{:S(2)}, u32[]{:S(2)}) collective-permute-start(bf16[2,256,2048]{2,1,0:T(8,128)(2,1)} %get-tuple-element.35), channel_id=1, source_target_pairs={{2,0},{3,1},{6,4},{7,5},{10,8},{11,9},{14,12},{15,13},{18,16},{19,... | collective-permute-start | bytes 6291464 | tf_op jit(solution)/shard_map/ppermute | solution.py:451
  483.2 4.7 copy-start.11
  486.4 11.1 %collective-permute-start.25 = (bf16[1,2,128,1024]{3,2,1,0:T(8,128)(2,1)S(1)}, bf16[1,2,128,1024]{3,2,1,0:T(8,128)(2,1)S(1)}, u32[]{:S(2)}, u32[]{:S(2)}) collective-permute-start(bf16[1,2,128,1024]{3,2,1,0:T(8,128)(2,1)S(1)} %dynamic-slice_convert_fusion.1), channel_id=1, source_target_pairs={{2,6},{3,7},{6,2},{7,3},{10,14},{11,15},{14,10},{15,11},{18,22},{1... | collective-permute-start | bytes 1572872 | tf_op jit(solution)/shard_map/ppermute | solution.py:427
  487.2 11.2 %collective-permute-start.27 = (bf16[2,1,128,1024]{3,2,1,0:T(8,128)(2,1)S(1)}, bf16[2,1,128,1024]{3,2,1,0:T(8,128)(2,1)S(1)}, u32[]{:S(2)}, u32[]{:S(2)}) collective-permute-start(bf16[2,1,128,1024]{3,2,1,0:T(8,128)(2,1)S(1)} %dynamic-slice_convert_fusion), channel_id=1, source_target_pairs={{2,3},{3,2},{6,7},{7,6},{10,11},{11,10},{14,15},{15,14},{18,19},{1... | collective-permute-start | bytes 1572872 | tf_op jit(solution)/shard_map/ppermute | solution.py:427
  490.6 13.9 %collective-permute-start.19 = (bf16[1,2,128,1024]{3,2,1,0:T(8,128)(2,1)S(1)}, bf16[1,2,128,1024]{3,2,1,0:T(8,128)(2,1)S(1)}, u32[]{:S(2)}, u32[]{:S(2)}) collective-permute-start(bf16[1,2,128,1024]{3,2,1,0:T(8,128)(2,1)S(1)} %dynamic-slice_convert_fusion.3), channel_id=1, source_target_pairs={{0,4},{1,5},{4,0},{5,1},{8,12},{9,13},{12,8},{13,9},{16,20},{17,21... | collective-permute-start | bytes 1572872 | tf_op jit(solution)/shard_map/ppermute | solution.py:427
  494.1 14.8 %collective-permute-start.21 = (bf16[2,1,128,1024]{3,2,1,0:T(8,128)(2,1)S(1)}, bf16[2,1,128,1024]{3,2,1,0:T(8,128)(2,1)S(1)}, u32[]{:S(2)}, u32[]{:S(2)}) collective-permute-start(bf16[2,1,128,1024]{3,2,1,0:T(8,128)(2,1)S(1)} %dynamic-slice_convert_fusion.2), channel_id=1, source_target_pairs={{0,1},{1,0},{4,5},{5,4},{8,9},{9,8},{12,13},{13,12},{16,17},{17,16... | collective-permute-start | bytes 1572872 | tf_op jit(solution)/shard_map/ppermute | solution.py:427
  497.7 14.1 %collective-permute-start.26 = (bf16[1,1,128,1024]{3,2,1,0:T(8,128)(2,1)S(1)}, bf16[1,1,128,1024]{3,2,1,0:T(8,128)(2,1)S(1)}, u32[]{:S(2)}, u32[]{:S(2)}) collective-permute-start(bf16[1,1,128,1024]{3,2,1,0:T(8,128)(2,1)S(1)} %dynamic-slice_convert_fusion.5), channel_id=1, source_target_pairs={{2,3},{3,2},{6,7},{7,6},{10,11},{11,10},{14,15},{15,14},{18,19},{1... | collective-permute-start | bytes 786440 | tf_op jit(solution)/shard_map/ppermute | solution.py:427
  498.6 13.3 %collective-permute-start.28 = (bf16[1,1,128,1024]{3,2,1,0:T(8,128)(2,1)S(1)}, bf16[1,1,128,1024]{3,2,1,0:T(8,128)(2,1)S(1)}, u32[]{:S(2)}, u32[]{:S(2)}) collective-permute-start(bf16[1,1,128,1024]{3,2,1,0:T(8,128)(2,1)S(1)} %dynamic-slice_convert_fusion.4), channel_id=1, source_target_pairs={{2,6},{3,7},{6,2},{7,3},{10,14},{11,15},{14,10},{15,11},{18,22},{1... | collective-permute-start | bytes 786440 | tf_op jit(solution)/shard_map/ppermute | solution.py:427
  504.7 8.6 %collective-permute-start.20 = (bf16[1,1,128,1024]{3,2,1,0:T(8,128)(2,1)S(1)}, bf16[1,1,128,1024]{3,2,1,0:T(8,128)(2,1)S(1)}, u32[]{:S(2)}, u32[]{:S(2)}) collective-permute-start(bf16[1,1,128,1024]{3,2,1,0:T(8,128)(2,1)S(1)} %dynamic-slice_convert_fusion.7), channel_id=1, source_target_pairs={{0,1},{1,0},{4,5},{5,4},{8,9},{9,8},{12,13},{13,12},{16,17},{17,16... | collective-permute-start | bytes 786440 | tf_op jit(solution)/shard_map/ppermute | solution.py:427
  509.1 8.3 %collective-permute-start.22 = (bf16[1,1,128,1024]{3,2,1,0:T(8,128)(2,1)S(1)}, bf16[1,1,128,1024]{3,2,1,0:T(8,128)(2,1)S(1)}, u32[]{:S(2)}, u32[]{:S(2)}) collective-permute-start(bf16[1,1,128,1024]{3,2,1,0:T(8,128)(2,1)S(1)} %dynamic-slice_convert_fusion.6), channel_id=1, source_target_pairs={{0,4},{1,5},{4,0},{5,1},{8,12},{9,13},{12,8},{13,9},{16,20},{17,21... | collective-permute-start | bytes 786440 | tf_op jit(solution)/shard_map/ppermute | solution.py:427
Sparse Core Ops, SparseCore 0:
  9.9 37.8 all-gather.2
  62.1 38.3 all-gather.4

commit v3 on v2

--- a/solution.py
+++ b/solution.py
@@ -64,11 +64,6 @@
 
 def columns(index, width):
     return pl.ds(pl.multiple_of(index * width, width), width)
-
-
-def valid_rows(value, rows, block):
-    at = lax.broadcasted_iota(jnp.int32, value.shape, 0) + pl.program_id(0) * block
-    return jnp.where(at < rows, value, jnp.zeros_like(value))
 
 
 def down_kernel(factors, k_ref, *refs):
@@ -95,14 +90,26 @@
         ).astype(jnp.bfloat16)
 
 
-def main_kernel(rows, has_acc, k_ref, *refs):
+def main_kernel(has_acc, k_ref, *refs):
     gates, uppers = refs[:6], refs[6:12]
-    part, r1, r2, r3, x_ref, wg_ref, wu_ref = refs[12:19]
+    part, r1, r2, r3, x_hbm, wg_ref, wu_ref = refs[12:19]
     acc_in = refs[19] if has_acc else None
-    acc, gate_out, up_out, gate_grad, up_grad = refs[-5:]
+    acc_out, gate_out, up_out = refs[-11:-8]
+    gate_grad, up_grad, gate_turned, up_turned, x_ref, acc, sems, out_sems = refs[-8:]
     block, width = gates[0].shape
-    ragged = rows % block != 0
     end = k_ref[1] == 1
+    first = pl.program_id(0) == 0
+    x_copy = pltpu.make_async_copy(x_hbm, x_ref, sems.at[0])
+    acc_copy = pltpu.make_async_copy(acc_in, acc, sems.at[1]) if has_acc else None
+
+    @pl.when(first)
+    def _():
+        x_copy.start()
+        if has_acc:
+            acc_copy.start()
+        else:
+            acc[...] = jnp.zeros_like(acc)
+
     for slot in range(4):
         gate, upper = slot_value(end, gates, slot), slot_value(end, uppers, slot)
         j = place(k_ref, slot)
@@ -117,84 +124,88 @@
         gate_value = (
             hidden_grad * upper * sigma * (1.0 + gate * (1.0 - sigma))
         ).astype(jnp.bfloat16)
-        if ragged:
-            up_value = valid_rows(up_value, rows, block)
-            gate_value = valid_rows(gate_value, rows, block)
         up_grad[:, at] = up_value
         gate_grad[:, at] = gate_value
-
-    @pl.when(pl.program_id(0) == 0)
-    def _():
-        if has_acc:
-            acc[...] = acc_in[...]
-        else:
-            acc[...] = jnp.zeros_like(acc)
+        up_turned[at, :] = up_value.T
+        gate_turned[at, :] = gate_value.T
 
     features = x_ref.shape[1]
     step = min(features, 512)
-    for c in range(0, features, step):
-        cols = slice(c, c + step)
+    tiles = [slice(c, c + step) for c in range(0, features, step)]
+
+    @pl.when(first)
+    def _():
+        x_copy.wait()
+
+    for cols in tiles:
         gate_out[:, cols] = jnp.dot(
             gate_grad[...], x_ref[:, cols], preferred_element_type=jnp.float32
         ).astype(jnp.bfloat16)
+
+    if has_acc:
+
+        @pl.when(first)
+        def _():
+            acc_copy.wait()
+
+    last = pl.program_id(0) == pl.num_programs(0) - 1
+    out_copies = [
+        pltpu.make_async_copy(acc.at[:, cols], acc_out.at[:, cols], out_sems.at[i])
+        for i, cols in enumerate(tiles)
+    ]
+    for i, cols in enumerate(tiles):
+        acc[:, cols] += jnp.dot(
+            gate_turned[...], wg_ref[:, cols], preferred_element_type=jnp.float32
+        ) + jnp.dot(
+            up_turned[...], wu_ref[:, cols], preferred_element_type=jnp.float32
+        )
+        pl.when(last)(out_copies[i].start)
+
+    for cols in tiles:
         up_out[:, cols] = jnp.dot(
             up_grad[...], x_ref[:, cols], preferred_element_type=jnp.float32
         ).astype(jnp.bfloat16)
-        wg, wu = wg_ref[:, cols], wu_ref[:, cols]
-        if ragged:
-            wg, wu = valid_rows(wg, rows, block), valid_rows(wu, rows, block)
-        dims = (((0,), (0,)), ((), ()))
-        acc[:, cols] += lax.dot_general(
-            gate_grad[...], wg, dims, preferred_element_type=jnp.float32
-        ) + lax.dot_general(
-            up_grad[...], wu, dims, preferred_element_type=jnp.float32
-        )
-
-
-def token_kernel(rows, block, *refs):
+
+    @pl.when(last)
+    def _():
+        for copy in out_copies:
+            copy.wait()
+
+
+def token_kernel(rows, *refs):
     up_factor, gate_factor, part, r1, r2, r3, wg_ref, wu_ref, acc_in = refs[1:10]
     k_ref, (gate_out, up_out, acc, rounded, gate_grad, up_grad) = refs[0], refs[10:]
-    count, _, width = part.shape
-    ragged = rows % block != 0
+    count, size, width = part.shape
+    ragged = rows < size
     end = k_ref[1] == 1
-    for j in range(count):
-        hidden_grad = (
-            part[j]
-            + r2[j].astype(jnp.float32)
-            + jnp.where(end, r3[j], r1[j]).astype(jnp.float32)
-        )
-        up_value = (hidden_grad * up_factor[j]).astype(jnp.bfloat16)
-        gate_value = (hidden_grad * gate_factor[j]).astype(jnp.bfloat16)
-        if ragged:
-            up_value = valid_rows(up_value, rows, block)
-            gate_value = valid_rows(gate_value, rows, block)
-        up_out[j] = up_value
-        gate_out[j] = gate_value
-        up_grad[:, j * width : (j + 1) * width] = up_value
-        gate_grad[:, j * width : (j + 1) * width] = gate_value
+
+    def valid(value):
+        if not ragged:
+            return value
+        at = lax.broadcasted_iota(jnp.int32, value.shape, 0)
+        return jnp.where(at < rows, value, jnp.zeros_like(value))
 
     @pl.when(pl.program_id(0) == 0)
     def _():
-        acc[...] = acc_in[...]
-
-    features = wg_ref.shape[1]
-    step = min(features, 512)
-    for c in range(0, features, step):
-        cols = slice(c, c + step)
-        wg, wu = wg_ref[:, cols], wu_ref[:, cols]
-        if ragged:
-            wg, wu = valid_rows(wg, rows, block), valid_rows(wu, rows, block)
-        dims = (((0,), (0,)), ((), ()))
-        more = lax.dot_general(
-            gate_grad[...], wg, dims, preferred_element_type=jnp.float32
-        ) + lax.dot_general(
-            up_grad[...], wu, dims, preferred_element_type=jnp.float32
-        )
-        acc[:, :, cols] += more.reshape(count, width, step)
-
-    @pl.when(pl.program_id(0) == pl.num_programs(0) - 1)
-    def _():
-        rounded[...] = acc[...].astype(jnp.bfloat16)
+        for j in range(count):
+            hidden_grad = (
+                part[j]
+                + r2[j].astype(jnp.float32)
+                + jnp.where(end, r3[j], r1[j]).astype(jnp.float32)
+            )
+            up_value = valid((hidden_grad * up_factor[j]).astype(jnp.bfloat16))
+            gate_value = valid((hidden_grad * gate_factor[j]).astype(jnp.bfloat16))
+            up_out[j] = up_value
+            gate_out[j] = gate_value
+            up_grad[j * width : (j + 1) * width, :] = up_value.T
+            gate_grad[j * width : (j + 1) * width, :] = gate_value.T
+
+    more = jnp.dot(
+        gate_grad[...], valid(wg_ref[...]), preferred_element_type=jnp.float32
+    ) + jnp.dot(up_grad[...], valid(wu_ref[...]), preferred_element_type=jnp.float32)
+    value = acc_in[...] + more.reshape(acc.shape)
+    acc[...] = value
+    rounded[...] = value.astype(jnp.bfloat16)
 
 
 def weight_kernel(parts, *refs):
@@ -240,9 +251,9 @@
     )(w_down, grad_whole)
 
 
-def slot_specs(a, block, width):
-    gate = pl.BlockSpec((None, block, width), lambda i, k: (a % 2, i, 0))
-    upper = pl.BlockSpec((None, block, width), lambda i, k: (2 + a % 2, i, 0))
+def slot_specs(a, block, width, at=0):
+    gate = pl.BlockSpec((None, block, width), lambda i, k: (a % 2, at + i, 0))
+    upper = pl.BlockSpec((None, block, width), lambda i, k: (2 + a % 2, at + i, 0))
     return [gate] * 6 + [upper] * 6
 
 
@@ -285,38 +296,47 @@
     )(k, *args)
 
 
-def main_group(k, slots, sums, x_whole, wg, wu, acc, outs, a, size, total):
+def main_group(k, slots, sums, r3, x_whole, wg, wu, acc, outs, a, run, size, total):
     tokens, features = x_whole.shape
     count, _, width = slots[0].shape
     block = block_rows(size)
-    blocks = size // block
-    wide = pl.BlockSpec((count, block, width), lambda i, k: (0, i, 0))
-    weight = pl.BlockSpec((block, features), lambda i, k: (a * blocks + i, 0))
+    base = a * (size // block) + run[0]
+    blocks = run[1] - run[0]
+    wide = pl.BlockSpec((count, block, width), lambda i, k: (0, run[0] + i, 0))
+    weight = pl.BlockSpec((block, features), lambda i, k: (base + i, 0))
     specs = (
-        slot_specs(a, block, width)
-        + [wide] * 4
-        + [once((tokens, features)), weight, weight]
-    )
-    args = list(slots) * 2 + list(sums) + [x_whole, wg, wu]
+        slot_specs(a, block, width, run[0])
+        + [wide] * 3
+        + [pl.BlockSpec((count, block, width), lambda i, k: (0, i, 0))]
+        + [pl.BlockSpec(memory_space=pl.ANY), weight, weight]
+    )
+    args = list(slots) * 2 + list(sums) + [r3, x_whole, wg, wu]
     aliases = {}
     if acc is not None:
         aliases[1 + len(args)] = 0
         args.append(acc)
-        specs.append(once((tokens, features)))
+        specs.append(pl.BlockSpec(memory_space=pl.ANY))
         for i, out in enumerate(outs):
             aliases[1 + len(args)] = 1 + i
             args.append(out)
             specs.append(pl.BlockSpec(memory_space=pl.ANY))
     wgrad = jax.ShapeDtypeStruct((total, features), jnp.bfloat16)
-    rows = min(size, total - a * size)
+    size = blocks * block
     return pl.pallas_call(
-        functools.partial(main_kernel, rows, acc is not None),
+        functools.partial(main_kernel, acc is not None),
         grid_spec=pltpu.PrefetchScalarGridSpec(
             num_scalar_prefetch=1,
             grid=(blocks,),
             in_specs=specs,
-            out_specs=(once((tokens, features)), weight, weight),
-            scratch_shapes=[pltpu.VMEM((block, tokens), jnp.bfloat16)] * 2,
+            out_specs=(pl.BlockSpec(memory_space=pl.ANY), weight, weight),
+            scratch_shapes=[pltpu.VMEM((block, tokens), jnp.bfloat16)] * 2
+            + [pltpu.VMEM((tokens, block), jnp.bfloat16)] * 2
+            + [
+                pltpu.VMEM((tokens, features), jnp.bfloat16),
+                pltpu.VMEM((tokens, features), jnp.float32),
+                pltpu.SemaphoreType.DMA((2,)),
+                pltpu.SemaphoreType.DMA((-(-features // min(features, 512)),)),
+            ],
         ),
         out_shape=(
             jax.ShapeDtypeStruct((tokens, features), jnp.float32),
@@ -336,39 +356,37 @@
 def token_group(k, factors, sums, r3, wg, wu, acc, q, a, size, total):
     tokens, features = acc.shape
     count, _, width = r3.shape
-    block = block_rows(size)
-    blocks = size // block
+    step = min(features, 512)
     parts = tokens // (count * width)
 
     def split(value):
         return value.reshape((count, parts) + value.shape[1:])
 
-    some = pl.BlockSpec((count, None, block, width), lambda i, k: (0, q, i, 0))
-    wide = pl.BlockSpec((count, block, width), lambda i, k: (0, i, 0))
-    weight = pl.BlockSpec((block, features), lambda i, k: (a * blocks + i, 0))
+    kept = pl.Buffered(1)
+    some = pl.BlockSpec(
+        (count, None, size, width), lambda i, k: (0, q, 0, 0), pipeline_mode=kept
+    )
+    wide = pl.BlockSpec(
+        (count, size, width), lambda i, k: (0, 0, 0), pipeline_mode=kept
+    )
+    weight = pl.BlockSpec((size, step), lambda i, k: (a, i))
     rows = min(size, total - a * size)
     grad = jax.ShapeDtypeStruct((count, size, width), jnp.bfloat16)
-    whole = pl.BlockSpec(
-        (count, width, features),
-        lambda i, k: (0, 0, 0),
-        pipeline_mode=pl.Buffered(1),
-    )
+    whole = pl.BlockSpec((count, width, step), lambda i, k: (0, 0, i))
     return pl.pallas_call(
-        functools.partial(token_kernel, rows, block),
+        functools.partial(token_kernel, rows),
         grid_spec=pltpu.PrefetchScalarGridSpec(
             num_scalar_prefetch=1,
-            grid=(blocks,),
+            grid=(-(-features // step),),
             in_specs=[some] * 5
             + [wide, weight, weight]
             + [
                 pl.BlockSpec(
-                    (count, None, width, features),
-                    lambda i, k: (0, q, 0, 0),
-                    pipeline_mode=pl.Buffered(1),
+                    (count, None, width, step), lambda i, k: (0, q, 0, i)
                 )
             ],
             out_specs=[wide, wide, whole, whole],
-            scratch_shapes=[pltpu.VMEM((block, count * width), jnp.bfloat16)] * 2,
+            scratch_shapes=[pltpu.VMEM((count * width, size), jnp.bfloat16)] * 2,
         ),
         out_shape=[
             grad,
@@ -393,7 +411,7 @@
     )
 
 
-def weight_group(grads, x_whole, out, a, size):
+def weight_group(grads, x_whole, out, a, size, after):
     tokens, features = x_whole.shape
     count, _, width = grads[0].shape
     block = block_rows(size)
@@ -403,7 +421,8 @@
         functools.partial(weight_kernel, len(grads)),
         grid=(blocks,),
         in_specs=[wide] * len(grads)
-        + [once((tokens, features)), pl.BlockSpec(memory_space=pl.ANY)],
+        + [once((tokens, features)), pl.BlockSpec(memory_space=pl.ANY)]
+        + [pl.BlockSpec(memory_space=pl.ANY)] * len(after),
         out_specs=pl.BlockSpec((block, features), lambda i: (a * blocks + i, 0)),
         scratch_shapes=[pltpu.VMEM((block, tokens), jnp.bfloat16)],
         out_shape=jax.ShapeDtypeStruct(out.shape, out.dtype),
@@ -414,7 +433,7 @@
             bytes_accessed=size * (features * 2 + tokens * 2),
             transcendentals=0,
         ),
-    )(*grads, x_whole, out)
+    )(*grads, x_whole, out, *after)
 
 
 def halve(value, axis, bit, mine, pairs):
@@ -448,7 +467,8 @@
     features = value.shape[-1]
     blocks = (n_wt // 2, n_dep, -1, features)
     value = value.reshape(blocks)
-    got = lax.ppermute(rounded, ("wt", "dep"), inward).reshape(blocks)
+    first = lax.ppermute(rounded, ("wt", "dep"), inward)
+    got = first.reshape(blocks)
 
     def over_wt(part):
         bit = 2
@@ -469,8 +489,10 @@
     half = features // 2
     one = value[..., :half] + got[..., :half].astype(jnp.float32)
     two = value[..., half:] + got[..., half:].astype(jnp.float32)
-    one, two = over_dep(over_wt(one)), over_wt(over_dep(two))
-    return jnp.concatenate([one[0, 0], two[0, 0]], axis=-1)
+    one, two = over_wt(one), over_dep(two)
+    stages = [first, one]
+    one, two = over_dep(one), over_wt(two)
+    return jnp.concatenate([one[0, 0], two[0, 0]], axis=-1), stages
 
 
 def own_half(gate, upper, half, size):
@@ -522,10 +544,10 @@
             outward = part[step - 2].astype(jnp.bfloat16)
             payload = jnp.where(end, outward, middle[step - 2])
             swap.append(send(payload, SWAP))
-        elif step < 9:
+        elif step < 8:
             payload = rounded(part[step - 6], middle[step - 2])
-            if step == 8:
-                payload = tie(payload, swap[6], down)
+            if step == 7:
+                payload = tie(payload, down)
             swap.append(send(payload, TO_ENDS))
         if 4 <= step < 8:
             middle.append(send(rounded(part[step - 4], swap[step - 2]), MIDDLE))
@@ -535,38 +557,52 @@
                     k, slots_of(a), grad_whole, down, a, size, total, a == last
                 )
 
-    def main(a, acc, wgrads):
-        sums = [part[a], swap[2 + a], middle[4 + a], swap[6 + a]]
-        acc, *wgrads = main_group(
-            k, slots_of(a), sums, x_whole, wg, wu, acc, wgrads, a, size, total
-        )
+    block = block_rows(size)
+    blocks = size // block
+    halves = [(0, blocks // 2), (blocks // 2, blocks)]
+    halves = [run for run in halves if run[0] < run[1]]
+
+    def main(a, run, r3, acc, wgrads):
+        sums = [part[a], swap[2 + a], middle[4 + a]]
+        args = (k, slots_of(a), sums, r3, x_whole, wg, wu, acc, wgrads)
+        acc, *wgrads = main_group(*args, a, run, size, total)
         return acc, wgrads
 
     def pieces(value):
         return value.reshape((2, 2) + value.shape[1:])
 
+    inner = []
+    for i, run in enumerate(halves):
+        rows = slice(run[0] * block, run[1] * block)
+        payload = rounded(part[2][:, rows], middle[6][:, rows])
+        payload = tie(payload, swap[6], down) if i == 0 else tie(payload, inner[0][1])
+        inner.append((run, payload, send(payload, TO_ENDS)))
+    acc, wgrads = main(0, (0, blocks), swap[6], acc, wgrads)
     final = []
     for q in range(2):
         payload = rounded(pieces(part[last])[:, q], pieces(middle[4 + last])[:, q])
-        if q == 0:
-            payload = tie(payload, swap[7])
-        else:
-            acc, wgrads = main(0, acc, wgrads)
-            payload = tie(payload, acc)
+        if q == 1:
+            acc, wgrads = main(1, (0, blocks), swap[7], acc, wgrads)
+        payload = tie(payload, swap[7], acc)
         final.append(send(payload, TO_ENDS))
-    for a in range(1, last):
-        acc, wgrads = main(a, acc, wgrads)
+    for run, _, r3 in inner:
+        acc, wgrads = main(2, run, r3, acc, wgrads)
     sums = [part[last], swap[2 + last], middle[4 + last]]
-    gate_grads, up_grads, shares = [], [], []
+    gate_grads, up_grads, shares, arrived = [], [], [], []
     for q in range(2):
         gate_part, up_part, value, small = token_group(
             k, factors, sums, final[q], wg, wu, acc, q, last, size, total
         )
         gate_grads.append(gate_part)
         up_grads.append(up_part)
-        shares.append(scatter_half(value, small, q, n_wt, n_dep))
-    gate_wgrad = weight_group(gate_grads, x_whole, wgrads[0], last, size)
-    up_wgrad = weight_group(up_grads, x_whole, wgrads[1], last, size)
+        share, stages = scatter_half(value, small, q, n_wt, n_dep)
+        shares.append(share)
+        arrived.append(stages)
+    behind = [arrived[0][0]], [arrived[0][1], arrived[1][1]]
+    gate_wgrad, up_wgrad = (
+        weight_group(grads, x_whole, out, last, size, after)
+        for grads, out, after in zip((gate_grads, up_grads), wgrads, behind)
+    )
     input_grad = jnp.where(lax.axis_index("wt") % 2 == 0, *shares)
     return (input_grad.astype(jnp.bfloat16), gate_wgrad.T, up_wgrad.T, down)
 

time: 535 us -> 551 us (1.030)
  the two profiles are of different devices: /device:TPU:8 before, /device:TPU:15 now
where the time goes in v3:
time: 551 us; the launch traced here: 542 us
  Pallas kernels  225 us (41%)
  waiting for transfers between devices  169 us (31%)
  starting transfers between devices  59.6 us (11%)
  other arithmetic  59.3 us (11%)
  between operations  15.3 us (3%)
  local copies, waits for them, and re-layouts  12.9 us (2%)
    ppermute x20, waiting for transfers between devices, send(): return lax.ppermute(value, 'inp', pairs)  143 us
    pallas_call x4, Pallas kernels, main_group(): pl.pallas_call(functools.partial(main_kernel, acc is not None), grid_spec...  99.4 us
    pallas_call x4, Pallas kernels, down_group(): pl.pallas_call(functools.partial(down_kernel, factors), grid_spec=pltpu.P...  48.8 us
    ppermute x20, starting transfers between devices, send(): return lax.ppermute(value, 'inp', pairs)  37.6 us
    pallas_call x4, Pallas kernels, sum_group(): pl.pallas_call(sum_kernel, grid=(blocks,), in_specs=[pl.BlockSpec((block,...  33.5 us
    convert_element_type x8, other arithmetic, rounded(): return (part + got.astype(jnp.float32)).astype(jnp.bfloat16)  28.3 us
    pallas_call x2, Pallas kernels, token_group(): pl.pallas_call(functools.partial(token_kernel, rows), grid_spec=pltpu.Pre...  27.2 us
    all_gather x1, waiting for transfers between devices, per_device(): lax.all_gather(out_grad, ('wt', 'dep'), axis=0, tiled=True)  25.6 us
  transfers between devices with their start and end apart: 32, of which 7 were waited for; matrix products, arithmetic and copies ran while one was open for 12% of the time, Pallas kernels for 42%

profile of v3, /device:TPU:15, one launch (start us, length us, event | category | flops | bytes accessed | tf_op | source)
XLA Modules:
  0.0 541.9 jit_solution(6654254819911559032)
XLA Ops:
  10.8 3.2 collective-permute-start.6
  21.7 25.6 %all-gather.3.cloned.1.call-done.grad_ref.refs_12_ = bf16[1024,2048]{1,0:T(8,128)(2,1)} async-done(((bf16[128,2048]{1,0:T(8,128)(2,1)}), bf16[1024,2048]{1,0:T(8,128)(2,1)}) %all-gather.3.cloned.1.call-update) | async-done | bytes 4194320 | tf_op jit(solution)/shard_map/all_gather | solution.py:527
  47.2 8.4 %shard_map.105.refs_1_.refs_12_ = f32[4,928,256]{2,1,0:T(8,128)} custom-call(bf16[3696,2048]{1,0:T(8,128)(2,1)} %w_ref.7, bf16[1024,2048]{1,0:T(8,128)(2,1)} %all-gather.3.cloned.1.call-done.grad_ref.refs_12_), custom_call_target="tpu_custom_call" | custom-call | flops 3892314112 | bytes 7602176 | tf_op jit(solution)/shard_map/pallas_call | solution.py:236
  56.9 3.6 convert_select_fusion.1
  60.8 4.1 collective-permute-start.8
  64.9 8.4 %shard_map.102.refs_1_.refs_12_ = f32[4,928,256]{2,1,0:T(8,128)} custom-call(bf16[3696,2048]{1,0:T(8,128)(2,1)} %w_ref.7, bf16[1024,2048]{1,0:T(8,128)(2,1)} %all-gather.3.cloned.1.call-done.grad_ref.refs_12_), custom_call_target="tpu_custom_call" | custom-call | flops 3892314112 | bytes 7602176 | tf_op jit(solution)/shard_map/pallas_call | solution.py:236
  73.2 23.8 %collective-permute-done.refs_0_ = bf16[4,928,256]{2,1,0:T(8,128)(2,1)} collective-permute-done((bf16[4,928,256]{2,1,0:T(8,128)(2,1)}, bf16[4,928,256]{2,1,0:T(8,128)(2,1)}, u32[]{:S(2)}, u32[]{:S(2)}) %collective-permute-start) | collective-permute-done | bytes 1900576 | tf_op jit(solution)/shard_map/ppermute | solution.py:29
  99.1 4.2 convert_select_fusion.3
  103.3 8.4 %shard_map.107.refs_12_ = f32[4,928,256]{2,1,0:T(8,128)} custom-call(bf16[3696,2048]{1,0:T(8,128)(2,1)} %w_ref.7, bf16[1024,2048]{1,0:T(8,128)(2,1)} %all-gather.3.cloned.1.call-done.grad_ref.refs_12_), custom_call_target="tpu_custom_call" | custom-call | flops 3892314112 | bytes 7602176 | tf_op jit(solution)/shard_map/pallas_call | solution.py:236
  111.7 8.4 %shard_map.104 = f32[4,928,256]{2,1,0:T(8,128)} custom-call(bf16[3696,2048]{1,0:T(8,128)(2,1)} %w_ref.7, bf16[1024,2048]{1,0:T(8,128)(2,1)} %all-gather.3.cloned.1.call-done.grad_ref.refs_12_), custom_call_target="tpu_custom_call" | custom-call | flops 3892314112 | bytes 7602176 | tf_op jit(solution)/shard_map/pallas_call | solution.py:236
  120.1 17.7 %collective-permute-done.7.refs_2_.refs_8_.refs_13_ = bf16[4,928,256]{2,1,0:T(8,128)(2,1)S(1)} collective-permute-done((bf16[4,928,256]{2,1,0:T(8,128)(2,1)}, bf16[4,928,256]{2,1,0:T(8,128)(2,1)S(1)}, u32[]{:S(2)}, u32[]{:S(2)}) %collective-permute-start.7) | collective-permute-done | bytes 1900576 | tf_op jit(solution)/shard_map/ppermute | solution.py:29
  137.8 4.5 add_convert_fusion.2
  142.2 2.3 collective-permute-start.13
  144.6 3.0 convert_select_fusion
  147.6 29.8 %collective-permute-done.3.refs_3_.refs_9_ = bf16[4,928,256]{2,1,0:T(8,128)(2,1)} collective-permute-done((bf16[4,928,256]{2,1,0:T(8,128)(2,1)}, bf16[4,928,256]{2,1,0:T(8,128)(2,1)}, u32[]{:S(2)}, u32[]{:S(2)}) %collective-permute-start.3) | collective-permute-done | bytes 1900576 | tf_op jit(solution)/shard_map/ppermute | solution.py:29
  177.4 3.0 convert_select_fusion.2
  181.1 4.5 add_convert_fusion.4
  185.6 3.5 collective-permute-start.11
  189.1 29.0 %collective-permute-done.13.refs_14_ = bf16[4,928,256]{2,1,0:T(8,128)(2,1)} collective-permute-done((bf16[4,928,256]{2,1,0:T(8,128)(2,1)}, bf16[4,928,256]{2,1,0:T(8,128)(2,1)}, u32[]{:S(2)}, u32[]{:S(2)}) %collective-permute-start.13) | collective-permute-done | bytes 1900576 | tf_op jit(solution)/shard_map/ppermute | solution.py:29
  218.2 3.2 add_convert_fusion.1
  221.4 3.0 collective-permute-start.14
  226.3 3.2 collective-permute-start.16
  229.5 30.4 %collective-permute-done.4.refs_4_.refs_10_ = bf16[4,928,256]{2,1,0:T(8,128)(2,1)} collective-permute-done((bf16[4,928,256]{2,1,0:T(8,128)(2,1)}, bf16[4,928,256]{2,1,0:T(8,128)(2,1)}, u32[]{:S(2)}, u32[]{:S(2)}) %collective-permute-start.4) | collective-permute-done | bytes 1900576 | tf_op jit(solution)/shard_map/ppermute | solution.py:29
  259.9 3.2 add_convert_fusion.5
  265.2 11.6 %shard_map.108.refs_13_ = bf16[3696,2048]{1,0:T(8,128)(2,1)} custom-call(s32[2]{0:T(128)} %pad_add_fusion.k_ref.refs_0_, bf16[4,928,256]{2,1,0:T(8,128)(2,1)} %pad_maximum_fusion.1.refs_0_.refs_6_, bf16[4,928,256]{2,1,0:T(8,128)(2,1)} %shard_map.106.refs_1_.refs_7_, bf16[4,928,256]{2,1,0:T(8,128)(2,1)} %copy-done.1, ...), custom_call_target="tpu_custom_call" | custom-call | flops 3892314112 | bytes 7602176 | tf_op jit(solution)/shard_map/pallas_call | solution.py:275
  276.8 11.6 %shard_map.109.refs_13_.refs_1_ = bf16[3696,2048]{1,0:T(8,128)(2,1)} custom-call(s32[2]{0:T(128)} %pad_add_fusion.k_ref.refs_0_, bf16[4,928,256]{2,1,0:T(8,128)(2,1)} %pad_maximum_fusion.1.refs_0_.refs_6_, bf16[4,928,256]{2,1,0:T(8,128)(2,1)} %shard_map.106.refs_1_.refs_7_, bf16[4,928,256]{2,1,0:T(8,128)(2,1)} %copy-done.1, ...), custom_call_target="tpu_custom_call", output_to_operand_aliasing={{}: (14, {})} | custom-call | flops 3892314112 | bytes 7602176 | tf_op jit(solution)/shard_map/pallas_call | solution.py:275
  288.4 3.3 add_convert_fusion.3.refs_0_
  291.7 3.3 collective-permute-start.12
  295.0 11.6 %shard_map.110.refs_13_ = bf16[3696,2048]{1,0:T(8,128)(2,1)} custom-call(s32[2]{0:T(128)} %pad_add_fusion.k_ref.refs_0_, bf16[4,928,256]{2,1,0:T(8,128)(2,1)} %pad_maximum_fusion.refs_0_.refs_6_, bf16[4,928,256]{2,1,0:T(8,128)(2,1)} %shard_map.103.refs_1_.refs_7_, ...), custom_call_target="tpu_custom_call", output_to_operand_aliasing={{}: (14, {})} | custom-call | flops 3892314112 | bytes 7602176 | tf_op jit(solution)/shard_map/pallas_call | solution.py:275
  306.7 14.0 %shard_map.111 = (bf16[3696,2048]{1,0:T(8,128)(2,1)}, f32[4,928,256]{2,1,0:T(8,128)}, f32[4,928,256]{2,1,0:T(8,128)}) custom-call(s32[2]{0:T(128)} %pad_add_fusion.k_ref.refs_0_, bf16[4,928,256]{2,1,0:T(8,128)(2,1)} %pad_maximum_fusion.refs_0_.refs_6_, bf16[4,928,256]{2,1,0:T(8,128)(2,1)} %shard_map.103.refs_1_.refs_7_, ...), custom_call_target="tpu_custom_call", output_to_operand_aliasing={{0}: (14, {})} | custom-call | flops 3892314112 | bytes 7602176 | tf_op jit(solution)/shard_map/pallas_call | solution.py:275
  320.7 3.3 fusion.1
  323.9 2.3 collective-permute-start.18
  328.0 12.4 %collective-permute-done.10 = bf16[4,928,256]{2,1,0:T(8,128)(2,1)} collective-permute-done((bf16[4,928,256]{2,1,0:T(8,128)(2,1)}, bf16[4,928,256]{2,1,0:T(8,128)(2,1)}, u32[]{:S(2)}, u32[]{:S(2)}) %collective-permute-start.10) | collective-permute-done | bytes 1900576 | tf_op jit(solution)/shard_map/ppermute | solution.py:29
  340.3 4.3 fusion.6
  344.7 30.1 %shard_map.113 = (f32[1024,2048]{1,0:T(8,128)}, bf16[3696,2048]{1,0:T(8,128)(2,1)}, bf16[3696,2048]{1,0:T(8,128)(2,1)}) custom-call(s32[2]{0:T(128)} %pad_add_fusion.k_ref.refs_0_, bf16[4,928,256]{2,1,0:T(8,128)(2,1)} %pad_maximum_fusion.1.refs_0_.refs_6_, bf16[4,928,256]{2,1,0:T(8,128)(2,1)} %shard_map.106.refs_1_.refs_7_, bf16[4,928,256]{2,1,0:T(8,128)(2,1)} %copy-done.1, ...), custom_call_target="tpu_custom_call" | custom-call | flops 15569256448 | bytes 28508160 | tf_op jit(solution)/shard_map/pallas_call | solution.py:325
  376.4 30.7 %shard_map.117 = (f32[1024,2048]{1,0:T(8,128)}, bf16[3696,2048]{1,0:T(8,128)(2,1)}, bf16[3696,2048]{1,0:T(8,128)(2,1)}) custom-call(s32[2]{0:T(128)} %pad_add_fusion.k_ref.refs_0_, bf16[4,928,256]{2,1,0:T(8,128)(2,1)} %pad_maximum_fusion.1.refs_0_.refs_6_, ...), custom_call_target="tpu_custom_call", output_to_operand_aliasing={{0}: (20, {}), {1}: (21, {}), {2}: (22, {})} | custom-call | flops 15569256448 | bytes 28508160 | tf_op jit(solution)/shard_map/pallas_call | solution.py:325
  408.7 19.1 %shard_map.118 = (f32[1024,2048]{1,0:T(8,128)}, bf16[3696,2048]{1,0:T(8,128)(2,1)}, bf16[3696,2048]{1,0:T(8,128)(2,1)}) custom-call(s32[2]{0:T(128)} %pad_add_fusion.k_ref.refs_0_, bf16[4,928,256]{2,1,0:T(8,128)(2,1)} %pad_maximum_fusion.refs_0_.refs_6_, ...), custom_call_target="tpu_custom_call", output_to_operand_aliasing={{0}: (20, {}), {1}: (21, {}), {2}: (22, {})} | custom-call | flops 7784628224 | bytes 14254080 | tf_op jit(solution)/shard_map/pallas_call | solution.py:325
  428.7 19.5 %shard_map.119 = (f32[1024,2048]{1,0:T(8,128)}, bf16[3696,2048]{1,0:T(8,128)(2,1)}, bf16[3696,2048]{1,0:T(8,128)(2,1)}) custom-call(s32[2]{0:T(128)} %pad_add_fusion.k_ref.refs_0_, bf16[4,928,256]{2,1,0:T(8,128)(2,1)} %pad_maximum_fusion.refs_0_.refs_6_, ...), custom_call_target="tpu_custom_call", output_to_operand_aliasing={{0}: (20, {}), {1}: (21, {}), {2}: (22, {})} | custom-call | flops 7784628224 | bytes 14254080 | tf_op jit(solution)/shard_map/pallas_call | solution.py:325
  449.2 13.6 %shard_map.122 = (bf16[2,928,256]{2,1,0:T(8,128)(2,1)}, bf16[2,928,256]{2,1,0:T(8,128)(2,1)}, f32[2,256,2048]{2,1,0:T(8,128)}, bf16[2,256,2048]{2,1,0:T(8,128)(2,1)}) custom-call(s32[2]{0:T(128)} %pad_add_fusion.k_ref.refs_0_, f32[2,2,928,256]{3,2,1,0:T(8,128)} %bitcast.53, f32[2,2,928,256]{3,2,1,0:T(8,128)} %bitcast.55, f32[2,2,928,256]{3,2,1,0:T(8,128)} %bitcast.51, ...), custom_call_target="tpu_custom_call" | custom-call | flops 3892314112 | bytes 18055168 | tf_op jit(solution)/shard_map/pallas_call | solution.py:376
  465.1 13.6 %shard_map.120 = (bf16[2,928,256]{2,1,0:T(8,128)(2,1)}, bf16[2,928,256]{2,1,0:T(8,128)(2,1)}, f32[2,256,2048]{2,1,0:T(8,128)}, bf16[2,256,2048]{2,1,0:T(8,128)(2,1)}) custom-call(s32[2]{0:T(128)} %pad_add_fusion.k_ref.refs_0_, f32[2,2,928,256]{3,2,1,0:T(8,128)} %bitcast.54, f32[2,2,928,256]{3,2,1,0:T(8,128)} %bitcast.56, f32[2,2,928,256]{3,2,1,0:T(8,128)} %bitcast.52, ...), custom_call_target="tpu_custom_call" | custom-call | flops 3892314112 | bytes 18055168 | tf_op jit(solution)/shard_map/pallas_call | solution.py:376
  478.7 4.9 collective-permute-start.19
  483.7 3.6 slice_add_fusion.1
  488.3 2.1 collective-permute-start.26
  494.8 2.1 collective-permute-start.28
  498.5 8.1 %shard_map.123 = bf16[3696,2048]{1,0:T(8,128)(2,1)} custom-call(bf16[2,928,256]{2,1,0:T(8,128)(2,1)} %get-tuple-element.44.refs_0_, bf16[2,928,256]{2,1,0:T(8,128)(2,1)} %get-tuple-element.45.refs_1_, bf16[1024,2048]{1,0:T(8,128)(2,1)} %all-gather.5.cloned.1.call-done.refs_16_.refs_2_, ...), custom_call_target="tpu_custom_call", output_to_operand_aliasing={{}: (3, {})} | custom-call | flops 3892314112 | bytes 5701632 | tf_op jit(solution)/shard_map/pallas_call | solution.py:420
  508.1 3.4 collective-permute-start.27
  513.4 3.1 collective-permute-start.29
  522.3 8.1 %shard_map.124 = bf16[3696,2048]{1,0:T(8,128)(2,1)} custom-call(bf16[2,928,256]{2,1,0:T(8,128)(2,1)} %get-tuple-element.47.refs_0_, bf16[2,928,256]{2,1,0:T(8,128)(2,1)} %get-tuple-element.48.refs_1_, bf16[1024,2048]{1,0:T(8,128)(2,1)} %all-gather.5.cloned.1.call-done.refs_16_.refs_2_, ...), custom_call_target="tpu_custom_call", output_to_operand_aliasing={{}: (3, {})} | custom-call | flops 3892314112 | bytes 5701632 | tf_op jit(solution)/shard_map/pallas_call | solution.py:420
  (141 shorter events, 48.4 us)
Async XLA Ops:
  7.2 40.1 %all-gather.3.cloned.1.call-start = ((), (), s32[]{:S(2)}) async-start(), calls=%async_computation | async-start | bytes 4718592 | tf_op jit(solution)/shard_map/all_gather | solution.py:527
  7.9 336.8 %all-gather.5.cloned.1.call-start = ((), (), s32[]{:S(2)}) async-start(), calls=%async_computation.1 | async-start | bytes 4718592 | tf_op jit(solution)/shard_map/all_gather | solution.py:526
  10.8 44.9 %collective-permute-start.6 = (bf16[4,928,256]{2,1,0:T(8,128)(2,1)}, bf16[4,928,256]{2,1,0:T(8,128)(2,1)S(1)}, u32[]{:S(2)}, u32[]{:S(2)}) collective-permute-start(bf16[4,928,256]{2,1,0:T(8,128)(2,1)} %pad_maximum_fusion.1.refs_0_.refs_6_), channel_id=1, source_target_pairs={{8,16},{16,8},{9,17},{17,9},{10,18},{18,10},{11,19},{19,11},{12,20... | collective-permute-start | bytes 5701640 | tf_op jit(solution)/shard_map/ppermute | solution.py:29
  14.0 46.8 %collective-permute-start.5 = (bf16[4,928,256]{2,1,0:T(8,128)(2,1)}, bf16[4,928,256]{2,1,0:T(8,128)(2,1)}, u32[]{:S(2)}, u32[]{:S(2)}) collective-permute-start(bf16[4,928,256]{2,1,0:T(8,128)(2,1)} %pad_maximum_fusion.1.refs_0_.refs_6_), channel_id=1, source_target_pairs={{0,8},{8,0},{16,24},{24,16},{1,9},{9,1},{17,25},{25,17},{2,10},{10... | collective-permute-start | bytes 5701640 | tf_op jit(solution)/shard_map/ppermute | solution.py:29
  18.1 78.9 %collective-permute-start = (bf16[4,928,256]{2,1,0:T(8,128)(2,1)}, bf16[4,928,256]{2,1,0:T(8,128)(2,1)}, u32[]{:S(2)}, u32[]{:S(2)}) collective-permute-start(bf16[4,928,256]{2,1,0:T(8,128)(2,1)} %pad_maximum_fusion.refs_0_.refs_6_), channel_id=1, source_target_pairs={{0,8},{8,0},{16,24},{24,16},{1,9},{9,1},{17,25},{25,17},{2,10},{10... | collective-permute-start | bytes 5701640 | tf_op jit(solution)/shard_map/ppermute | solution.py:29
  19.6 79.5 %collective-permute-start.1 = (bf16[4,928,256]{2,1,0:T(8,128)(2,1)}, bf16[4,928,256]{2,1,0:T(8,128)(2,1)}, u32[]{:S(2)}, u32[]{:S(2)}) collective-permute-start(bf16[4,928,256]{2,1,0:T(8,128)(2,1)} %pad_maximum_fusion.refs_0_.refs_6_), channel_id=1, source_target_pairs={{8,16},{16,8},{9,17},{17,9},{10,18},{18,10},{11,19},{19,11},{12,20... | collective-permute-start | bytes 5701640 | tf_op jit(solution)/shard_map/ppermute | solution.py:29
  60.5 77.3 %collective-permute-start.7 = (bf16[4,928,256]{2,1,0:T(8,128)(2,1)}, bf16[4,928,256]{2,1,0:T(8,128)(2,1)S(1)}, u32[]{:S(2)}, u32[]{:S(2)}) collective-permute-start(bf16[4,928,256]{2,1,0:T(8,128)(2,1)} %convert_select_fusion.1), channel_id=1, source_target_pairs={{0,8},{8,0},{16,24},{24,16},{1,9},{9,1},{17,25},{25,17},{2,10},{10... | collective-permute-start | bytes 5701640 | tf_op jit(solution)/shard_map/ppermute | solution.py:29
  60.8 83.8 %collective-permute-start.8 = (bf16[4,928,256]{2,1,0:T(8,128)(2,1)}, bf16[4,928,256]{2,1,0:T(8,128)(2,1)}, u32[]{:S(2)}, u32[]{:S(2)}) collective-permute-start(bf16[4,928,256]{2,1,0:T(8,128)(2,1)} %shard_map.106.refs_1_.refs_7_), channel_id=1, source_target_pairs={{8,16},{16,8},{9,17},{17,9},{10,18},{18,10},{11,19},{19,11},{12,20... | collective-permute-start | bytes 5701640 | tf_op jit(solution)/shard_map/ppermute | solution.py:29
  97.0 80.4 %collective-permute-start.3 = (bf16[4,928,256]{2,1,0:T(8,128)(2,1)}, bf16[4,928,256]{2,1,0:T(8,128)(2,1)}, u32[]{:S(2)}, u32[]{:S(2)}) collective-permute-start(bf16[4,928,256]{2,1,0:T(8,128)(2,1)} %shard_map.103.refs_1_.refs_7_), channel_id=1, source_target_pairs={{8,16},{16,8},{9,17},{17,9},{10,18},{18,10},{11,19},{19,11},{12,20... | collective-permute-start | bytes 5701640 | tf_op jit(solution)/shard_map/ppermute | solution.py:29
  103.3 77.8 %collective-permute-start.2 = (bf16[4,928,256]{2,1,0:T(8,128)(2,1)}, bf16[4,928,256]{2,1,0:T(8,128)(2,1)}, u32[]{:S(2)}, u32[]{:S(2)}) collective-permute-start(bf16[4,928,256]{2,1,0:T(8,128)(2,1)} %convert_select_fusion.3), channel_id=1, source_target_pairs={{0,8},{8,0},{16,24},{24,16},{1,9},{9,1},{17,25},{25,17},{2,10},{10... | collective-permute-start | bytes 5701640 | tf_op jit(solution)/shard_map/ppermute | solution.py:29
  120.1 24.5 %copy-start.5 = (f32[4,928,256]{2,1,0:T(8,128)S(1)}, f32[4,928,256]{2,1,0:T(8,128)}, u32[]{:S(2)}) copy-start(f32[4,928,256]{2,1,0:T(8,128)} %shard_map.107.refs_12_) | copy-start | bytes 11403268
  142.2 35.2 %copy-start.3 = (f32[4,928,256]{2,1,0:T(8,128)S(1)}, f32[4,928,256]{2,1,0:T(8,128)}, u32[]{:S(2)}) copy-start(f32[4,928,256]{2,1,0:T(8,128)} %shard_map.104) | copy-start | bytes 11403268
  142.2 75.9 %collective-permute-start.13 = (bf16[4,928,256]{2,1,0:T(8,128)(2,1)}, bf16[4,928,256]{2,1,0:T(8,128)(2,1)}, u32[]{:S(2)}, u32[]{:S(2)}) collective-permute-start(bf16[4,928,256]{2,1,0:T(8,128)(2,1)} %add_convert_fusion.2), channel_id=1, source_target_pairs={{8,16},{16,8},{9,17},{17,9},{10,18},{18,10},{11,19},{19,11},{12,20... | collective-permute-start | bytes 5701640 | tf_op jit(solution)/shard_map/ppermute | solution.py:29
  147.6 76.7 %collective-permute-start.9 = (bf16[4,928,256]{2,1,0:T(8,128)(2,1)}, bf16[4,928,256]{2,1,0:T(8,128)(2,1)S(1)}, u32[]{:S(2)}, u32[]{:S(2)}) collective-permute-start(bf16[4,928,256]{2,1,0:T(8,128)(2,1)} %convert_select_fusion), channel_id=1, source_target_pairs={{0,8},{8,0},{16,24},{24,16},{1,9},{9,1},{17,25},{25,17},{2,10},{10... | collective-permute-start | bytes 5701640 | tf_op jit(solution)/shard_map/ppermute | solution.py:29
  180.4 79.5 %collective-permute-start.4 = (bf16[4,928,256]{2,1,0:T(8,128)(2,1)}, bf16[4,928,256]{2,1,0:T(8,128)(2,1)}, u32[]{:S(2)}, u32[]{:S(2)}) collective-permute-start(bf16[4,928,256]{2,1,0:T(8,128)(2,1)} %convert_select_fusion.2), channel_id=1, source_target_pairs={{0,8},{8,0},{16,24},{24,16},{1,9},{9,1},{17,25},{25,17},{2,10},{10... | collective-permute-start | bytes 5701640 | tf_op jit(solution)/shard_map/ppermute | solution.py:29
  181.1 37.1 %copy-start.8 = (f32[4,928,256]{2,1,0:T(8,128)S(1)}, f32[4,928,256]{2,1,0:T(8,128)}, u32[]{:S(2)}) copy-start(f32[4,928,256]{2,1,0:T(8,128)} %shard_map.105.refs_1_.refs_12_) | copy-start | bytes 11403268
  185.6 38.8 %copy-start.6 = (f32[4,928,256]{2,1,0:T(8,128)S(1)}, f32[4,928,256]{2,1,0:T(8,128)}, u32[]{:S(2)}) copy-start(f32[4,928,256]{2,1,0:T(8,128)} %shard_map.107.refs_12_) | copy-start | bytes 11403268
  185.6 102.8 %collective-permute-start.11 = (bf16[4,928,256]{2,1,0:T(8,128)(2,1)}, bf16[4,928,256]{2,1,0:T(8,128)(2,1)}, u32[]{:S(2)}, u32[]{:S(2)}) collective-permute-start(bf16[4,928,256]{2,1,0:T(8,128)(2,1)} %add_convert_fusion.4), channel_id=1, source_target_pairs={{8,16},{16,8},{9,17},{17,9},{10,18},{18,10},{11,19},{19,11},{12,20... | collective-permute-start | bytes 5701640 | tf_op jit(solution)/shard_map/ppermute | solution.py:29
  221.4 38.6 %copy-start.4 = (f32[4,928,256]{2,1,0:T(8,128)S(1)}, f32[4,928,256]{2,1,0:T(8,128)}, u32[]{:S(2)}) copy-start(f32[4,928,256]{2,1,0:T(8,128)} %shard_map.104) | copy-start | bytes 11403268
  221.4 102.6 %collective-permute-start.14 = (bf16[4,928,256]{2,1,0:T(8,128)(2,1)}, bf16[4,928,256]{2,1,0:T(8,128)(2,1)}, u32[]{:S(2)}, u32[]{:S(2)}) collective-permute-start(bf16[4,928,256]{2,1,0:T(8,128)(2,1)} %add_convert_fusion.1), channel_id=1, source_target_pairs={{8,0},{16,24},{9,1},{17,25},{10,2},{18,26},{11,3},{19,27},{12,4},{... | collective-permute-start | bytes 5701640 | tf_op jit(solution)/shard_map/ppermute | solution.py:29
  226.3 94.3 %collective-permute-start.16 = (bf16[4,928,256]{2,1,0:T(8,128)(2,1)}, bf16[4,928,256]{2,1,0:T(8,128)(2,1)}, u32[]{:S(2)}, u32[]{:S(2)}) collective-permute-start(bf16[4,928,256]{2,1,0:T(8,128)(2,1)} %add_convert_fusion), channel_id=1, source_target_pairs={{8,16},{16,8},{9,17},{17,9},{10,18},{18,10},{11,19},{19,11},{12,20... | collective-permute-start | bytes 5701640 | tf_op jit(solution)/shard_map/ppermute | solution.py:29
  263.2 77.2 %collective-permute-start.10 = (bf16[4,928,256]{2,1,0:T(8,128)(2,1)}, bf16[4,928,256]{2,1,0:T(8,128)(2,1)}, u32[]{:S(2)}, u32[]{:S(2)}) collective-permute-start(bf16[4,928,256]{2,1,0:T(8,128)(2,1)} %add_convert_fusion.5), channel_id=1, source_target_pairs={{8,16},{16,8},{9,17},{17,9},{10,18},{18,10},{11,19},{19,11},{12,20... | collective-permute-start | bytes 5701640 | tf_op jit(solution)/shard_map/ppermute | solution.py:29
  276.8 11.6 %copy-start.9 = (f32[4,928,256]{2,1,0:T(8,128)S(1)}, f32[4,928,256]{2,1,0:T(8,128)}, u32[]{:S(2)}) copy-start(f32[4,928,256]{2,1,0:T(8,128)} %shard_map.102.refs_1_.refs_12_) | copy-start | bytes 11403268
  291.7 83.1 %collective-permute-start.12 = (bf16[4,928,256]{2,1,0:T(8,128)(2,1)}, bf16[4,928,256]{2,1,0:T(8,128)(2,1)}, u32[]{:S(2)}, u32[]{:S(2)}) collective-permute-start(bf16[4,928,256]{2,1,0:T(8,128)(2,1)} %shard_map.112), channel_id=1, source_target_pairs={{8,0},{16,24},{9,1},{17,25},{10,2},{18,26},{11,3},{19,27},{12,4},{... | collective-permute-start | bytes 5701640 | tf_op jit(solution)/shard_map/ppermute | solution.py:29
  306.7 14.0 %copy-start.7 = (f32[4,928,256]{2,1,0:T(8,128)S(1)}, f32[4,928,256]{2,1,0:T(8,128)}, u32[]{:S(2)}) copy-start(f32[4,928,256]{2,1,0:T(8,128)} %shard_map.107.refs_12_) | copy-start | bytes 11403268
  323.9 84.7 %collective-permute-start.18 = (bf16[4,464,256]{2,1,0:T(8,128)(2,1)}, bf16[4,464,256]{2,1,0:T(8,128)(2,1)}, u32[]{:S(2)}, u32[]{:S(2)}) collective-permute-start(bf16[4,464,256]{2,1,0:T(8,128)(2,1)} %shard_map.115.refs_1_), channel_id=1, source_target_pairs={{8,0},{16,24},{9,1},{17,25},{10,2},{18,26},{11,3},{19,27},{12,4},{... | collective-permute-start | bytes 2850824 | tf_op jit(solution)/shard_map/ppermute | solution.py:29
  326.2 101.6 %collective-permute-start.17 = (bf16[4,464,256]{2,1,0:T(8,128)(2,1)}, bf16[4,464,256]{2,1,0:T(8,128)(2,1)S(1)}, u32[]{:S(2)}, u32[]{:S(2)}) collective-permute-start(bf16[4,464,256]{2,1,0:T(8,128)(2,1)} %shard_map.116), channel_id=1, source_target_pairs={{8,0},{16,24},{9,1},{17,25},{10,2},{18,26},{11,3},{19,27},{12,4},{... | collective-permute-start | bytes 2850824 | tf_op jit(solution)/shard_map/ppermute | solution.py:29
  374.8 89.3 %collective-permute-start.15 = (bf16[2,928,256]{2,1,0:T(8,128)(2,1)}, bf16[2,928,256]{2,1,0:T(8,128)(2,1)S(1)}, u32[]{:S(2)}, u32[]{:S(2)}) collective-permute-start(bf16[2,928,256]{2,1,0:T(8,128)(2,1)} %shard_map.114), channel_id=1, source_target_pairs={{8,0},{16,24},{9,1},{17,25},{10,2},{18,26},{11,3},{19,27},{12,4},{... | collective-permute-start | bytes 2850824 | tf_op jit(solution)/shard_map/ppermute | solution.py:29
  407.1 41.2 %collective-permute-start.24 = (bf16[2,928,256]{2,1,0:T(8,128)(2,1)}, bf16[2,928,256]{2,1,0:T(8,128)(2,1)S(1)}, u32[]{:S(2)}, u32[]{:S(2)}) collective-permute-start(bf16[2,928,256]{2,1,0:T(8,128)(2,1)} %shard_map.121), channel_id=1, source_target_pairs={{8,0},{16,24},{9,1},{17,25},{10,2},{18,26},{11,3},{19,27},{12,4},{... | collective-permute-start | bytes 2850824 | tf_op jit(solution)/shard_map/ppermute | solution.py:29
  462.8 20.8 %collective-permute-start.25 = (bf16[2,256,2048]{2,1,0:T(8,128)(2,1)}, bf16[2,256,2048]{2,1,0:T(8,128)(2,1)}, u32[]{:S(2)}, u32[]{:S(2)}) collective-permute-start(bf16[2,256,2048]{2,1,0:T(8,128)(2,1)} %get-tuple-element.43), channel_id=1, source_target_pairs={{0,2},{1,3},{4,6},{5,7},{8,10},{9,11},{12,14},{13,15},{16,18},{17,... | collective-permute-start | bytes 6291464 | tf_op jit(solution)/shard_map/ppermute | solution.py:470
  478.7 11.8 %collective-permute-start.19 = (bf16[2,256,2048]{2,1,0:T(8,128)(2,1)}, bf16[2,256,2048]{2,1,0:T(8,128)(2,1)S(1)}, u32[]{:S(2)}, u32[]{:S(2)}) collective-permute-start(bf16[2,256,2048]{2,1,0:T(8,128)(2,1)} %get-tuple-element.41), channel_id=1, source_target_pairs={{2,0},{3,1},{6,4},{7,5},{10,8},{11,9},{14,12},{15,13},{18,16},{19,... | collective-permute-start | bytes 6291464 | tf_op jit(solution)/shard_map/ppermute | solution.py:470
  483.6 6.8 %copy-start.23 = (f32[2,256,2048]{2,1,0:T(8,128)S(1)}, f32[2,256,2048]{2,1,0:T(8,128)}, u32[]{:S(2)}) copy-start(f32[2,256,2048]{2,1,0:T(8,128)} %get-tuple-element.40) | copy-start | bytes 12582916
  487.3 7.4 %copy-start.17 = (f32[2,2,128,1024]{3,2,1,0:T(8,128)}, f32[2,2,128,1024]{3,2,1,0:T(8,128)S(1)}, u32[]{:S(2)}) copy-start(f32[2,2,128,1024]{3,2,1,0:T(8,128)S(1)} %get-tuple-element.51) | copy-start | bytes 6291460
  488.3 18.3 %collective-permute-start.26 = (bf16[1,2,128,1024]{3,2,1,0:T(8,128)(2,1)}, bf16[1,2,128,1024]{3,2,1,0:T(8,128)(2,1)}, u32[]{:S(2)}, u32[]{:S(2)}) collective-permute-start(bf16[1,2,128,1024]{3,2,1,0:T(8,128)(2,1)} %dynamic-slice_convert_fusion.1), channel_id=1, source_target_pairs={{2,6},{3,7},{6,2},{7,3},{10,14},{11,15},{14,10},{15,11},{18,22},{1... | collective-permute-start | bytes 1572872 | tf_op jit(solution)/shard_map/ppermute | solution.py:446
  492.3 4.8 copy-start.19
  493.2 23.3 %collective-permute-start.20 = (bf16[1,2,128,1024]{3,2,1,0:T(8,128)(2,1)}, bf16[1,2,128,1024]{3,2,1,0:T(8,128)(2,1)}, u32[]{:S(2)}, u32[]{:S(2)}) collective-permute-start(bf16[1,2,128,1024]{3,2,1,0:T(8,128)(2,1)} %dynamic-slice_convert_fusion.3), channel_id=1, source_target_pairs={{0,4},{1,5},{4,0},{5,1},{8,12},{9,13},{12,8},{13,9},{16,20},{17,21... | collective-permute-start | bytes 1572872 | tf_op jit(solution)/shard_map/ppermute | solution.py:446
  494.8 16.7 %collective-permute-start.28 = (bf16[2,1,128,1024]{3,2,1,0:T(8,128)(2,1)S(1)}, bf16[2,1,128,1024]{3,2,1,0:T(8,128)(2,1)}, u32[]{:S(2)}, u32[]{:S(2)}) collective-permute-start(bf16[2,1,128,1024]{3,2,1,0:T(8,128)(2,1)S(1)} %dynamic-slice_convert_fusion), channel_id=1, source_target_pairs={{2,3},{3,2},{6,7},{7,6},{10,11},{11,10},{14,15},{15,14},{18,19},{1... | collective-permute-start | bytes 1572872 | tf_op jit(solution)/shard_map/ppermute | solution.py:446
  497.0 22.9 %collective-permute-start.22 = (bf16[2,1,128,1024]{3,2,1,0:T(8,128)(2,1)S(1)}, bf16[2,1,128,1024]{3,2,1,0:T(8,128)(2,1)}, u32[]{:S(2)}, u32[]{:S(2)}) collective-permute-start(bf16[2,1,128,1024]{3,2,1,0:T(8,128)(2,1)S(1)} %dynamic-slice_convert_fusion.2), channel_id=1, source_target_pairs={{0,1},{1,0},{4,5},{5,4},{8,9},{9,8},{12,13},{13,12},{16,17},{17,16... | collective-permute-start | bytes 1572872 | tf_op jit(solution)/shard_map/ppermute | solution.py:446
  498.5 8.2 %copy-start.22 = (f32[2,2,128,1024]{3,2,1,0:T(8,128)S(1)}, f32[2,2,128,1024]{3,2,1,0:T(8,128)}, u32[]{:S(2)}) copy-start(f32[2,2,128,1024]{3,2,1,0:T(8,128)} %copy-done.21) | copy-start | bytes 6291460
  506.6 4.8 copy-start.18
  508.0 9.8 %copy-start.11 = (f32[1,2,128,1024]{3,2,1,0:T(8,128)}, f32[1,2,128,1024]{3,2,1,0:T(8,128)S(1)}, u32[]{:S(2)}) copy-start(f32[1,2,128,1024]{3,2,1,0:T(8,128)S(1)} %convert_add_fusion.1.refs_5_) | copy-start | bytes 3145732
  508.0 8.6 %copy-start.20 = (f32[2,2,128,1024]{3,2,1,0:T(8,128)S(1)}, f32[2,2,128,1024]{3,2,1,0:T(8,128)}, u32[]{:S(2)}) copy-start(f32[2,2,128,1024]{3,2,1,0:T(8,128)} %copy-done.19) | copy-start | bytes 6291460
  508.1 22.3 %collective-permute-start.27 = (bf16[1,1,128,1024]{3,2,1,0:T(8,128)(2,1)S(1)}, bf16[1,1,128,1024]{3,2,1,0:T(8,128)(2,1)}, u32[]{:S(2)}, u32[]{:S(2)}) collective-permute-start(bf16[1,1,128,1024]{3,2,1,0:T(8,128)(2,1)S(1)} %dynamic-slice_convert_fusion.5), channel_id=1, source_target_pairs={{2,3},{3,2},{6,7},{7,6},{10,11},{11,10},{14,15},{15,14},{18,19},{1... | collective-permute-start | bytes 786440 | tf_op jit(solution)/shard_map/ppermute | solution.py:446
  512.7 7.3 %copy-start.16 = (f32[2,2,128,1024]{3,2,1,0:T(8,128)S(1)}, f32[2,2,128,1024]{3,2,1,0:T(8,128)}, u32[]{:S(2)}) copy-start(f32[2,2,128,1024]{3,2,1,0:T(8,128)} %copy-done.15) | copy-start | bytes 6291460
  513.4 18.1 %collective-permute-start.29 = (bf16[1,1,128,1024]{3,2,1,0:T(8,128)(2,1)}, bf16[1,1,128,1024]{3,2,1,0:T(8,128)(2,1)}, u32[]{:S(2)}, u32[]{:S(2)}) collective-permute-start(bf16[1,1,128,1024]{3,2,1,0:T(8,128)(2,1)} %dynamic-slice_convert_fusion.4), channel_id=1, source_target_pairs={{2,6},{3,7},{6,2},{7,3},{10,14},{11,15},{14,10},{15,11},{18,22},{1... | collective-permute-start | bytes 786440 | tf_op jit(solution)/shard_map/ppermute | solution.py:446
  518.6 14.0 %collective-permute-start.21 = (bf16[1,1,128,1024]{3,2,1,0:T(8,128)(2,1)}, bf16[1,1,128,1024]{3,2,1,0:T(8,128)(2,1)}, u32[]{:S(2)}, u32[]{:S(2)}) collective-permute-start(bf16[1,1,128,1024]{3,2,1,0:T(8,128)(2,1)} %dynamic-slice_convert_fusion.7), channel_id=1, source_target_pairs={{0,1},{1,0},{4,5},{5,4},{8,9},{9,8},{12,13},{13,12},{16,17},{17,16... | collective-permute-start | bytes 786440 | tf_op jit(solution)/shard_map/ppermute | solution.py:446
  521.3 12.4 %collective-permute-start.23 = (bf16[1,1,128,1024]{3,2,1,0:T(8,128)(2,1)S(1)}, bf16[1,1,128,1024]{3,2,1,0:T(8,128)(2,1)S(1)}, u32[]{:S(2)}, u32[]{:S(2)}) collective-permute-start(bf16[1,1,128,1024]{3,2,1,0:T(8,128)(2,1)S(1)} %dynamic-slice_convert_fusion.6), channel_id=1, source_target_pairs={{0,4},{1,5},{4,0},{5,1},{8,12},{9,13},{12,8},{13,9},{16,20},{17,21... | collective-permute-start | bytes 786440 | tf_op jit(solution)/shard_map/ppermute | solution.py:446
  522.3 8.1 %copy-start.12 = (f32[1,2,128,1024]{3,2,1,0:T(8,128)S(1)}, f32[1,2,128,1024]{3,2,1,0:T(8,128)}, u32[]{:S(2)}) copy-start(f32[1,2,128,1024]{3,2,1,0:T(8,128)} %copy-done.11) | copy-start | bytes 3145732
  (14 other events, 33.3 us)
Sparse Core Ops, SparseCore 0:
  9.9 37.2 all-gather.2
  60.9 39.0 all-gather.4

commit v4 on v3

--- a/solution.py
+++ b/solution.py
@@ -436,18 +436,26 @@
     )(*grads, x_whole, out, *after)
 
 
-def halve(value, axis, bit, mine, pairs):
-    size = value.shape[axis]
-    shape = value.shape
-    view = value.reshape(shape[:axis] + (size // (2 * bit), 2, bit) + shape[axis + 1 :])
-    away = lax.dynamic_index_in_dim(view, 1 - mine, axis + 1, keepdims=False)
-    kept = lax.dynamic_index_in_dim(view, mine, axis + 1, keepdims=False)
+def total_of(terms):
+    return functools.reduce(jnp.add, [t.astype(jnp.float32) for t in terms])
+
+
+def halve(terms, axis, mine, pairs):
+    shape = terms[0].shape
+    size = shape[axis]
     rest = shape[:axis] + (size // 2,) + shape[axis + 1 :]
-    got = lax.ppermute(away.reshape(rest).astype(jnp.bfloat16), ("wt", "dep"), pairs)
-    return kept.reshape(rest) + got.astype(jnp.float32)
-
-
-def scatter_half(value, rounded, q, n_wt, n_dep):
+
+    def pick(value, which):
+        view = value.reshape(shape[:axis] + (size // 2, 2) + shape[axis + 1 :])
+        part = lax.dynamic_index_in_dim(view, which, axis + 1, keepdims=False)
+        return part.reshape(rest)
+
+    away = total_of([pick(t, 1 - mine) for t in terms]).astype(jnp.bfloat16)
+    got = lax.ppermute(away, ("wt", "dep"), pairs)
+    return [pick(t, mine) for t in terms] + [got]
+
+
+def scatter_plan(q, n_wt, n_dep):
     at_wt, at_dep = lax.axis_index("wt"), lax.axis_index("dep")
 
     def pairs(bit_wt, bit_dep):
@@ -464,35 +472,16 @@
         for d in range(n_dep)
         if w % 2 != q
     ]
-    features = value.shape[-1]
-    blocks = (n_wt // 2, n_dep, -1, features)
-    value = value.reshape(blocks)
-    first = lax.ppermute(rounded, ("wt", "dep"), inward)
-    got = first.reshape(blocks)
-
-    def over_wt(part):
-        bit = 2
-        while bit < n_wt:
-            mine = (at_wt // bit) % 2
-            part = halve(part, 0, 1, mine, pairs(bit, 0))
-            bit *= 2
-        return part
-
-    def over_dep(part):
-        bit = 1
-        while bit < n_dep:
-            mine = (at_dep // bit) % 2
-            part = halve(part, 1, 1, mine, pairs(0, bit))
-            bit *= 2
-        return part
-
-    half = features // 2
-    one = value[..., :half] + got[..., :half].astype(jnp.float32)
-    two = value[..., half:] + got[..., half:].astype(jnp.float32)
-    one, two = over_wt(one), over_dep(two)
-    stages = [first, one]
-    one, two = over_dep(one), over_wt(two)
-    return jnp.concatenate([one[0, 0], two[0, 0]], axis=-1), stages
+    over_wt, over_dep = [], []
+    bit = 2
+    while bit < n_wt:
+        over_wt.append((0, (at_wt // bit) % 2, pairs(bit, 0)))
+        bit *= 2
+    bit = 1
+    while bit < n_dep:
+        over_dep.append((1, (at_dep // bit) % 2, pairs(0, bit)))
+        bit *= 2
+    return inward, over_wt + over_dep if q == 0 else over_dep + over_wt
 
 
 def own_half(gate, upper, half, size):
@@ -536,7 +525,7 @@
         h = a // 2
         return [own[h], swap[h], swap[2 + h], middle[2 + h], swap[4 + h], middle[h]]
 
-    for step in range(2, 10):
+    for step in range(2, 8):
         if step < 4:
             swap[step - 2] = tie(swap[step - 2], part[step - 2])
             middle.append(send(swap[step - 2], MIDDLE))
@@ -544,67 +533,69 @@
             outward = part[step - 2].astype(jnp.bfloat16)
             payload = jnp.where(end, outward, middle[step - 2])
             swap.append(send(payload, SWAP))
-        elif step < 8:
-            payload = rounded(part[step - 6], middle[step - 2])
+        else:
+            swap.append(send(rounded(part[step - 6], middle[step - 2]), TO_ENDS))
+        if 4 <= step:
             if step == 7:
-                payload = tie(payload, down)
-            swap.append(send(payload, TO_ENDS))
-        if 4 <= step < 8:
+                swap[5] = tie(swap[5], down)
             middle.append(send(rounded(part[step - 4], swap[step - 2]), MIDDLE))
-        if step == 6 or step == 7:
+        if 6 <= step:
             for a in (2 * step - 12, 2 * step - 11):
                 down, *factors = down_group(
                     k, slots_of(a), grad_whole, down, a, size, total, a == last
                 )
 
-    block = block_rows(size)
-    blocks = size // block
-    halves = [(0, blocks // 2), (blocks // 2, blocks)]
-    halves = [run for run in halves if run[0] < run[1]]
-
-    def main(a, run, r3, acc, wgrads):
+    blocks = size // block_rows(size)
+
+    def main(a, acc, wgrads):
         sums = [part[a], swap[2 + a], middle[4 + a]]
-        args = (k, slots_of(a), sums, r3, x_whole, wg, wu, acc, wgrads)
-        acc, *wgrads = main_group(*args, a, run, size, total)
+        args = (k, slots_of(a), sums, swap[6 + a], x_whole, wg, wu, acc, wgrads)
+        acc, *wgrads = main_group(*args, a, (0, blocks), size, total)
         return acc, wgrads
 
     def pieces(value):
         return value.reshape((2, 2) + value.shape[1:])
 
-    inner = []
-    for i, run in enumerate(halves):
-        rows = slice(run[0] * block, run[1] * block)
-        payload = rounded(part[2][:, rows], middle[6][:, rows])
-        payload = tie(payload, swap[6], down) if i == 0 else tie(payload, inner[0][1])
-        inner.append((run, payload, send(payload, TO_ENDS)))
-    acc, wgrads = main(0, (0, blocks), swap[6], acc, wgrads)
+    middle[6] = tie(middle[6], down)
+    swap.append(send(rounded(part[2], middle[6]), TO_ENDS))
+    acc, wgrads = main(0, acc, wgrads)
+    middle[7] = tie(middle[7], acc)
     final = []
     for q in range(2):
-        payload = rounded(pieces(part[last])[:, q], pieces(middle[4 + last])[:, q])
+        payload = rounded(pieces(part[last])[:, q], pieces(middle[7])[:, q])
         if q == 1:
-            acc, wgrads = main(1, (0, blocks), swap[7], acc, wgrads)
-        payload = tie(payload, swap[7], acc)
+            acc, wgrads = main(1, acc, wgrads)
+            payload = tie(payload, acc)
         final.append(send(payload, TO_ENDS))
-    for run, _, r3 in inner:
-        acc, wgrads = main(2, run, r3, acc, wgrads)
+    acc, wgrads = main(2, acc, wgrads)
     sums = [part[last], swap[2 + last], middle[4 + last]]
-    gate_grads, up_grads, shares, arrived = [], [], [], []
+    gate_grads, up_grads, terms, plans = [], [], [], []
     for q in range(2):
         gate_part, up_part, value, small = token_group(
             k, factors, sums, final[q], wg, wu, acc, q, last, size, total
         )
         gate_grads.append(gate_part)
         up_grads.append(up_part)
-        share, stages = scatter_half(value, small, q, n_wt, n_dep)
-        shares.append(share)
-        arrived.append(stages)
-    behind = [arrived[0][0]], [arrived[0][1], arrived[1][1]]
-    gate_wgrad, up_wgrad = (
-        weight_group(grads, x_whole, out, last, size, after)
-        for grads, out, after in zip((gate_grads, up_grads), wgrads, behind)
-    )
-    input_grad = jnp.where(lax.axis_index("wt") % 2 == 0, *shares)
-    return (input_grad.astype(jnp.bfloat16), gate_wgrad.T, up_wgrad.T, down)
+        inward, plan = scatter_plan(q, n_wt, n_dep)
+        view = (n_wt // 2, n_dep, -1, value.shape[-1])
+        got = lax.ppermute(small, ("wt", "dep"), inward)
+        terms.append([value.reshape(view), got.reshape(view)])
+        plans.append(plan)
+
+    def newest():
+        return [t[-1] for t in terms]
+
+    gate_wgrad = weight_group(gate_grads, x_whole, wgrads[0], last, size, newest())
+    for stage in range(len(plans[0])):
+        terms = [halve(t, *plan[stage]) for t, plan in zip(terms, plans)]
+        if stage == 0:
+            for t in terms:
+                t[-1] = tie(t[-1], gate_wgrad)
+            up_wgrad = weight_group(up_grads, x_whole, wgrads[1], last, size, newest())
+    shares = [[t[0, 0] for t in of] for of in terms]
+    even = lax.axis_index("wt") % 2 == 0
+    share = [jnp.where(even, *pair) for pair in zip(*shares)]
+    return (total_of(share).astype(jnp.bfloat16), gate_wgrad.T, up_wgrad.T, down)
 
 
 def solution(mesh):

time: 551 us -> 509 us (0.924)
  the two profiles are of different devices: /device:TPU:15 before, /device:TPU:1 now
where the time goes in v4:
time: 509 us; the launch traced here: 499 us
  Pallas kernels  217 us (43%)
  waiting for transfers between devices  131 us (26%)
  starting transfers between devices  67.3 us (13%)
  other arithmetic  57.2 us (11%)
  between operations  14.7 us (3%)
  local copies, waits for them, and re-layouts  11.7 us (2%)
    ppermute x19, waiting for transfers between devices, send(): return lax.ppermute(value, 'inp', pairs)  101 us
    pallas_call x3, Pallas kernels, main_group(): pl.pallas_call(functools.partial(main_kernel, acc is not None), grid_spec...  92.1 us
    ppermute x19, starting transfers between devices, send(): return lax.ppermute(value, 'inp', pairs)  52.2 us
    pallas_call x4, Pallas kernels, down_group(): pl.pallas_call(functools.partial(down_kernel, factors), grid_spec=pltpu.P...  48 us
    pallas_call x4, Pallas kernels, sum_group(): pl.pallas_call(sum_kernel, grid=(blocks,), in_specs=[pl.BlockSpec((block,...  33.5 us
    convert_element_type x8, other arithmetic, rounded(): return (part + got.astype(jnp.float32)).astype(jnp.bfloat16)  29.4 us
    pallas_call x2, Pallas kernels, token_group(): pl.pallas_call(functools.partial(token_kernel, rows), grid_spec=pltpu.Pre...  27.3 us
    all_gather x1, waiting for transfers between devices, per_device(): lax.all_gather(out_grad, ('wt', 'dep'), axis=0, tiled=True)  27 us
  transfers between devices with their start and end apart: 27, of which 8 were waited for; matrix products, arithmetic and copies ran while one was open for 12% of the time, Pallas kernels for 44%

profile of v4, /device:TPU:1, one launch (start us, length us, event | category | flops | bytes accessed | tf_op | source)
XLA Modules:
  0.0 499.4 jit_solution(16639780400085801730)
XLA Ops:
  11.5 4.6 collective-permute-start.5
  20.2 1.9 collective-permute-start.1
  22.1 27.0 %all-gather.3.cloned.1.call-done.grad_ref.refs_12_ = bf16[1024,2048]{1,0:T(8,128)(2,1)} async-done(((bf16[128,2048]{1,0:T(8,128)(2,1)}), bf16[1024,2048]{1,0:T(8,128)(2,1)}) %all-gather.3.cloned.1.call-update) | async-done | bytes 4194320 | tf_op jit(solution)/shard_map/all_gather | solution.py:516
  49.2 8.3 %shard_map.105.refs_1_.refs_12_ = f32[4,928,256]{2,1,0:T(8,128)} custom-call(bf16[3696,2048]{1,0:T(8,128)(2,1)} %w_ref.7, bf16[1024,2048]{1,0:T(8,128)(2,1)} %all-gather.3.cloned.1.call-done.grad_ref.refs_12_), custom_call_target="tpu_custom_call" | custom-call | flops 3892314112 | bytes 7602176 | tf_op jit(solution)/shard_map/pallas_call | solution.py:236
  58.7 3.6 convert_select_fusion.1
  63.5 2.0 collective-permute-start.8
  65.5 8.4 %shard_map.102.refs_1_.refs_12_ = f32[4,928,256]{2,1,0:T(8,128)} custom-call(bf16[3696,2048]{1,0:T(8,128)(2,1)} %w_ref.7, bf16[1024,2048]{1,0:T(8,128)(2,1)} %all-gather.3.cloned.1.call-done.grad_ref.refs_12_), custom_call_target="tpu_custom_call" | custom-call | flops 3892314112 | bytes 7602176 | tf_op jit(solution)/shard_map/pallas_call | solution.py:236
  73.8 24.1 %collective-permute-done.refs_0_ = bf16[4,928,256]{2,1,0:T(8,128)(2,1)} collective-permute-done((bf16[4,928,256]{2,1,0:T(8,128)(2,1)}, bf16[4,928,256]{2,1,0:T(8,128)(2,1)}, u32[]{:S(2)}, u32[]{:S(2)}) %collective-permute-start) | collective-permute-done | bytes 1900576 | tf_op jit(solution)/shard_map/ppermute | solution.py:29
  98.0 1.9 collective-permute-start.3
  99.9 3.6 convert_select_fusion.3
  105.4 8.4 %shard_map.107.refs_12_ = f32[4,928,256]{2,1,0:T(8,128)} custom-call(bf16[3696,2048]{1,0:T(8,128)(2,1)} %w_ref.7, bf16[1024,2048]{1,0:T(8,128)(2,1)} %all-gather.3.cloned.1.call-done.grad_ref.refs_12_), custom_call_target="tpu_custom_call" | custom-call | flops 3892314112 | bytes 7602176 | tf_op jit(solution)/shard_map/pallas_call | solution.py:236
  113.8 24.8 %collective-permute-done.7.refs_2_.refs_8_.refs_13_ = bf16[4,928,256]{2,1,0:T(8,128)(2,1)S(1)} collective-permute-done((bf16[4,928,256]{2,1,0:T(8,128)(2,1)}, bf16[4,928,256]{2,1,0:T(8,128)(2,1)S(1)}, u32[]{:S(2)}, u32[]{:S(2)}) %collective-permute-start.7) | collective-permute-done | bytes 1900576 | tf_op jit(solution)/shard_map/ppermute | solution.py:29
  138.6 4.5 add_convert_fusion.5
  143.1 1.9 collective-permute-start.11
  146.5 2.9 collective-permute-start.9
  150.0 8.4 %shard_map.104 = f32[4,928,256]{2,1,0:T(8,128)} custom-call(bf16[3696,2048]{1,0:T(8,128)(2,1)} %w_ref.7, bf16[1024,2048]{1,0:T(8,128)(2,1)} %all-gather.3.cloned.1.call-done.grad_ref.refs_12_), custom_call_target="tpu_custom_call" | custom-call | flops 3892314112 | bytes 7602176 | tf_op jit(solution)/shard_map/pallas_call | solution.py:236
  158.4 3.7 convert_select_fusion.2
  162.1 21.5 %collective-permute-start.4 = (bf16[4,928,256]{2,1,0:T(8,128)(2,1)}, bf16[4,928,256]{2,1,0:T(8,128)(2,1)}, u32[]{:S(2)}, u32[]{:S(2)}) collective-permute-start(bf16[4,928,256]{2,1,0:T(8,128)(2,1)} %convert_select_fusion.2), channel_id=1, source_target_pairs={{0,8},{8,0},{16,24},{24,16},{1,9},{9,1},{17,25},{25,17},{2,10},{10... | collective-permute-start | bytes 5701640 | tf_op jit(solution)/shard_map/ppermute | solution.py:29
  183.7 3.3 add_convert_fusion.1
  186.9 2.1 collective-permute-start.16
  189.0 3.2 add_convert_fusion.4
  193.7 26.4 %collective-permute-done.9.refs_4_.refs_10_.refs_13_ = bf16[4,928,256]{2,1,0:T(8,128)(2,1)S(1)} collective-permute-done((bf16[4,928,256]{2,1,0:T(8,128)(2,1)}, bf16[4,928,256]{2,1,0:T(8,128)(2,1)S(1)}, u32[]{:S(2)}, u32[]{:S(2)}) %collective-permute-start.9) | collective-permute-done | bytes 1900576 | tf_op jit(solution)/shard_map/ppermute | solution.py:29
  221.9 1.9 collective-permute-start.14
  223.8 11.6 %shard_map.108.refs_13_ = bf16[3696,2048]{1,0:T(8,128)(2,1)} custom-call(s32[2]{0:T(128)} %pad_add_fusion.k_ref.refs_0_, bf16[4,928,256]{2,1,0:T(8,128)(2,1)} %pad_maximum_fusion.1.refs_0_.refs_6_, bf16[4,928,256]{2,1,0:T(8,128)(2,1)} %shard_map.106.refs_1_.refs_7_, bf16[4,928,256]{2,1,0:T(8,128)(2,1)} %copy-done.1, ...), custom_call_target="tpu_custom_call" | custom-call | flops 3892314112 | bytes 7602176 | tf_op jit(solution)/shard_map/pallas_call | solution.py:275
  235.3 11.2 %shard_map.109.refs_1_.refs_13_ = bf16[3696,2048]{1,0:T(8,128)(2,1)} custom-call(s32[2]{0:T(128)} %pad_add_fusion.k_ref.refs_0_, bf16[4,928,256]{2,1,0:T(8,128)(2,1)} %pad_maximum_fusion.1.refs_0_.refs_6_, bf16[4,928,256]{2,1,0:T(8,128)(2,1)} %shard_map.106.refs_1_.refs_7_, bf16[4,928,256]{2,1,0:T(8,128)(2,1)} %copy-done.1, ...), custom_call_target="tpu_custom_call", output_to_operand_aliasing={{}: (14, {})} | custom-call | flops 3892314112 | bytes 7602176 | tf_op jit(solution)/shard_map/pallas_call | solution.py:275
  246.5 14.3 %collective-permute-done.4.refs_0_ = bf16[4,928,256]{2,1,0:T(8,128)(2,1)} collective-permute-done((bf16[4,928,256]{2,1,0:T(8,128)(2,1)}, bf16[4,928,256]{2,1,0:T(8,128)(2,1)}, u32[]{:S(2)}, u32[]{:S(2)}) %collective-permute-start.4) | collective-permute-done | bytes 1900576 | tf_op jit(solution)/shard_map/ppermute | solution.py:29
  260.9 4.6 add_convert_fusion.6
  266.3 3.3 add_convert_fusion
  270.8 11.6 %shard_map.111.refs_13_ = bf16[3696,2048]{1,0:T(8,128)(2,1)} custom-call(s32[2]{0:T(128)} %pad_add_fusion.k_ref.refs_0_, bf16[4,928,256]{2,1,0:T(8,128)(2,1)} %pad_maximum_fusion.refs_0_.refs_6_, bf16[4,928,256]{2,1,0:T(8,128)(2,1)} %shard_map.103.refs_1_.refs_7_, ...), custom_call_target="tpu_custom_call", output_to_operand_aliasing={{}: (14, {})} | custom-call | flops 3892314112 | bytes 7602176 | tf_op jit(solution)/shard_map/pallas_call | solution.py:275
  282.5 13.6 %shard_map.112 = (bf16[3696,2048]{1,0:T(8,128)(2,1)}, f32[4,928,256]{2,1,0:T(8,128)}, f32[4,928,256]{2,1,0:T(8,128)}) custom-call(s32[2]{0:T(128)} %pad_add_fusion.k_ref.refs_0_, bf16[4,928,256]{2,1,0:T(8,128)(2,1)} %pad_maximum_fusion.refs_0_.refs_6_, bf16[4,928,256]{2,1,0:T(8,128)(2,1)} %shard_map.103.refs_1_.refs_7_, ...), custom_call_target="tpu_custom_call", output_to_operand_aliasing={{0}: (14, {})} | custom-call | flops 3892314112 | bytes 7602176 | tf_op jit(solution)/shard_map/pallas_call | solution.py:275
  296.1 4.4 add_convert_fusion.2
  302.0 30.1 %shard_map.113 = (f32[1024,2048]{1,0:T(8,128)}, bf16[3696,2048]{1,0:T(8,128)(2,1)}, bf16[3696,2048]{1,0:T(8,128)(2,1)}) custom-call(s32[2]{0:T(128)} %pad_add_fusion.k_ref.refs_0_, bf16[4,928,256]{2,1,0:T(8,128)(2,1)} %pad_maximum_fusion.1.refs_0_.refs_6_, bf16[4,928,256]{2,1,0:T(8,128)(2,1)} %shard_map.106.refs_1_.refs_7_, bf16[4,928,256]{2,1,0:T(8,128)(2,1)} %copy-done.1, ...), custom_call_target="tpu_custom_call" | custom-call | flops 15569256448 | bytes 28508160 | tf_op jit(solution)/shard_map/pallas_call | solution.py:325
  333.4 4.4 fusion.8
  337.8 4.5 collective-permute-done.17.refs_15_
  342.3 31.1 %shard_map.116 = (f32[1024,2048]{1,0:T(8,128)}, bf16[3696,2048]{1,0:T(8,128)(2,1)}, bf16[3696,2048]{1,0:T(8,128)(2,1)}) custom-call(s32[2]{0:T(128)} %pad_add_fusion.k_ref.refs_0_, bf16[4,928,256]{2,1,0:T(8,128)(2,1)} %pad_maximum_fusion.1.refs_0_.refs_6_, ...), custom_call_target="tpu_custom_call", output_to_operand_aliasing={{0}: (20, {}), {1}: (21, {}), {2}: (22, {})} | custom-call | flops 15569256448 | bytes 28508160 | tf_op jit(solution)/shard_map/pallas_call | solution.py:325
  376.1 7.0 %collective-permute-done.15.refs_15_ = bf16[4,928,256]{2,1,0:T(8,128)(2,1)} collective-permute-done((bf16[4,928,256]{2,1,0:T(8,128)(2,1)}, bf16[4,928,256]{2,1,0:T(8,128)(2,1)}, u32[]{:S(2)}, u32[]{:S(2)}) %collective-permute-start.15) | collective-permute-done | bytes 1900576 | tf_op jit(solution)/shard_map/ppermute | solution.py:29
  383.1 30.9 %shard_map.117 = (f32[1024,2048]{1,0:T(8,128)}, bf16[3696,2048]{1,0:T(8,128)(2,1)}, bf16[3696,2048]{1,0:T(8,128)(2,1)}) custom-call(s32[2]{0:T(128)} %pad_add_fusion.k_ref.refs_0_, bf16[4,928,256]{2,1,0:T(8,128)(2,1)} %pad_maximum_fusion.refs_0_.refs_6_, ...), custom_call_target="tpu_custom_call", output_to_operand_aliasing={{0}: (20, {}), {1}: (21, {}), {2}: (22, {})} | custom-call | flops 15569256448 | bytes 28508160 | tf_op jit(solution)/shard_map/pallas_call | solution.py:325
  414.9 13.6 %shard_map.120 = (bf16[2,928,256]{2,1,0:T(8,128)(2,1)}, bf16[2,928,256]{2,1,0:T(8,128)(2,1)}, f32[2,256,2048]{2,1,0:T(8,128)}, bf16[2,256,2048]{2,1,0:T(8,128)(2,1)}) custom-call(s32[2]{0:T(128)} %pad_add_fusion.k_ref.refs_0_, f32[2,2,928,256]{3,2,1,0:T(8,128)} %bitcast.80, f32[2,2,928,256]{3,2,1,0:T(8,128)} %bitcast.82, f32[2,2,928,256]{3,2,1,0:T(8,128)} %bitcast.74, ...), custom_call_target="tpu_custom_call" | custom-call | flops 3892314112 | bytes 18055168 | tf_op jit(solution)/shard_map/pallas_call | solution.py:376
  430.8 13.7 %shard_map.118 = (bf16[2,928,256]{2,1,0:T(8,128)(2,1)}, bf16[2,928,256]{2,1,0:T(8,128)(2,1)}, f32[2,256,2048]{2,1,0:T(8,128)}, bf16[2,256,2048]{2,1,0:T(8,128)(2,1)}) custom-call(s32[2]{0:T(128)} %pad_add_fusion.k_ref.refs_0_, f32[2,2,928,256]{3,2,1,0:T(8,128)} %bitcast.81, f32[2,2,928,256]{3,2,1,0:T(8,128)} %bitcast.83, f32[2,2,928,256]{3,2,1,0:T(8,128)} %bitcast.75, ...), custom_call_target="tpu_custom_call" | custom-call | flops 3892314112 | bytes 18055168 | tf_op jit(solution)/shard_map/pallas_call | solution.py:376
  444.5 6.1 %collective-permute-start.19 = (bf16[2,256,2048]{2,1,0:T(8,128)(2,1)}, bf16[2,256,2048]{2,1,0:T(8,128)(2,1)}, u32[]{:S(2)}, u32[]{:S(2)}) collective-permute-start(bf16[2,256,2048]{2,1,0:T(8,128)(2,1)} %get-tuple-element.36), channel_id=1, source_target_pairs={{2,0},{3,1},{6,4},{7,5},{10,8},{11,9},{14,12},{15,13},{18,16},{19,... | collective-permute-start | bytes 6291464 | tf_op jit(solution)/shard_map/ppermute | solution.py:581
  451.9 3.0 fusion.4
  454.9 3.1 collective-permute-start.22
  460.4 8.3 %shard_map.121.refs_1_ = bf16[3696,2048]{1,0:T(8,128)(2,1)} custom-call(bf16[2,928,256]{2,1,0:T(8,128)(2,1)} %get-tuple-element.38.refs_0_, bf16[2,928,256]{2,1,0:T(8,128)(2,1)} %get-tuple-element.39.refs_1_, bf16[1024,2048]{1,0:T(8,128)(2,1)} %all-gather.5.cloned.1.call-done.refs_16_.refs_2_, ...), custom_call_target="tpu_custom_call", output_to_operand_aliasing={{}: (3, {})} | custom-call | flops 3892314112 | bytes 5701632 | tf_op jit(solution)/shard_map/pallas_call | solution.py:420
  468.7 2.3 collective-permute-done.22.refs_0_
  471.9 2.5 fusion.6
  474.4 3.1 collective-permute-start.24
  480.9 8.2 %shard_map.124 = bf16[3696,2048]{1,0:T(8,128)(2,1)} custom-call(bf16[2,928,256]{2,1,0:T(8,128)(2,1)} %get-tuple-element.41.refs_0_, bf16[2,928,256]{2,1,0:T(8,128)(2,1)} %get-tuple-element.42.refs_1_, bf16[1024,2048]{1,0:T(8,128)(2,1)} %all-gather.5.cloned.1.call-done.refs_16_.refs_2_, ...), custom_call_target="tpu_custom_call", output_to_operand_aliasing={{}: (3, {})} | custom-call | flops 3892314112 | bytes 5701632 | tf_op jit(solution)/shard_map/pallas_call | solution.py:420
  489.1 3.2 fusion.5
  (93 shorter events, 36.7 us)
Async XLA Ops:
  7.2 2.1 copy-start.15
  7.2 42.0 %all-gather.3.cloned.1.call-start = ((), (), s32[]{:S(2)}) async-start(), calls=%async_computation | async-start | bytes 4718592 | tf_op jit(solution)/shard_map/all_gather | solution.py:516
  7.9 294.1 %all-gather.5.cloned.1.call-start = ((), (), s32[]{:S(2)}) async-start(), calls=%async_computation.1 | async-start | bytes 4718592 | tf_op jit(solution)/shard_map/all_gather | solution.py:515
  10.7 46.8 %collective-permute-start.6 = (bf16[4,928,256]{2,1,0:T(8,128)(2,1)}, bf16[4,928,256]{2,1,0:T(8,128)(2,1)S(1)}, u32[]{:S(2)}, u32[]{:S(2)}) collective-permute-start(bf16[4,928,256]{2,1,0:T(8,128)(2,1)} %pad_maximum_fusion.1.refs_0_.refs_6_), channel_id=1, source_target_pairs={{8,16},{16,8},{9,17},{17,9},{10,18},{18,10},{11,19},{19,11},{12,20... | collective-permute-start | bytes 5701640 | tf_op jit(solution)/shard_map/ppermute | solution.py:29
  11.5 52.0 %collective-permute-start.5 = (bf16[4,928,256]{2,1,0:T(8,128)(2,1)}, bf16[4,928,256]{2,1,0:T(8,128)(2,1)}, u32[]{:S(2)}, u32[]{:S(2)}) collective-permute-start(bf16[4,928,256]{2,1,0:T(8,128)(2,1)} %pad_maximum_fusion.1.refs_0_.refs_6_), channel_id=1, source_target_pairs={{0,8},{8,0},{16,24},{24,16},{1,9},{9,1},{17,25},{25,17},{2,10},{10... | collective-permute-start | bytes 5701640 | tf_op jit(solution)/shard_map/ppermute | solution.py:29
  20.2 77.8 %collective-permute-start = (bf16[4,928,256]{2,1,0:T(8,128)(2,1)}, bf16[4,928,256]{2,1,0:T(8,128)(2,1)}, u32[]{:S(2)}, u32[]{:S(2)}) collective-permute-start(bf16[4,928,256]{2,1,0:T(8,128)(2,1)} %pad_maximum_fusion.refs_0_.refs_6_), channel_id=1, source_target_pairs={{0,8},{8,0},{16,24},{24,16},{1,9},{9,1},{17,25},{25,17},{2,10},{10... | collective-permute-start | bytes 5701640 | tf_op jit(solution)/shard_map/ppermute | solution.py:29
  20.2 79.7 %collective-permute-start.1 = (bf16[4,928,256]{2,1,0:T(8,128)(2,1)}, bf16[4,928,256]{2,1,0:T(8,128)(2,1)}, u32[]{:S(2)}, u32[]{:S(2)}) collective-permute-start(bf16[4,928,256]{2,1,0:T(8,128)(2,1)} %pad_maximum_fusion.refs_0_.refs_6_), channel_id=1, source_target_pairs={{8,16},{16,8},{9,17},{17,9},{10,18},{18,10},{11,19},{19,11},{12,20... | collective-permute-start | bytes 5701640 | tf_op jit(solution)/shard_map/ppermute | solution.py:29
  57.5 1.2 copy-start.2
  62.3 76.3 %collective-permute-start.7 = (bf16[4,928,256]{2,1,0:T(8,128)(2,1)}, bf16[4,928,256]{2,1,0:T(8,128)(2,1)S(1)}, u32[]{:S(2)}, u32[]{:S(2)}) collective-permute-start(bf16[4,928,256]{2,1,0:T(8,128)(2,1)} %convert_select_fusion.1), channel_id=1, source_target_pairs={{0,8},{8,0},{16,24},{24,16},{1,9},{9,1},{17,25},{25,17},{2,10},{10... | collective-permute-start | bytes 5701640 | tf_op jit(solution)/shard_map/ppermute | solution.py:29
  63.5 81.5 %collective-permute-start.8 = (bf16[4,928,256]{2,1,0:T(8,128)(2,1)}, bf16[4,928,256]{2,1,0:T(8,128)(2,1)}, u32[]{:S(2)}, u32[]{:S(2)}) collective-permute-start(bf16[4,928,256]{2,1,0:T(8,128)(2,1)} %shard_map.106.refs_1_.refs_7_), channel_id=1, source_target_pairs={{8,16},{16,8},{9,17},{17,9},{10,18},{18,10},{11,19},{19,11},{12,20... | collective-permute-start | bytes 5701640 | tf_op jit(solution)/shard_map/ppermute | solution.py:29
  98.0 60.4 %collective-permute-start.3 = (bf16[4,928,256]{2,1,0:T(8,128)(2,1)}, bf16[4,928,256]{2,1,0:T(8,128)(2,1)}, u32[]{:S(2)}, u32[]{:S(2)}) collective-permute-start(bf16[4,928,256]{2,1,0:T(8,128)(2,1)} %shard_map.103.refs_1_.refs_7_), channel_id=1, source_target_pairs={{8,16},{16,8},{9,17},{17,9},{10,18},{18,10},{11,19},{19,11},{12,20... | collective-permute-start | bytes 5701640 | tf_op jit(solution)/shard_map/ppermute | solution.py:29
  103.5 80.1 %collective-permute-start.2 = (bf16[4,928,256]{2,1,0:T(8,128)(2,1)}, bf16[4,928,256]{2,1,0:T(8,128)(2,1)}, u32[]{:S(2)}, u32[]{:S(2)}) collective-permute-start(bf16[4,928,256]{2,1,0:T(8,128)(2,1)} %convert_select_fusion.3), channel_id=1, source_target_pairs={{0,8},{8,0},{16,24},{24,16},{1,9},{9,1},{17,25},{25,17},{2,10},{10... | collective-permute-start | bytes 5701640 | tf_op jit(solution)/shard_map/ppermute | solution.py:29
  113.8 31.2 %copy-start.6 = (f32[4,928,256]{2,1,0:T(8,128)S(1)}, f32[4,928,256]{2,1,0:T(8,128)}, u32[]{:S(2)}) copy-start(f32[4,928,256]{2,1,0:T(8,128)} %shard_map.107.refs_12_) | copy-start | bytes 11403268
  138.6 4.5 copy-start.1
  143.1 45.9 %collective-permute-start.11 = (bf16[4,928,256]{2,1,0:T(8,128)(2,1)}, bf16[4,928,256]{2,1,0:T(8,128)(2,1)}, u32[]{:S(2)}, u32[]{:S(2)}) collective-permute-start(bf16[4,928,256]{2,1,0:T(8,128)(2,1)} %add_convert_fusion.5), channel_id=1, source_target_pairs={{8,16},{16,8},{9,17},{17,9},{10,18},{18,10},{11,19},{19,11},{12,20... | collective-permute-start | bytes 5701640 | tf_op jit(solution)/shard_map/ppermute | solution.py:29
  146.5 73.5 %collective-permute-start.9 = (bf16[4,928,256]{2,1,0:T(8,128)(2,1)}, bf16[4,928,256]{2,1,0:T(8,128)(2,1)S(1)}, u32[]{:S(2)}, u32[]{:S(2)}) collective-permute-start(bf16[4,928,256]{2,1,0:T(8,128)(2,1)} %convert_select_fusion), channel_id=1, source_target_pairs={{0,8},{8,0},{16,24},{24,16},{1,9},{9,1},{17,25},{25,17},{2,10},{10... | collective-permute-start | bytes 5701640 | tf_op jit(solution)/shard_map/ppermute | solution.py:29
  158.4 25.2 %copy-start.3 = (f32[4,928,256]{2,1,0:T(8,128)S(1)}, f32[4,928,256]{2,1,0:T(8,128)}, u32[]{:S(2)}) copy-start(f32[4,928,256]{2,1,0:T(8,128)} %shard_map.102.refs_1_.refs_12_) | copy-start | bytes 11403268
  162.1 26.9 %copy-start.5 = (f32[4,928,256]{2,1,0:T(8,128)S(1)}, f32[4,928,256]{2,1,0:T(8,128)}, u32[]{:S(2)}) copy-start(f32[4,928,256]{2,1,0:T(8,128)} %shard_map.105.refs_1_.refs_12_) | copy-start | bytes 11403268
  162.1 98.7 %collective-permute-start.4 = (bf16[4,928,256]{2,1,0:T(8,128)(2,1)}, bf16[4,928,256]{2,1,0:T(8,128)(2,1)}, u32[]{:S(2)}, u32[]{:S(2)}) collective-permute-start(bf16[4,928,256]{2,1,0:T(8,128)(2,1)} %convert_select_fusion.2), channel_id=1, source_target_pairs={{0,8},{8,0},{16,24},{24,16},{1,9},{9,1},{17,25},{25,17},{2,10},{10... | collective-permute-start | bytes 5701640 | tf_op jit(solution)/shard_map/ppermute | solution.py:29
  186.9 33.1 %copy-start.7 = (f32[4,928,256]{2,1,0:T(8,128)S(1)}, f32[4,928,256]{2,1,0:T(8,128)}, u32[]{:S(2)}) copy-start(f32[4,928,256]{2,1,0:T(8,128)} %shard_map.107.refs_12_) | copy-start | bytes 11403268
  186.9 79.3 %collective-permute-start.16 = (bf16[4,928,256]{2,1,0:T(8,128)(2,1)}, bf16[4,928,256]{2,1,0:T(8,128)(2,1)}, u32[]{:S(2)}, u32[]{:S(2)}) collective-permute-start(bf16[4,928,256]{2,1,0:T(8,128)(2,1)} %add_convert_fusion.1), channel_id=1, source_target_pairs={{8,16},{16,8},{9,17},{17,9},{10,18},{18,10},{11,19},{19,11},{12,20... | collective-permute-start | bytes 5701640 | tf_op jit(solution)/shard_map/ppermute | solution.py:29
  192.2 109.8 %collective-permute-start.12 = (bf16[4,928,256]{2,1,0:T(8,128)(2,1)}, bf16[4,928,256]{2,1,0:T(8,128)(2,1)}, u32[]{:S(2)}, u32[]{:S(2)}) collective-permute-start(bf16[4,928,256]{2,1,0:T(8,128)(2,1)} %add_convert_fusion.4), channel_id=1, source_target_pairs={{8,0},{16,24},{9,1},{17,25},{10,2},{18,26},{11,3},{19,27},{12,4},{... | collective-permute-start | bytes 5701640 | tf_op jit(solution)/shard_map/ppermute | solution.py:29
  220.0 1.8 copy-start
  221.9 74.2 %collective-permute-start.14 = (bf16[4,928,256]{2,1,0:T(8,128)(2,1)}, bf16[4,928,256]{2,1,0:T(8,128)(2,1)}, u32[]{:S(2)}, u32[]{:S(2)}) collective-permute-start(bf16[4,928,256]{2,1,0:T(8,128)(2,1)} %add_convert_fusion.3), channel_id=1, source_target_pairs={{8,16},{16,8},{9,17},{17,9},{10,18},{18,10},{11,19},{19,11},{12,20... | collective-permute-start | bytes 5701640 | tf_op jit(solution)/shard_map/ppermute | solution.py:29
  260.9 5.4 %copy-start.4 = (f32[4,928,256]{2,1,0:T(8,128)S(1)}, f32[4,928,256]{2,1,0:T(8,128)}, u32[]{:S(2)}) copy-start(f32[4,928,256]{2,1,0:T(8,128)} %shard_map.102.refs_1_.refs_12_) | copy-start | bytes 11403268
  265.5 66.7 %collective-permute-start.10 = (bf16[4,928,256]{2,1,0:T(8,128)(2,1)}, bf16[4,928,256]{2,1,0:T(8,128)(2,1)S(1)}, u32[]{:S(2)}, u32[]{:S(2)}) collective-permute-start(bf16[4,928,256]{2,1,0:T(8,128)(2,1)} %add_convert_fusion.6), channel_id=1, source_target_pairs={{8,16},{16,8},{9,17},{17,9},{10,18},{18,10},{11,19},{19,11},{12,20... | collective-permute-start | bytes 5701640 | tf_op jit(solution)/shard_map/ppermute | solution.py:29
  269.5 72.8 %collective-permute-start.17 = (bf16[4,928,256]{2,1,0:T(8,128)(2,1)}, bf16[4,928,256]{2,1,0:T(8,128)(2,1)}, u32[]{:S(2)}, u32[]{:S(2)}) collective-permute-start(bf16[4,928,256]{2,1,0:T(8,128)(2,1)} %add_convert_fusion), channel_id=1, source_target_pairs={{8,0},{16,24},{9,1},{17,25},{10,2},{18,26},{11,3},{19,27},{12,4},{... | collective-permute-start | bytes 5701640 | tf_op jit(solution)/shard_map/ppermute | solution.py:29
  300.5 82.6 %collective-permute-start.15 = (bf16[4,928,256]{2,1,0:T(8,128)(2,1)}, bf16[4,928,256]{2,1,0:T(8,128)(2,1)}, u32[]{:S(2)}, u32[]{:S(2)}) collective-permute-start(bf16[4,928,256]{2,1,0:T(8,128)(2,1)} %add_convert_fusion.2), channel_id=1, source_target_pairs={{8,0},{16,24},{9,1},{17,25},{10,2},{18,26},{11,3},{19,27},{12,4},{... | collective-permute-start | bytes 5701640 | tf_op jit(solution)/shard_map/ppermute | solution.py:29
  332.1 1.3 copy-start.8
  373.5 40.5 %collective-permute-start.18 = (bf16[2,928,256]{2,1,0:T(8,128)(2,1)}, bf16[2,928,256]{2,1,0:T(8,128)(2,1)S(1)}, u32[]{:S(2)}, u32[]{:S(2)}) collective-permute-start(bf16[2,928,256]{2,1,0:T(8,128)(2,1)} %shard_map.119), channel_id=1, source_target_pairs={{8,0},{16,24},{9,1},{17,25},{10,2},{18,26},{11,3},{19,27},{12,4},{... | collective-permute-start | bytes 2850824 | tf_op jit(solution)/shard_map/ppermute | solution.py:29
  374.8 55.1 %collective-permute-start.13 = (bf16[2,928,256]{2,1,0:T(8,128)(2,1)}, bf16[2,928,256]{2,1,0:T(8,128)(2,1)S(1)}, u32[]{:S(2)}, u32[]{:S(2)}) collective-permute-start(bf16[2,928,256]{2,1,0:T(8,128)(2,1)} %get-tuple-element.44), channel_id=1, source_target_pairs={{8,0},{16,24},{9,1},{17,25},{10,2},{18,26},{11,3},{19,27},{12,4},{... | collective-permute-start | bytes 2850824 | tf_op jit(solution)/shard_map/ppermute | solution.py:29
  414.0 1.0 copy-start.17
  428.6 22.0 %collective-permute-start.20 = (bf16[2,256,2048]{2,1,0:T(8,128)(2,1)}, bf16[2,256,2048]{2,1,0:T(8,128)(2,1)S(1)}, u32[]{:S(2)}, u32[]{:S(2)}) collective-permute-start(bf16[2,256,2048]{2,1,0:T(8,128)(2,1)} %get-tuple-element.37), channel_id=1, source_target_pairs={{0,2},{1,3},{4,6},{5,7},{8,10},{9,11},{12,14},{13,15},{16,18},{17,... | collective-permute-start | bytes 6291464 | tf_op jit(solution)/shard_map/ppermute | solution.py:581
  429.9 0.9 copy-start.16
  444.5 13.6 %collective-permute-start.19 = (bf16[2,256,2048]{2,1,0:T(8,128)(2,1)}, bf16[2,256,2048]{2,1,0:T(8,128)(2,1)}, u32[]{:S(2)}, u32[]{:S(2)}) collective-permute-start(bf16[2,256,2048]{2,1,0:T(8,128)(2,1)} %get-tuple-element.36), channel_id=1, source_target_pairs={{2,0},{3,1},{6,4},{7,5},{10,8},{11,9},{14,12},{15,13},{18,16},{19,... | collective-permute-start | bytes 6291464 | tf_op jit(solution)/shard_map/ppermute | solution.py:581
  450.5 1.4 copy-start.13
  451.9 6.1 %copy-start.14 = (f32[2,256,2048]{2,1,0:T(8,128)S(1)}, f32[2,256,2048]{2,1,0:T(8,128)}, u32[]{:S(2)}) copy-start(f32[2,256,2048]{2,1,0:T(8,128)} %get-tuple-element.34) | copy-start | bytes 12582916
  454.9 16.0 %collective-permute-start.22 = (bf16[2,1,128,2048]{3,2,1,0:T(8,128)(2,1)}, bf16[2,1,128,2048]{3,2,1,0:T(8,128)(2,1)S(1)}, u32[]{:S(2)}, u32[]{:S(2)}) collective-permute-start(bf16[2,1,128,2048]{3,2,1,0:T(8,128)(2,1)} %fusion.4), channel_id=1, source_target_pairs={{2,3},{3,2},{6,7},{7,6},{10,11},{11,10},{14,15},{15,14},{18,19},{1... | collective-permute-start | bytes 3145736 | tf_op jit(solution)/shard_map/ppermute | solution.py:454
  459.6 17.9 %collective-permute-start.21 = (bf16[1,2,128,2048]{3,2,1,0:T(8,128)(2,1)S(1)}, bf16[1,2,128,2048]{3,2,1,0:T(8,128)(2,1)S(1)}, u32[]{:S(2)}, u32[]{:S(2)}) collective-permute-start(bf16[1,2,128,2048]{3,2,1,0:T(8,128)(2,1)S(1)} %fusion.3), channel_id=1, source_target_pairs={{0,4},{1,5},{4,0},{5,1},{8,12},{9,13},{12,8},{13,9},{16,20},{17,21... | collective-permute-start | bytes 3145736 | tf_op jit(solution)/shard_map/ppermute | solution.py:454
  470.9 1.0 copy-start.11
  474.4 14.7 %collective-permute-start.24 = (bf16[1,1,128,2048]{3,2,1,0:T(8,128)(2,1)}, bf16[1,1,128,2048]{3,2,1,0:T(8,128)(2,1)S(1)}, u32[]{:S(2)}, u32[]{:S(2)}) collective-permute-start(bf16[1,1,128,2048]{3,2,1,0:T(8,128)(2,1)} %fusion.6), channel_id=1, source_target_pairs={{2,6},{3,7},{6,2},{7,3},{10,14},{11,15},{14,10},{15,11},{18,22},{1... | collective-permute-start | bytes 1572872 | tf_op jit(solution)/shard_map/ppermute | solution.py:454
  477.5 1.0 copy-start.9
  480.2 8.9 %collective-permute-start.23 = (bf16[1,1,128,2048]{3,2,1,0:T(8,128)(2,1)S(1)}, bf16[1,1,128,2048]{3,2,1,0:T(8,128)(2,1)S(1)}, u32[]{:S(2)}, u32[]{:S(2)}) collective-permute-start(bf16[1,1,128,2048]{3,2,1,0:T(8,128)(2,1)S(1)} %fusion.7), channel_id=1, source_target_pairs={{0,1},{1,0},{4,5},{5,4},{8,9},{9,8},{12,13},{13,12},{16,17},{17,16... | collective-permute-start | bytes 1572872 | tf_op jit(solution)/shard_map/ppermute | solution.py:454
  480.9 8.2 %copy-start.10 = (bf16[1,2,128,2048]{3,2,1,0:T(8,128)(2,1)S(1)}, bf16[1,2,128,2048]{3,2,1,0:T(8,128)(2,1)}, u32[]{:S(2)}) copy-start(bf16[1,2,128,2048]{3,2,1,0:T(8,128)(2,1)} %shard_map.122.refs_4_) | copy-start | bytes 3145732
  480.9 8.2 %copy-start.12 = (bf16[2,1,128,2048]{3,2,1,0:T(8,128)(2,1)S(1)}, bf16[2,1,128,2048]{3,2,1,0:T(8,128)(2,1)}, u32[]{:S(2)}) copy-start(bf16[2,1,128,2048]{3,2,1,0:T(8,128)(2,1)} %shard_map.123.refs_5_) | copy-start | bytes 3145732
Sparse Core Ops, SparseCore 0:
  9.9 39.2 all-gather.2
  65.6 38.0 all-gather.4

commit v5 on v4

--- a/solution.py
+++ b/solution.py
@@ -8,7 +8,7 @@
 from jax.sharding import PartitionSpec as P
 
 GROUPS = 4
-VMEM_LIMIT = 60 * 1024 * 1024
+VMEM_LIMIT = 63 * 1024 * 1024
 
 SWAP = [(0, 1), (1, 0), (2, 3), (3, 2)]
 MIDDLE = [(1, 2), (2, 1)]
@@ -92,84 +92,42 @@
 
 def main_kernel(has_acc, k_ref, *refs):
     gates, uppers = refs[:6], refs[6:12]
-    part, r1, r2, r3, x_hbm, wg_ref, wu_ref = refs[12:19]
-    acc_in = refs[19] if has_acc else None
-    acc_out, gate_out, up_out = refs[-11:-8]
-    gate_grad, up_grad, gate_turned, up_turned, x_ref, acc, sems, out_sems = refs[-8:]
-    block, width = gates[0].shape
+    part, r1, r2, r3, x_ref, wg_ref, wu_ref = refs[12:19]
+    acc, gate_out, up_out, gate_grad, up_grad, gate_turned, up_turned = refs[-7:]
+    width = gates[0].shape[1]
     end = k_ref[1] == 1
-    first = pl.program_id(0) == 0
-    x_copy = pltpu.make_async_copy(x_hbm, x_ref, sems.at[0])
-    acc_copy = pltpu.make_async_copy(acc_in, acc, sems.at[1]) if has_acc else None
-
-    @pl.when(first)
+
+    @pl.when(pl.program_id(0) == 0)
     def _():
-        x_copy.start()
-        if has_acc:
-            acc_copy.start()
-        else:
-            acc[...] = jnp.zeros_like(acc)
-
-    for slot in range(4):
-        gate, upper = slot_value(end, gates, slot), slot_value(end, uppers, slot)
-        j = place(k_ref, slot)
-        at = columns(j, width)
-        hidden_grad = (
-            part[j]
-            + r2[j].astype(jnp.float32)
-            + jnp.where(end, r3[j], r1[j]).astype(jnp.float32)
-        )
-        sigma = sigmoid(gate)
-        up_value = (hidden_grad * (gate * sigma)).astype(jnp.bfloat16)
-        gate_value = (
-            hidden_grad * upper * sigma * (1.0 + gate * (1.0 - sigma))
-        ).astype(jnp.bfloat16)
-        up_grad[:, at] = up_value
-        gate_grad[:, at] = gate_value
-        up_turned[at, :] = up_value.T
-        gate_turned[at, :] = gate_value.T
-
-    features = x_ref.shape[1]
-    step = min(features, 512)
-    tiles = [slice(c, c + step) for c in range(0, features, step)]
-
-    @pl.when(first)
-    def _():
-        x_copy.wait()
-
-    for cols in tiles:
-        gate_out[:, cols] = jnp.dot(
-            gate_grad[...], x_ref[:, cols], preferred_element_type=jnp.float32
-        ).astype(jnp.bfloat16)
-
-    if has_acc:
-
-        @pl.when(first)
-        def _():
-            acc_copy.wait()
-
-    last = pl.program_id(0) == pl.num_programs(0) - 1
-    out_copies = [
-        pltpu.make_async_copy(acc.at[:, cols], acc_out.at[:, cols], out_sems.at[i])
-        for i, cols in enumerate(tiles)
-    ]
-    for i, cols in enumerate(tiles):
-        acc[:, cols] += jnp.dot(
-            gate_turned[...], wg_ref[:, cols], preferred_element_type=jnp.float32
-        ) + jnp.dot(
-            up_turned[...], wu_ref[:, cols], preferred_element_type=jnp.float32
-        )
-        pl.when(last)(out_copies[i].start)
-
-    for cols in tiles:
-        up_out[:, cols] = jnp.dot(
-            up_grad[...], x_ref[:, cols], preferred_element_type=jnp.float32
-        ).astype(jnp.bfloat16)
-
-    @pl.when(last)
-    def _():
-        for copy in out_copies:
-            copy.wait()
+        for slot in range(4):
+            gate, upper = slot_value(end, gates, slot), slot_value(end, uppers, slot)
+            j = place(k_ref, slot)
+            at = columns(j, width)
+            hidden_grad = (
+                part[j]
+                + r2[j].astype(jnp.float32)
+                + jnp.where(end, r3[j], r1[j]).astype(jnp.float32)
+            )
+            sigma = sigmoid(gate)
+            up_value = (hidden_grad * (gate * sigma)).astype(jnp.bfloat16)
+            gate_value = (
+                hidden_grad * upper * sigma * (1.0 + gate * (1.0 - sigma))
+            ).astype(jnp.bfloat16)
+            up_grad[:, at] = up_value
+            gate_grad[:, at] = gate_value
+            up_turned[at, :] = up_value.T
+            gate_turned[at, :] = gate_value.T
+
+    gate_out[...] = jnp.dot(
+        gate_grad[...], x_ref[...], preferred_element_type=jnp.float32
+    ).astype(jnp.bfloat16)
+    up_out[...] = jnp.dot(
+        up_grad[...], x_ref[...], preferred_element_type=jnp.float32
+    ).astype(jnp.bfloat16)
+    more = jnp.dot(
+        gate_turned[...], wg_ref[...], preferred_element_type=jnp.float32
+    ) + jnp.dot(up_turned[...], wu_ref[...], preferred_element_type=jnp.float32)
+    acc[...] = refs[19][...] + more if has_acc else more
 
 
 def token_kernel(rows, *refs):
@@ -211,17 +169,17 @@
 def weight_kernel(parts, *refs):
     x_ref, out_ref, grad = refs[parts], refs[-2], refs[-1]
     count, _, width = refs[0].shape
-    for q in range(parts):
-        for j in range(count):
-            at = (j * parts + q) * width
-            grad[:, at : at + width] = refs[q][j]
-    features = x_ref.shape[1]
-    step = min(features, 512)
-    for c in range(0, features, step):
-        cols = slice(c, c + step)
-        out_ref[:, cols] = jnp.dot(
-            grad[...], x_ref[:, cols], preferred_element_type=jnp.float32
-        ).astype(jnp.bfloat16)
+
+    @pl.when(pl.program_id(0) == 0)
+    def _():
+        for q in range(parts):
+            for j in range(count):
+                at = (j * parts + q) * width
+                grad[:, at : at + width] = refs[q][j]
+
+    out_ref[...] = jnp.dot(
+        grad[...], x_ref[...], preferred_element_type=jnp.float32
+    ).astype(jnp.bfloat16)
 
 
 def once(shape):
@@ -296,47 +254,43 @@
     )(k, *args)
 
 
-def main_group(k, slots, sums, r3, x_whole, wg, wu, acc, outs, a, run, size, total):
+def main_group(k, slots, sums, x_whole, wg, wu, acc, outs, a, size, total):
     tokens, features = x_whole.shape
     count, _, width = slots[0].shape
-    block = block_rows(size)
-    base = a * (size // block) + run[0]
-    blocks = run[1] - run[0]
-    wide = pl.BlockSpec((count, block, width), lambda i, k: (0, run[0] + i, 0))
-    weight = pl.BlockSpec((block, features), lambda i, k: (base + i, 0))
-    specs = (
-        slot_specs(a, block, width, run[0])
-        + [wide] * 3
-        + [pl.BlockSpec((count, block, width), lambda i, k: (0, i, 0))]
-        + [pl.BlockSpec(memory_space=pl.ANY), weight, weight]
-    )
-    args = list(slots) * 2 + list(sums) + [r3, x_whole, wg, wu]
+    step = min(features, 512)
+    kept = pl.Buffered(1)
+    gate = pl.BlockSpec(
+        (None, size, width), lambda i, k: (a % 2, 0, 0), pipeline_mode=kept
+    )
+    upper = pl.BlockSpec(
+        (None, size, width), lambda i, k: (2 + a % 2, 0, 0), pipeline_mode=kept
+    )
+    wide = pl.BlockSpec(
+        (count, size, width), lambda i, k: (0, 0, 0), pipeline_mode=kept
+    )
+    weight = pl.BlockSpec((size, step), lambda i, k: (a, i))
+    tile = pl.BlockSpec((tokens, step), lambda i, k: (0, i))
+    specs = [gate] * 6 + [upper] * 6 + [wide] * 4 + [tile, weight, weight]
+    args = list(slots) * 2 + list(sums) + [x_whole, wg, wu]
     aliases = {}
     if acc is not None:
         aliases[1 + len(args)] = 0
         args.append(acc)
-        specs.append(pl.BlockSpec(memory_space=pl.ANY))
+        specs.append(tile)
         for i, out in enumerate(outs):
             aliases[1 + len(args)] = 1 + i
             args.append(out)
             specs.append(pl.BlockSpec(memory_space=pl.ANY))
     wgrad = jax.ShapeDtypeStruct((total, features), jnp.bfloat16)
-    size = blocks * block
     return pl.pallas_call(
         functools.partial(main_kernel, acc is not None),
         grid_spec=pltpu.PrefetchScalarGridSpec(
             num_scalar_prefetch=1,
-            grid=(blocks,),
+            grid=(-(-features // step),),
             in_specs=specs,
-            out_specs=(pl.BlockSpec(memory_space=pl.ANY), weight, weight),
-            scratch_shapes=[pltpu.VMEM((block, tokens), jnp.bfloat16)] * 2
-            + [pltpu.VMEM((tokens, block), jnp.bfloat16)] * 2
-            + [
-                pltpu.VMEM((tokens, features), jnp.bfloat16),
-                pltpu.VMEM((tokens, features), jnp.float32),
-                pltpu.SemaphoreType.DMA((2,)),
-                pltpu.SemaphoreType.DMA((-(-features // min(features, 512)),)),
-            ],
+            out_specs=(tile, weight, weight),
+            scratch_shapes=[pltpu.VMEM((size, tokens), jnp.bfloat16)] * 2
+            + [pltpu.VMEM((tokens, size), jnp.bfloat16)] * 2,
         ),
         out_shape=(
             jax.ShapeDtypeStruct((tokens, features), jnp.float32),
@@ -414,17 +368,21 @@
 def weight_group(grads, x_whole, out, a, size, after):
     tokens, features = x_whole.shape
     count, _, width = grads[0].shape
-    block = block_rows(size)
-    blocks = size // block
-    wide = pl.BlockSpec((count, block, width), lambda i: (0, i, 0))
+    step = min(features, 512)
+    wide = pl.BlockSpec(
+        (count, size, width), lambda i: (0, 0, 0), pipeline_mode=pl.Buffered(1)
+    )
     return pl.pallas_call(
         functools.partial(weight_kernel, len(grads)),
-        grid=(blocks,),
+        grid=(-(-features // step),),
         in_specs=[wide] * len(grads)
-        + [once((tokens, features)), pl.BlockSpec(memory_space=pl.ANY)]
+        + [
+            pl.BlockSpec((tokens, step), lambda i: (0, i)),
+            pl.BlockSpec(memory_space=pl.ANY),
+        ]
         + [pl.BlockSpec(memory_space=pl.ANY)] * len(after),
-        out_specs=pl.BlockSpec((block, features), lambda i: (a * blocks + i, 0)),
-        scratch_shapes=[pltpu.VMEM((block, tokens), jnp.bfloat16)],
+        out_specs=pl.BlockSpec((size, step), lambda i: (a, i)),
+        scratch_shapes=[pltpu.VMEM((size, tokens), jnp.bfloat16)],
         out_shape=jax.ShapeDtypeStruct(out.shape, out.dtype),
         input_output_aliases={len(grads) + 1: 0},
         compiler_params=pltpu.CompilerParams(vmem_limit_bytes=VMEM_LIMIT),
@@ -545,12 +503,10 @@
                     k, slots_of(a), grad_whole, down, a, size, total, a == last
                 )
 
-    blocks = size // block_rows(size)
-
     def main(a, acc, wgrads):
-        sums = [part[a], swap[2 + a], middle[4 + a]]
-        args = (k, slots_of(a), sums, swap[6 + a], x_whole, wg, wu, acc, wgrads)
-        acc, *wgrads = main_group(*args, a, (0, blocks), size, total)
+        sums = [part[a], swap[2 + a], middle[4 + a], swap[6 + a]]
+        args = (k, slots_of(a), sums, x_whole, wg, wu, acc, wgrads)
+        acc, *wgrads = main_group(*args, a, size, total)
         return acc, wgrads
 
     def pieces(value):

time: 509 us -> 505 us (level)
  local copies, waits for them, and re-layouts: 11.7 us -> 3.76 us
    unnamed x36 -> x18, local copies, waits for them, and re-layouts: 7.72 us -> 1.01 us
  transfers between devices with their start and end apart: 27 -> 27, of which waited for: 8 -> 8; matrix products, arithmetic and copies ran while one was open for 12% -> 12% of each run, Pallas kernels for 44% -> 43%
where the time goes in v5:
time: 505 us; the launch traced here: 496 us
  Pallas kernels  213 us (42%)
  waiting for transfers between devices  133 us (26%)
  starting transfers between devices  71.2 us (14%)
  other arithmetic  60 us (12%)
  between operations  14.6 us (3%)
    ppermute x19, waiting for transfers between devices, send(): return lax.ppermute(value, 'inp', pairs)  102 us
    pallas_call x3, Pallas kernels, main_group(): pl.pallas_call(functools.partial(main_kernel, acc is not None), grid_spec...  88.4 us
    ppermute x19, starting transfers between devices, send(): return lax.ppermute(value, 'inp', pairs)  54.3 us
    pallas_call x4, Pallas kernels, down_group(): pl.pallas_call(functools.partial(down_kernel, factors), grid_spec=pltpu.P...  48 us
    pallas_call x4, Pallas kernels, sum_group(): pl.pallas_call(sum_kernel, grid=(blocks,), in_specs=[pl.BlockSpec((block,...  33.6 us
    convert_element_type x8, other arithmetic, rounded(): return (part + got.astype(jnp.float32)).astype(jnp.bfloat16)  30.7 us
    all_gather x1, waiting for transfers between devices, per_device(): lax.all_gather(out_grad, ('wt', 'dep'), axis=0, tiled=True)  28.2 us
    pallas_call x2, Pallas kernels, token_group(): pl.pallas_call(functools.partial(token_kernel, rows), grid_spec=pltpu.Pre...  27.1 us
  transfers between devices with their start and end apart: 27, of which 8 were waited for; matrix products, arithmetic and copies ran while one was open for 12% of the time, Pallas kernels for 43%

profile of v5, /device:TPU:1, one launch (start us, length us, event | category | flops | bytes accessed | tf_op | source)
XLA Modules:
  0.0 495.7 jit_solution(5256273176783011046)
XLA Ops:
  12.6 3.5 collective-permute-start.5
  21.0 28.2 %all-gather.3.cloned.1.call-done.grad_ref.refs_12_ = bf16[1024,2048]{1,0:T(8,128)(2,1)} async-done(((bf16[128,2048]{1,0:T(8,128)(2,1)}), bf16[1024,2048]{1,0:T(8,128)(2,1)}) %all-gather.3.cloned.1.call-update) | async-done | bytes 4194320 | tf_op jit(solution)/shard_map/all_gather | solution.py:474
  49.2 8.4 %shard_map.105.refs_1_.refs_12_ = f32[4,928,256]{2,1,0:T(8,128)} custom-call(bf16[3696,2048]{1,0:T(8,128)(2,1)} %w_ref.7, bf16[1024,2048]{1,0:T(8,128)(2,1)} %all-gather.3.cloned.1.call-done.grad_ref.refs_12_), custom_call_target="tpu_custom_call" | custom-call | flops 3892314112 | bytes 7602176 | tf_op jit(solution)/shard_map/pallas_call | solution.py:194
  57.6 3.6 convert_select_fusion.1
  62.9 1.9 collective-permute-start.8
  64.9 8.4 %shard_map.102.refs_1_.refs_12_ = f32[4,928,256]{2,1,0:T(8,128)} custom-call(bf16[3696,2048]{1,0:T(8,128)(2,1)} %w_ref.7, bf16[1024,2048]{1,0:T(8,128)(2,1)} %all-gather.3.cloned.1.call-done.grad_ref.refs_12_), custom_call_target="tpu_custom_call" | custom-call | flops 3892314112 | bytes 7602176 | tf_op jit(solution)/shard_map/pallas_call | solution.py:194
  73.2 24.7 %collective-permute-done.refs_0_ = bf16[4,928,256]{2,1,0:T(8,128)(2,1)} collective-permute-done((bf16[4,928,256]{2,1,0:T(8,128)(2,1)}, bf16[4,928,256]{2,1,0:T(8,128)(2,1)}, u32[]{:S(2)}, u32[]{:S(2)}) %collective-permute-start) | collective-permute-done | bytes 1900576 | tf_op jit(solution)/shard_map/ppermute | solution.py:29
  99.9 3.6 convert_select_fusion.3
  103.5 1.9 collective-permute-start.2
  105.4 8.4 %shard_map.107.refs_12_ = f32[4,928,256]{2,1,0:T(8,128)} custom-call(bf16[3696,2048]{1,0:T(8,128)(2,1)} %w_ref.7, bf16[1024,2048]{1,0:T(8,128)(2,1)} %all-gather.3.cloned.1.call-done.grad_ref.refs_12_), custom_call_target="tpu_custom_call" | custom-call | flops 3892314112 | bytes 7602176 | tf_op jit(solution)/shard_map/pallas_call | solution.py:194
  113.8 24.9 %collective-permute-done.7.refs_2_.refs_8_.refs_13_ = bf16[4,928,256]{2,1,0:T(8,128)(2,1)} collective-permute-done((bf16[4,928,256]{2,1,0:T(8,128)(2,1)}, bf16[4,928,256]{2,1,0:T(8,128)(2,1)}, u32[]{:S(2)}, u32[]{:S(2)}) %collective-permute-start.7) | collective-permute-done | bytes 1900576 | tf_op jit(solution)/shard_map/ppermute | solution.py:29
  138.7 4.4 add_convert_fusion.5
  146.5 2.9 collective-permute-start.9
  150.0 8.4 %shard_map.104 = f32[4,928,256]{2,1,0:T(8,128)} custom-call(bf16[3696,2048]{1,0:T(8,128)(2,1)} %w_ref.7, bf16[1024,2048]{1,0:T(8,128)(2,1)} %all-gather.3.cloned.1.call-done.grad_ref.refs_12_), custom_call_target="tpu_custom_call" | custom-call | flops 3892314112 | bytes 7602176 | tf_op jit(solution)/shard_map/pallas_call | solution.py:194
  158.4 3.7 convert_select_fusion.2
  162.1 21.5 %collective-permute-start.4 = (bf16[4,928,256]{2,1,0:T(8,128)(2,1)}, bf16[4,928,256]{2,1,0:T(8,128)(2,1)}, u32[]{:S(2)}, u32[]{:S(2)}) collective-permute-start(bf16[4,928,256]{2,1,0:T(8,128)(2,1)} %convert_select_fusion.2), channel_id=1, source_target_pairs={{0,8},{8,0},{16,24},{24,16},{1,9},{9,1},{17,25},{25,17},{2,10},{10... | collective-permute-start | bytes 5701640 | tf_op jit(solution)/shard_map/ppermute | solution.py:29
  183.7 3.3 add_convert_fusion.1
  186.9 2.1 collective-permute-start.16
  189.0 3.2 add_convert_fusion.4
  193.7 26.4 %collective-permute-done.9.refs_4_.refs_10_.refs_13_ = bf16[4,928,256]{2,1,0:T(8,128)(2,1)} collective-permute-done((bf16[4,928,256]{2,1,0:T(8,128)(2,1)}, bf16[4,928,256]{2,1,0:T(8,128)(2,1)}, u32[]{:S(2)}, u32[]{:S(2)}) %collective-permute-start.9) | collective-permute-done | bytes 1900576 | tf_op jit(solution)/shard_map/ppermute | solution.py:29
  220.2 3.2 add_convert_fusion.3
  223.4 1.9 collective-permute-start.14
  225.3 11.6 %shard_map.108.refs_13_ = bf16[3696,2048]{1,0:T(8,128)(2,1)} custom-call(s32[2]{0:T(128)} %pad_add_fusion.k_ref.refs_0_, bf16[4,928,256]{2,1,0:T(8,128)(2,1)} %pad_maximum_fusion.1.refs_0_.refs_6_, bf16[4,928,256]{2,1,0:T(8,128)(2,1)} %shard_map.106.refs_1_.refs_7_, bf16[4,928,256]{2,1,0:T(8,128)(2,1)} %collective-permute-done.7.refs_2_.refs_8_.refs_13_, ...), custom_call_target="tpu_custom_call" | custom-call | flops 3892314112 | bytes 7602176 | tf_op jit(solution)/shard_map/pallas_call | solution.py:233
  236.9 11.2 %shard_map.109.refs_1_.refs_13_ = bf16[3696,2048]{1,0:T(8,128)(2,1)} custom-call(s32[2]{0:T(128)} %pad_add_fusion.k_ref.refs_0_, bf16[4,928,256]{2,1,0:T(8,128)(2,1)} %pad_maximum_fusion.1.refs_0_.refs_6_, bf16[4,928,256]{2,1,0:T(8,128)(2,1)} %shard_map.106.refs_1_.refs_7_, ...), custom_call_target="tpu_custom_call", output_to_operand_aliasing={{}: (14, {})} | custom-call | flops 3892314112 | bytes 7602176 | tf_op jit(solution)/shard_map/pallas_call | solution.py:233
  248.1 12.8 %collective-permute-done.4.refs_0_ = bf16[4,928,256]{2,1,0:T(8,128)(2,1)} collective-permute-done((bf16[4,928,256]{2,1,0:T(8,128)(2,1)}, bf16[4,928,256]{2,1,0:T(8,128)(2,1)}, u32[]{:S(2)}, u32[]{:S(2)}) %collective-permute-start.4) | collective-permute-done | bytes 1900576 | tf_op jit(solution)/shard_map/ppermute | solution.py:29
  260.9 4.5 add_convert_fusion.6
  265.4 1.9 collective-permute-start.10
  267.4 3.3 add_convert_fusion
  271.9 11.6 %shard_map.111.refs_13_ = bf16[3696,2048]{1,0:T(8,128)(2,1)} custom-call(s32[2]{0:T(128)} %pad_add_fusion.k_ref.refs_0_, bf16[4,928,256]{2,1,0:T(8,128)(2,1)} %pad_maximum_fusion.refs_0_.refs_6_, bf16[4,928,256]{2,1,0:T(8,128)(2,1)} %shard_map.103.refs_1_.refs_7_, ...), custom_call_target="tpu_custom_call", output_to_operand_aliasing={{}: (14, {})} | custom-call | flops 3892314112 | bytes 7602176 | tf_op jit(solution)/shard_map/pallas_call | solution.py:233
  283.6 13.6 %shard_map.112 = (bf16[3696,2048]{1,0:T(8,128)(2,1)}, f32[4,928,256]{2,1,0:T(8,128)}, f32[4,928,256]{2,1,0:T(8,128)}) custom-call(s32[2]{0:T(128)} %pad_add_fusion.k_ref.refs_0_, bf16[4,928,256]{2,1,0:T(8,128)(2,1)} %pad_maximum_fusion.refs_0_.refs_6_, bf16[4,928,256]{2,1,0:T(8,128)(2,1)} %shard_map.103.refs_1_.refs_7_, ...), custom_call_target="tpu_custom_call", output_to_operand_aliasing={{0}: (14, {})} | custom-call | flops 3892314112 | bytes 7602176 | tf_op jit(solution)/shard_map/pallas_call | solution.py:233
  297.2 4.4 add_convert_fusion.2
  303.4 29.4 %shard_map.113 = (f32[1024,2048]{1,0:T(8,128)}, bf16[3696,2048]{1,0:T(8,128)(2,1)}, bf16[3696,2048]{1,0:T(8,128)(2,1)}) custom-call(s32[2]{0:T(128)} %pad_add_fusion.k_ref.refs_0_, bf16[4,928,256]{2,1,0:T(8,128)(2,1)} %pad_maximum_fusion.1.refs_0_.refs_6_, bf16[4,928,256]{2,1,0:T(8,128)(2,1)} %shard_map.106.refs_1_.refs_7_, ...), custom_call_target="tpu_custom_call" | custom-call | flops 15569256448 | bytes 28508160 | tf_op jit(solution)/shard_map/pallas_call | solution.py:285
  332.8 4.4 fusion.8
  337.2 5.1 %collective-permute-done.17.refs_15_ = bf16[4,928,256]{2,1,0:T(8,128)(2,1)} collective-permute-done((bf16[4,928,256]{2,1,0:T(8,128)(2,1)}, bf16[4,928,256]{2,1,0:T(8,128)(2,1)}, u32[]{:S(2)}, u32[]{:S(2)}) %collective-permute-start.17) | collective-permute-done | bytes 1900576 | tf_op jit(solution)/shard_map/ppermute | solution.py:29
  342.3 29.5 %shard_map.116 = (f32[1024,2048]{1,0:T(8,128)}, bf16[3696,2048]{1,0:T(8,128)(2,1)}, bf16[3696,2048]{1,0:T(8,128)(2,1)}) custom-call(s32[2]{0:T(128)} %pad_add_fusion.k_ref.refs_0_, bf16[4,928,256]{2,1,0:T(8,128)(2,1)} %pad_maximum_fusion.1.refs_0_.refs_6_, ...), custom_call_target="tpu_custom_call", output_to_operand_aliasing={{0}: (20, {}), {1}: (21, {}), {2}: (22, {})} | custom-call | flops 15569256448 | bytes 28508160 | tf_op jit(solution)/shard_map/pallas_call | solution.py:285
  374.6 8.4 %collective-permute-done.15.refs_15_ = bf16[4,928,256]{2,1,0:T(8,128)(2,1)} collective-permute-done((bf16[4,928,256]{2,1,0:T(8,128)(2,1)}, bf16[4,928,256]{2,1,0:T(8,128)(2,1)}, u32[]{:S(2)}, u32[]{:S(2)}) %collective-permute-start.15) | collective-permute-done | bytes 1900576 | tf_op jit(solution)/shard_map/ppermute | solution.py:29
  383.1 29.4 %shard_map.117 = (f32[1024,2048]{1,0:T(8,128)}, bf16[3696,2048]{1,0:T(8,128)(2,1)}, bf16[3696,2048]{1,0:T(8,128)(2,1)}) custom-call(s32[2]{0:T(128)} %pad_add_fusion.k_ref.refs_0_, bf16[4,928,256]{2,1,0:T(8,128)(2,1)} %pad_maximum_fusion.refs_0_.refs_6_, ...), custom_call_target="tpu_custom_call", output_to_operand_aliasing={{0}: (20, {}), {1}: (21, {}), {2}: (22, {})} | custom-call | flops 15569256448 | bytes 28508160 | tf_op jit(solution)/shard_map/pallas_call | solution.py:285
  412.5 13.6 %shard_map.120 = (bf16[2,928,256]{2,1,0:T(8,128)(2,1)}, bf16[2,928,256]{2,1,0:T(8,128)(2,1)}, f32[2,256,2048]{2,1,0:T(8,128)}, bf16[2,256,2048]{2,1,0:T(8,128)(2,1)}) custom-call(s32[2]{0:T(128)} %pad_add_fusion.k_ref.refs_0_, f32[2,2,928,256]{3,2,1,0:T(8,128)} %bitcast.77, f32[2,2,928,256]{3,2,1,0:T(8,128)} %bitcast.79, f32[2,2,928,256]{3,2,1,0:T(8,128)} %bitcast.74, ...), custom_call_target="tpu_custom_call" | custom-call | flops 3892314112 | bytes 18055168 | tf_op jit(solution)/shard_map/pallas_call | solution.py:330
  428.3 13.5 %shard_map.118 = (bf16[2,928,256]{2,1,0:T(8,128)(2,1)}, bf16[2,928,256]{2,1,0:T(8,128)(2,1)}, f32[2,256,2048]{2,1,0:T(8,128)}, bf16[2,256,2048]{2,1,0:T(8,128)(2,1)}) custom-call(s32[2]{0:T(128)} %pad_add_fusion.k_ref.refs_0_, f32[2,2,928,256]{3,2,1,0:T(8,128)} %bitcast.78, f32[2,2,928,256]{3,2,1,0:T(8,128)} %bitcast.80, f32[2,2,928,256]{3,2,1,0:T(8,128)} %bitcast.75, ...), custom_call_target="tpu_custom_call" | custom-call | flops 3892314112 | bytes 18055168 | tf_op jit(solution)/shard_map/pallas_call | solution.py:330
  441.8 6.1 %collective-permute-start.19 = (bf16[2,256,2048]{2,1,0:T(8,128)(2,1)}, bf16[2,256,2048]{2,1,0:T(8,128)(2,1)S(1)}, u32[]{:S(2)}, u32[]{:S(2)}) collective-permute-start(bf16[2,256,2048]{2,1,0:T(8,128)(2,1)} %get-tuple-element.36), channel_id=1, source_target_pairs={{2,0},{3,1},{6,4},{7,5},{10,8},{11,9},{14,12},{15,13},{18,16},{19,... | collective-permute-start | bytes 6291464 | tf_op jit(solution)/shard_map/ppermute | solution.py:537
  448.0 3.3 fusion.4
  451.3 3.1 collective-permute-start.22
  457.7 8.1 %shard_map.121.refs_1_ = bf16[3696,2048]{1,0:T(8,128)(2,1)} custom-call(bf16[2,928,256]{2,1,0:T(8,128)(2,1)} %get-tuple-element.38.refs_0_, bf16[2,928,256]{2,1,0:T(8,128)(2,1)} %get-tuple-element.39.refs_1_, bf16[1024,2048]{1,0:T(8,128)(2,1)} %all-gather.5.cloned.1.call-done.refs_16_.refs_2_, ...), custom_call_target="tpu_custom_call", output_to_operand_aliasing={{}: (3, {})} | custom-call | flops 3892314112 | bytes 5701632 | tf_op jit(solution)/shard_map/pallas_call | solution.py:375
  467.4 2.5 fusion.6
  469.9 3.1 collective-permute-start.24
  473.0 2.5 fusion.7
  477.0 8.1 %shard_map.124 = bf16[3696,2048]{1,0:T(8,128)(2,1)} custom-call(bf16[2,928,256]{2,1,0:T(8,128)(2,1)} %get-tuple-element.41.refs_0_, bf16[2,928,256]{2,1,0:T(8,128)(2,1)} %get-tuple-element.42.refs_1_, bf16[1024,2048]{1,0:T(8,128)(2,1)} %all-gather.5.cloned.1.call-done.refs_16_.refs_2_, ...), custom_call_target="tpu_custom_call", output_to_operand_aliasing={{}: (3, {})} | custom-call | flops 3892314112 | bytes 5701632 | tf_op jit(solution)/shard_map/pallas_call | solution.py:375
  485.2 3.6 fusion.5
  (75 shorter events, 33.8 us)
Async XLA Ops:
  7.2 2.0 copy-start.7
  7.2 42.0 %all-gather.3.cloned.1.call-start = ((), (), s32[]{:S(2)}) async-start(), calls=%async_computation | async-start | bytes 4718592 | tf_op jit(solution)/shard_map/all_gather | solution.py:474
  7.9 295.4 %all-gather.5.cloned.1.call-start = ((), (), s32[]{:S(2)}) async-start(), calls=%async_computation.1 | async-start | bytes 4718592 | tf_op jit(solution)/shard_map/all_gather | solution.py:473
  10.7 46.8 %collective-permute-start.6 = (bf16[4,928,256]{2,1,0:T(8,128)(2,1)}, bf16[4,928,256]{2,1,0:T(8,128)(2,1)}, u32[]{:S(2)}, u32[]{:S(2)}) collective-permute-start(bf16[4,928,256]{2,1,0:T(8,128)(2,1)} %pad_maximum_fusion.1.refs_0_.refs_6_), channel_id=1, source_target_pairs={{8,16},{16,8},{9,17},{17,9},{10,18},{18,10},{11,19},{19,11},{12,20... | collective-permute-start | bytes 5701640 | tf_op jit(solution)/shard_map/ppermute | solution.py:29
  12.6 50.3 %collective-permute-start.5 = (bf16[4,928,256]{2,1,0:T(8,128)(2,1)}, bf16[4,928,256]{2,1,0:T(8,128)(2,1)}, u32[]{:S(2)}, u32[]{:S(2)}) collective-permute-start(bf16[4,928,256]{2,1,0:T(8,128)(2,1)} %pad_maximum_fusion.1.refs_0_.refs_6_), channel_id=1, source_target_pairs={{0,8},{8,0},{16,24},{24,16},{1,9},{9,1},{17,25},{25,17},{2,10},{10... | collective-permute-start | bytes 5701640 | tf_op jit(solution)/shard_map/ppermute | solution.py:29
  19.0 78.9 %collective-permute-start = (bf16[4,928,256]{2,1,0:T(8,128)(2,1)}, bf16[4,928,256]{2,1,0:T(8,128)(2,1)}, u32[]{:S(2)}, u32[]{:S(2)}) collective-permute-start(bf16[4,928,256]{2,1,0:T(8,128)(2,1)} %pad_maximum_fusion.refs_0_.refs_6_), channel_id=1, source_target_pairs={{0,8},{8,0},{16,24},{24,16},{1,9},{9,1},{17,25},{25,17},{2,10},{10... | collective-permute-start | bytes 5701640 | tf_op jit(solution)/shard_map/ppermute | solution.py:29
  19.1 80.8 %collective-permute-start.1 = (bf16[4,928,256]{2,1,0:T(8,128)(2,1)}, bf16[4,928,256]{2,1,0:T(8,128)(2,1)}, u32[]{:S(2)}, u32[]{:S(2)}) collective-permute-start(bf16[4,928,256]{2,1,0:T(8,128)(2,1)} %pad_maximum_fusion.refs_0_.refs_6_), channel_id=1, source_target_pairs={{8,16},{16,8},{9,17},{17,9},{10,18},{18,10},{11,19},{19,11},{12,20... | collective-permute-start | bytes 5701640 | tf_op jit(solution)/shard_map/ppermute | solution.py:29
  61.1 77.6 %collective-permute-start.7 = (bf16[4,928,256]{2,1,0:T(8,128)(2,1)}, bf16[4,928,256]{2,1,0:T(8,128)(2,1)}, u32[]{:S(2)}, u32[]{:S(2)}) collective-permute-start(bf16[4,928,256]{2,1,0:T(8,128)(2,1)} %convert_select_fusion.1), channel_id=1, source_target_pairs={{0,8},{8,0},{16,24},{24,16},{1,9},{9,1},{17,25},{25,17},{2,10},{10... | collective-permute-start | bytes 5701640 | tf_op jit(solution)/shard_map/ppermute | solution.py:29
  62.9 82.1 %collective-permute-start.8 = (bf16[4,928,256]{2,1,0:T(8,128)(2,1)}, bf16[4,928,256]{2,1,0:T(8,128)(2,1)}, u32[]{:S(2)}, u32[]{:S(2)}) collective-permute-start(bf16[4,928,256]{2,1,0:T(8,128)(2,1)} %shard_map.106.refs_1_.refs_7_), channel_id=1, source_target_pairs={{8,16},{16,8},{9,17},{17,9},{10,18},{18,10},{11,19},{19,11},{12,20... | collective-permute-start | bytes 5701640 | tf_op jit(solution)/shard_map/ppermute | solution.py:29
  98.0 60.4 %collective-permute-start.3 = (bf16[4,928,256]{2,1,0:T(8,128)(2,1)}, bf16[4,928,256]{2,1,0:T(8,128)(2,1)}, u32[]{:S(2)}, u32[]{:S(2)}) collective-permute-start(bf16[4,928,256]{2,1,0:T(8,128)(2,1)} %shard_map.103.refs_1_.refs_7_), channel_id=1, source_target_pairs={{8,16},{16,8},{9,17},{17,9},{10,18},{18,10},{11,19},{19,11},{12,20... | collective-permute-start | bytes 5701640 | tf_op jit(solution)/shard_map/ppermute | solution.py:29
  103.5 80.2 %collective-permute-start.2 = (bf16[4,928,256]{2,1,0:T(8,128)(2,1)}, bf16[4,928,256]{2,1,0:T(8,128)(2,1)}, u32[]{:S(2)}, u32[]{:S(2)}) collective-permute-start(bf16[4,928,256]{2,1,0:T(8,128)(2,1)} %convert_select_fusion.3), channel_id=1, source_target_pairs={{0,8},{8,0},{16,24},{24,16},{1,9},{9,1},{17,25},{25,17},{2,10},{10... | collective-permute-start | bytes 5701640 | tf_op jit(solution)/shard_map/ppermute | solution.py:29
  113.8 31.2 %copy-start.3 = (f32[4,928,256]{2,1,0:T(8,128)S(1)}, f32[4,928,256]{2,1,0:T(8,128)}, u32[]{:S(2)}) copy-start(f32[4,928,256]{2,1,0:T(8,128)} %shard_map.107.refs_12_) | copy-start | bytes 11403268
  143.1 45.9 %collective-permute-start.11 = (bf16[4,928,256]{2,1,0:T(8,128)(2,1)}, bf16[4,928,256]{2,1,0:T(8,128)(2,1)}, u32[]{:S(2)}, u32[]{:S(2)}) collective-permute-start(bf16[4,928,256]{2,1,0:T(8,128)(2,1)} %add_convert_fusion.5), channel_id=1, source_target_pairs={{8,16},{16,8},{9,17},{17,9},{10,18},{18,10},{11,19},{19,11},{12,20... | collective-permute-start | bytes 5701640 | tf_op jit(solution)/shard_map/ppermute | solution.py:29
  146.5 73.6 %collective-permute-start.9 = (bf16[4,928,256]{2,1,0:T(8,128)(2,1)}, bf16[4,928,256]{2,1,0:T(8,128)(2,1)}, u32[]{:S(2)}, u32[]{:S(2)}) collective-permute-start(bf16[4,928,256]{2,1,0:T(8,128)(2,1)} %convert_select_fusion), channel_id=1, source_target_pairs={{0,8},{8,0},{16,24},{24,16},{1,9},{9,1},{17,25},{25,17},{2,10},{10... | collective-permute-start | bytes 5701640 | tf_op jit(solution)/shard_map/ppermute | solution.py:29
  158.4 25.3 %copy-start = (f32[4,928,256]{2,1,0:T(8,128)S(1)}, f32[4,928,256]{2,1,0:T(8,128)}, u32[]{:S(2)}) copy-start(f32[4,928,256]{2,1,0:T(8,128)} %shard_map.102.refs_1_.refs_12_) | copy-start | bytes 11403268
  162.1 26.9 %copy-start.2 = (f32[4,928,256]{2,1,0:T(8,128)S(1)}, f32[4,928,256]{2,1,0:T(8,128)}, u32[]{:S(2)}) copy-start(f32[4,928,256]{2,1,0:T(8,128)} %shard_map.105.refs_1_.refs_12_) | copy-start | bytes 11403268
  162.1 98.8 %collective-permute-start.4 = (bf16[4,928,256]{2,1,0:T(8,128)(2,1)}, bf16[4,928,256]{2,1,0:T(8,128)(2,1)}, u32[]{:S(2)}, u32[]{:S(2)}) collective-permute-start(bf16[4,928,256]{2,1,0:T(8,128)(2,1)} %convert_select_fusion.2), channel_id=1, source_target_pairs={{0,8},{8,0},{16,24},{24,16},{1,9},{9,1},{17,25},{25,17},{2,10},{10... | collective-permute-start | bytes 5701640 | tf_op jit(solution)/shard_map/ppermute | solution.py:29
  186.9 33.2 %copy-start.4 = (f32[4,928,256]{2,1,0:T(8,128)S(1)}, f32[4,928,256]{2,1,0:T(8,128)}, u32[]{:S(2)}) copy-start(f32[4,928,256]{2,1,0:T(8,128)} %shard_map.107.refs_12_) | copy-start | bytes 11403268
  186.9 80.4 %collective-permute-start.16 = (bf16[4,928,256]{2,1,0:T(8,128)(2,1)}, bf16[4,928,256]{2,1,0:T(8,128)(2,1)}, u32[]{:S(2)}, u32[]{:S(2)}) collective-permute-start(bf16[4,928,256]{2,1,0:T(8,128)(2,1)} %add_convert_fusion.1), channel_id=1, source_target_pairs={{8,16},{16,8},{9,17},{17,9},{10,18},{18,10},{11,19},{19,11},{12,20... | collective-permute-start | bytes 5701640 | tf_op jit(solution)/shard_map/ppermute | solution.py:29
  192.2 111.1 %collective-permute-start.12 = (bf16[4,928,256]{2,1,0:T(8,128)(2,1)}, bf16[4,928,256]{2,1,0:T(8,128)(2,1)}, u32[]{:S(2)}, u32[]{:S(2)}) collective-permute-start(bf16[4,928,256]{2,1,0:T(8,128)(2,1)} %add_convert_fusion.4), channel_id=1, source_target_pairs={{8,0},{16,24},{9,1},{17,25},{10,2},{18,26},{11,3},{19,27},{12,4},{... | collective-permute-start | bytes 5701640 | tf_op jit(solution)/shard_map/ppermute | solution.py:29
  223.4 73.8 %collective-permute-start.14 = (bf16[4,928,256]{2,1,0:T(8,128)(2,1)}, bf16[4,928,256]{2,1,0:T(8,128)(2,1)}, u32[]{:S(2)}, u32[]{:S(2)}) collective-permute-start(bf16[4,928,256]{2,1,0:T(8,128)(2,1)} %add_convert_fusion.3), channel_id=1, source_target_pairs={{8,16},{16,8},{9,17},{17,9},{10,18},{18,10},{11,19},{19,11},{12,20... | collective-permute-start | bytes 5701640 | tf_op jit(solution)/shard_map/ppermute | solution.py:29
  260.9 6.5 %copy-start.1 = (f32[4,928,256]{2,1,0:T(8,128)S(1)}, f32[4,928,256]{2,1,0:T(8,128)}, u32[]{:S(2)}) copy-start(f32[4,928,256]{2,1,0:T(8,128)} %shard_map.102.refs_1_.refs_12_) | copy-start | bytes 11403268
  265.4 67.4 %collective-permute-start.10 = (bf16[4,928,256]{2,1,0:T(8,128)(2,1)}, bf16[4,928,256]{2,1,0:T(8,128)(2,1)}, u32[]{:S(2)}, u32[]{:S(2)}) collective-permute-start(bf16[4,928,256]{2,1,0:T(8,128)(2,1)} %add_convert_fusion.6), channel_id=1, source_target_pairs={{8,16},{16,8},{9,17},{17,9},{10,18},{18,10},{11,19},{19,11},{12,20... | collective-permute-start | bytes 5701640 | tf_op jit(solution)/shard_map/ppermute | solution.py:29
  270.6 71.7 %collective-permute-start.17 = (bf16[4,928,256]{2,1,0:T(8,128)(2,1)}, bf16[4,928,256]{2,1,0:T(8,128)(2,1)}, u32[]{:S(2)}, u32[]{:S(2)}) collective-permute-start(bf16[4,928,256]{2,1,0:T(8,128)(2,1)} %add_convert_fusion), channel_id=1, source_target_pairs={{8,0},{16,24},{9,1},{17,25},{10,2},{18,26},{11,3},{19,27},{12,4},{... | collective-permute-start | bytes 5701640 | tf_op jit(solution)/shard_map/ppermute | solution.py:29
  301.6 81.4 %collective-permute-start.15 = (bf16[4,928,256]{2,1,0:T(8,128)(2,1)}, bf16[4,928,256]{2,1,0:T(8,128)(2,1)}, u32[]{:S(2)}, u32[]{:S(2)}) collective-permute-start(bf16[4,928,256]{2,1,0:T(8,128)(2,1)} %add_convert_fusion.2), channel_id=1, source_target_pairs={{8,0},{16,24},{9,1},{17,25},{10,2},{18,26},{11,3},{19,27},{12,4},{... | collective-permute-start | bytes 5701640 | tf_op jit(solution)/shard_map/ppermute | solution.py:29
  371.9 40.6 %collective-permute-start.18 = (bf16[2,928,256]{2,1,0:T(8,128)(2,1)}, bf16[2,928,256]{2,1,0:T(8,128)(2,1)}, u32[]{:S(2)}, u32[]{:S(2)}) collective-permute-start(bf16[2,928,256]{2,1,0:T(8,128)(2,1)} %shard_map.119), channel_id=1, source_target_pairs={{8,0},{16,24},{9,1},{17,25},{10,2},{18,26},{11,3},{19,27},{12,4},{... | collective-permute-start | bytes 2850824 | tf_op jit(solution)/shard_map/ppermute | solution.py:29
  373.2 54.2 %collective-permute-start.13 = (bf16[2,928,256]{2,1,0:T(8,128)(2,1)}, bf16[2,928,256]{2,1,0:T(8,128)(2,1)S(1)}, u32[]{:S(2)}, u32[]{:S(2)}) collective-permute-start(bf16[2,928,256]{2,1,0:T(8,128)(2,1)} %get-tuple-element.44), channel_id=1, source_target_pairs={{8,0},{16,24},{9,1},{17,25},{10,2},{18,26},{11,3},{19,27},{12,4},{... | collective-permute-start | bytes 2850824 | tf_op jit(solution)/shard_map/ppermute | solution.py:29
  426.1 21.9 %collective-permute-start.20 = (bf16[2,256,2048]{2,1,0:T(8,128)(2,1)}, bf16[2,256,2048]{2,1,0:T(8,128)(2,1)}, u32[]{:S(2)}, u32[]{:S(2)}) collective-permute-start(bf16[2,256,2048]{2,1,0:T(8,128)(2,1)} %get-tuple-element.37), channel_id=1, source_target_pairs={{0,2},{1,3},{4,6},{5,7},{8,10},{9,11},{12,14},{13,15},{16,18},{17,... | collective-permute-start | bytes 6291464 | tf_op jit(solution)/shard_map/ppermute | solution.py:537
  427.4 0.9 copy-start.8
  441.8 12.6 %collective-permute-start.19 = (bf16[2,256,2048]{2,1,0:T(8,128)(2,1)}, bf16[2,256,2048]{2,1,0:T(8,128)(2,1)S(1)}, u32[]{:S(2)}, u32[]{:S(2)}) collective-permute-start(bf16[2,256,2048]{2,1,0:T(8,128)(2,1)} %get-tuple-element.36), channel_id=1, source_target_pairs={{2,0},{3,1},{6,4},{7,5},{10,8},{11,9},{14,12},{15,13},{18,16},{19,... | collective-permute-start | bytes 6291464 | tf_op jit(solution)/shard_map/ppermute | solution.py:537
  448.0 6.5 %copy-start.6 = (f32[2,256,2048]{2,1,0:T(8,128)S(1)}, f32[2,256,2048]{2,1,0:T(8,128)}, u32[]{:S(2)}) copy-start(f32[2,256,2048]{2,1,0:T(8,128)} %get-tuple-element.34) | copy-start | bytes 12582916
  451.3 16.1 %collective-permute-start.22 = (bf16[2,1,128,2048]{3,2,1,0:T(8,128)(2,1)}, bf16[2,1,128,2048]{3,2,1,0:T(8,128)(2,1)}, u32[]{:S(2)}, u32[]{:S(2)}) collective-permute-start(bf16[2,1,128,2048]{3,2,1,0:T(8,128)(2,1)} %fusion.4), channel_id=1, source_target_pairs={{2,3},{3,2},{6,7},{7,6},{10,11},{11,10},{14,15},{15,14},{18,19},{1... | collective-permute-start | bytes 3145736 | tf_op jit(solution)/shard_map/ppermute | solution.py:412
  454.4 1.6 copy-start.5
  456.1 17.0 %collective-permute-start.21 = (bf16[1,2,128,2048]{3,2,1,0:T(8,128)(2,1)}, bf16[1,2,128,2048]{3,2,1,0:T(8,128)(2,1)}, u32[]{:S(2)}, u32[]{:S(2)}) collective-permute-start(bf16[1,2,128,2048]{3,2,1,0:T(8,128)(2,1)} %fusion.3), channel_id=1, source_target_pairs={{0,4},{1,5},{4,0},{5,1},{8,12},{9,13},{12,8},{13,9},{16,20},{17,21... | collective-permute-start | bytes 3145736 | tf_op jit(solution)/shard_map/ppermute | solution.py:412
  469.9 15.2 %collective-permute-start.24 = (bf16[1,1,128,2048]{3,2,1,0:T(8,128)(2,1)}, bf16[1,1,128,2048]{3,2,1,0:T(8,128)(2,1)S(1)}, u32[]{:S(2)}, u32[]{:S(2)}) collective-permute-start(bf16[1,1,128,2048]{3,2,1,0:T(8,128)(2,1)} %fusion.6), channel_id=1, source_target_pairs={{2,6},{3,7},{6,2},{7,3},{10,14},{11,15},{14,10},{15,11},{18,22},{1... | collective-permute-start | bytes 1572872 | tf_op jit(solution)/shard_map/ppermute | solution.py:412
  475.5 9.6 %collective-permute-start.23 = (bf16[1,1,128,2048]{3,2,1,0:T(8,128)(2,1)}, bf16[1,1,128,2048]{3,2,1,0:T(8,128)(2,1)}, u32[]{:S(2)}, u32[]{:S(2)}) collective-permute-start(bf16[1,1,128,2048]{3,2,1,0:T(8,128)(2,1)} %fusion.7), channel_id=1, source_target_pairs={{0,1},{1,0},{4,5},{5,4},{8,9},{9,8},{12,13},{13,12},{16,17},{17,16... | collective-permute-start | bytes 1572872 | tf_op jit(solution)/shard_map/ppermute | solution.py:412
Sparse Core Ops, SparseCore 0:
  9.9 39.2 all-gather.2
  65.0 38.1 all-gather.4

commit v6 on v5

--- a/solution.py
+++ b/solution.py
@@ -254,23 +254,28 @@
     )(k, *args)
 
 
-def main_group(k, slots, sums, x_whole, wg, wu, acc, outs, a, size, total):
+def main_group(k, slots, sums, x_whole, wg, wu, acc, outs, a, cut, size, total):
     tokens, features = x_whole.shape
     count, _, width = slots[0].shape
     step = min(features, 512)
+    at, size = cut[0], size // cut[1]
+    base = a * cut[1] + at
     kept = pl.Buffered(1)
     gate = pl.BlockSpec(
-        (None, size, width), lambda i, k: (a % 2, 0, 0), pipeline_mode=kept
+        (None, size, width), lambda i, k: (a % 2, at, 0), pipeline_mode=kept
     )
     upper = pl.BlockSpec(
-        (None, size, width), lambda i, k: (2 + a % 2, 0, 0), pipeline_mode=kept
+        (None, size, width), lambda i, k: (2 + a % 2, at, 0), pipeline_mode=kept
     )
     wide = pl.BlockSpec(
+        (count, size, width), lambda i, k: (0, at, 0), pipeline_mode=kept
+    )
+    alone = pl.BlockSpec(
         (count, size, width), lambda i, k: (0, 0, 0), pipeline_mode=kept
     )
-    weight = pl.BlockSpec((size, step), lambda i, k: (a, i))
+    weight = pl.BlockSpec((size, step), lambda i, k: (base, i))
     tile = pl.BlockSpec((tokens, step), lambda i, k: (0, i))
-    specs = [gate] * 6 + [upper] * 6 + [wide] * 4 + [tile, weight, weight]
+    specs = [gate] * 6 + [upper] * 6 + [wide] * 3 + [alone, tile, weight, weight]
     args = list(slots) * 2 + list(sums) + [x_whole, wg, wu]
     aliases = {}
     if acc is not None:
@@ -310,7 +315,7 @@
 def token_group(k, factors, sums, r3, wg, wu, acc, q, a, size, total):
     tokens, features = acc.shape
     count, _, width = r3.shape
-    step = min(features, 512)
+    step = min(features, 1024)
     parts = tokens // (count * width)
 
     def split(value):
@@ -368,7 +373,7 @@
 def weight_group(grads, x_whole, out, a, size, after):
     tokens, features = x_whole.shape
     count, _, width = grads[0].shape
-    step = min(features, 512)
+    step = min(features, 1024)
     wide = pl.BlockSpec(
         (count, size, width), lambda i: (0, 0, 0), pipeline_mode=pl.Buffered(1)
     )
@@ -503,27 +508,38 @@
                     k, slots_of(a), grad_whole, down, a, size, total, a == last
                 )
 
-    def main(a, acc, wgrads):
-        sums = [part[a], swap[2 + a], middle[4 + a], swap[6 + a]]
+    def main(a, acc, wgrads, r3, cut=(0, 1)):
+        sums = [part[a], swap[2 + a], middle[4 + a], r3]
         args = (k, slots_of(a), sums, x_whole, wg, wu, acc, wgrads)
-        acc, *wgrads = main_group(*args, a, size, total)
+        acc, *wgrads = main_group(*args, a, cut, size, total)
         return acc, wgrads
 
     def pieces(value):
         return value.reshape((2, 2) + value.shape[1:])
 
     middle[6] = tie(middle[6], down)
-    swap.append(send(rounded(part[2], middle[6]), TO_ENDS))
-    acc, wgrads = main(0, acc, wgrads)
+    cuts = 1 if size % 32 else 2
+    rows = size // cuts
+    inner = []
+    for i in range(cuts):
+        cut = slice(i * rows, (i + 1) * rows)
+        payload = rounded(part[2][:, cut], middle[6][:, cut])
+        if i == 1:
+            acc, wgrads = main(0, acc, wgrads, swap[6])
+            payload = tie(payload, acc)
+        inner.append(send(payload, TO_ENDS))
+    if cuts == 1:
+        acc, wgrads = main(0, acc, wgrads, swap[6])
     middle[7] = tie(middle[7], acc)
     final = []
     for q in range(2):
         payload = rounded(pieces(part[last])[:, q], pieces(middle[7])[:, q])
         if q == 1:
-            acc, wgrads = main(1, acc, wgrads)
+            acc, wgrads = main(1, acc, wgrads, swap[7])
             payload = tie(payload, acc)
         final.append(send(payload, TO_ENDS))
-    acc, wgrads = main(2, acc, wgrads)
+    for i in range(cuts):
+        acc, wgrads = main(2, acc, wgrads, inner[i], (i, cuts))
     sums = [part[last], swap[2 + last], middle[4 + last]]
     gate_grads, up_grads, terms, plans = [], [], [], []
     for q in range(2):

time: 505 us -> 511 us (1.012)
  the two profiles are of different devices: /device:TPU:1 before, /device:TPU:21 now
where the time goes in v6:
time: 511 us; the launch traced here: 507 us
  Pallas kernels  219 us (43%)
  waiting for transfers between devices  141 us (28%)
  starting transfers between devices  65.2 us (13%)
  other arithmetic  63.6 us (12%)
  between operations  14.7 us (3%)
    ppermute x20, waiting for transfers between devices, send(): return lax.ppermute(value, 'inp', pairs)  110 us
    pallas_call x4, Pallas kernels, main_group(): pl.pallas_call(functools.partial(main_kernel, acc is not None), grid_spec...  94.7 us
    ppermute x20, starting transfers between devices, send(): return lax.ppermute(value, 'inp', pairs)  48.8 us
    pallas_call x4, Pallas kernels, down_group(): pl.pallas_call(functools.partial(down_kernel, factors), grid_spec=pltpu.P...  48 us
    pallas_call x4, Pallas kernels, sum_group(): pl.pallas_call(sum_kernel, grid=(blocks,), in_specs=[pl.BlockSpec((block,...  33.6 us
    convert_element_type x8, other arithmetic, rounded(): return (part + got.astype(jnp.float32)).astype(jnp.bfloat16)  29.7 us
    all_gather x1, waiting for transfers between devices, per_device(): lax.all_gather(out_grad, ('wt', 'dep'), axis=0, tiled=True)  27.6 us
    pallas_call x2, Pallas kernels, token_group(): pl.pallas_call(functools.partial(token_kernel, rows), grid_spec=pltpu.Pre...  26.7 us
  transfers between devices with their start and end apart: 28, of which 9 were waited for; matrix products, arithmetic and copies ran while one was open for 12% of the time, Pallas kernels for 43%

profile of v6, /device:TPU:21, one launch (start us, length us, event | category | flops | bytes accessed | tf_op | source)
XLA Modules:
  0.0 507.3 jit_solution(9428208195217752559)
XLA Ops:
  17.1 3.2 collective-permute-start.1
  20.3 27.6 %all-gather.3.cloned.1.call-done.grad_ref.refs_12_ = bf16[1024,2048]{1,0:T(8,128)(2,1)} async-done(((bf16[128,2048]{1,0:T(8,128)(2,1)}), bf16[1024,2048]{1,0:T(8,128)(2,1)}) %all-gather.3.cloned.1.call-update) | async-done | bytes 4194320 | tf_op jit(solution)/shard_map/all_gather | solution.py:479
  47.9 8.4 %shard_map.105.refs_1_.refs_12_ = f32[4,928,256]{2,1,0:T(8,128)} custom-call(bf16[3696,2048]{1,0:T(8,128)(2,1)} %w_ref.7, bf16[1024,2048]{1,0:T(8,128)(2,1)} %all-gather.3.cloned.1.call-done.grad_ref.refs_12_), custom_call_target="tpu_custom_call" | custom-call | flops 3892314112 | bytes 7602176 | tf_op jit(solution)/shard_map/pallas_call | solution.py:194
  58.5 4.2 convert_select_fusion.1
  63.1 8.4 %shard_map.102.refs_1_.refs_12_ = f32[4,928,256]{2,1,0:T(8,128)} custom-call(bf16[3696,2048]{1,0:T(8,128)(2,1)} %w_ref.7, bf16[1024,2048]{1,0:T(8,128)(2,1)} %all-gather.3.cloned.1.call-done.grad_ref.refs_12_), custom_call_target="tpu_custom_call" | custom-call | flops 3892314112 | bytes 7602176 | tf_op jit(solution)/shard_map/pallas_call | solution.py:194
  71.6 22.5 %collective-permute-done.refs_0_ = bf16[4,928,256]{2,1,0:T(8,128)(2,1)} collective-permute-done((bf16[4,928,256]{2,1,0:T(8,128)(2,1)}, bf16[4,928,256]{2,1,0:T(8,128)(2,1)}, u32[]{:S(2)}, u32[]{:S(2)}) %collective-permute-start) | collective-permute-done | bytes 1900576 | tf_op jit(solution)/shard_map/ppermute | solution.py:29
  97.0 4.1 convert_select_fusion.3
  101.1 8.4 %shard_map.107.refs_12_ = f32[4,928,256]{2,1,0:T(8,128)} custom-call(bf16[3696,2048]{1,0:T(8,128)(2,1)} %w_ref.7, bf16[1024,2048]{1,0:T(8,128)(2,1)} %all-gather.3.cloned.1.call-done.grad_ref.refs_12_), custom_call_target="tpu_custom_call" | custom-call | flops 3892314112 | bytes 7602176 | tf_op jit(solution)/shard_map/pallas_call | solution.py:194
  109.5 28.2 %collective-permute-done.8.refs_3_.refs_9_ = bf16[4,928,256]{2,1,0:T(8,128)(2,1)} collective-permute-done((bf16[4,928,256]{2,1,0:T(8,128)(2,1)}, bf16[4,928,256]{2,1,0:T(8,128)(2,1)}, u32[]{:S(2)}, u32[]{:S(2)}) %collective-permute-start.8) | collective-permute-done | bytes 1900576 | tf_op jit(solution)/shard_map/ppermute | solution.py:29
  137.7 4.3 convert_select_fusion
  142.0 3.2 add_convert_fusion.4
  148.1 8.4 %shard_map.104 = f32[4,928,256]{2,1,0:T(8,128)} custom-call(bf16[3696,2048]{1,0:T(8,128)(2,1)} %w_ref.7, bf16[1024,2048]{1,0:T(8,128)(2,1)} %all-gather.3.cloned.1.call-done.grad_ref.refs_12_), custom_call_target="tpu_custom_call" | custom-call | flops 3892314112 | bytes 7602176 | tf_op jit(solution)/shard_map/pallas_call | solution.py:194
  156.5 21.9 %collective-permute-done.3.refs_3_.refs_9_ = bf16[4,928,256]{2,1,0:T(8,128)(2,1)} collective-permute-done((bf16[4,928,256]{2,1,0:T(8,128)(2,1)}, bf16[4,928,256]{2,1,0:T(8,128)(2,1)}, u32[]{:S(2)}, u32[]{:S(2)}) %collective-permute-start.3) | collective-permute-done | bytes 1900576 | tf_op jit(solution)/shard_map/ppermute | solution.py:29
  178.4 4.3 convert_select_fusion.2
  182.7 3.4 add_convert_fusion.1
  188.4 27.9 %collective-permute-done.9.refs_4_.refs_10_.refs_13_ = bf16[4,928,256]{2,1,0:T(8,128)(2,1)} collective-permute-done((bf16[4,928,256]{2,1,0:T(8,128)(2,1)}, bf16[4,928,256]{2,1,0:T(8,128)(2,1)}, u32[]{:S(2)}, u32[]{:S(2)}) %collective-permute-start.9) | collective-permute-done | bytes 1900576 | tf_op jit(solution)/shard_map/ppermute | solution.py:29
  216.3 3.4 add_convert_fusion.2
  219.7 2.4 collective-permute-start.14
  222.1 3.2 add_convert_fusion.3
  225.4 4.3 collective-permute-start.12
  229.7 11.6 %shard_map.108.refs_13_ = bf16[3696,2048]{1,0:T(8,128)(2,1)} custom-call(s32[2]{0:T(128)} %pad_add_fusion.k_ref.refs_0_, bf16[4,928,256]{2,1,0:T(8,128)(2,1)} %pad_maximum_fusion.1.refs_0_.refs_6_, bf16[4,928,256]{2,1,0:T(8,128)(2,1)} %shard_map.106.refs_1_.refs_7_, bf16[4,928,256]{2,1,0:T(8,128)(2,1)} %collective-permute-done.7.refs_2_.refs_8_.refs_13_, ...), custom_call_target="tpu_custom_call" | custom-call | flops 3892314112 | bytes 7602176 | tf_op jit(solution)/shard_map/pallas_call | solution.py:233
  241.3 11.2 %shard_map.109.refs_1_.refs_13_ = bf16[3696,2048]{1,0:T(8,128)(2,1)} custom-call(s32[2]{0:T(128)} %pad_add_fusion.k_ref.refs_0_, bf16[4,928,256]{2,1,0:T(8,128)(2,1)} %pad_maximum_fusion.1.refs_0_.refs_6_, bf16[4,928,256]{2,1,0:T(8,128)(2,1)} %shard_map.106.refs_1_.refs_7_, ...), custom_call_target="tpu_custom_call", output_to_operand_aliasing={{}: (14, {})} | custom-call | flops 3892314112 | bytes 7602176 | tf_op jit(solution)/shard_map/pallas_call | solution.py:233
  252.5 4.5 collective-permute-done.4.refs_0_
  257.0 4.5 add_convert_fusion.5
  263.7 3.2 add_convert_fusion
  266.9 4.3 collective-permute-start.18
  271.2 11.6 %shard_map.111.refs_13_ = bf16[3696,2048]{1,0:T(8,128)(2,1)} custom-call(s32[2]{0:T(128)} %pad_add_fusion.k_ref.refs_0_, bf16[4,928,256]{2,1,0:T(8,128)(2,1)} %pad_maximum_fusion.refs_0_.refs_6_, bf16[4,928,256]{2,1,0:T(8,128)(2,1)} %shard_map.103.refs_1_.refs_7_, ...), custom_call_target="tpu_custom_call", output_to_operand_aliasing={{}: (14, {})} | custom-call | flops 3892314112 | bytes 7602176 | tf_op jit(solution)/shard_map/pallas_call | solution.py:233
  282.8 13.6 %shard_map.112 = (bf16[3696,2048]{1,0:T(8,128)(2,1)}, f32[4,928,256]{2,1,0:T(8,128)}, f32[4,928,256]{2,1,0:T(8,128)}) custom-call(s32[2]{0:T(128)} %pad_add_fusion.k_ref.refs_0_, bf16[4,928,256]{2,1,0:T(8,128)(2,1)} %pad_maximum_fusion.refs_0_.refs_6_, bf16[4,928,256]{2,1,0:T(8,128)(2,1)} %shard_map.103.refs_1_.refs_7_, ...), custom_call_target="tpu_custom_call", output_to_operand_aliasing={{0}: (14, {})} | custom-call | flops 3892314112 | bytes 7602176 | tf_op jit(solution)/shard_map/pallas_call | solution.py:233
  296.4 4.2 collective-permute-done.14.refs_0_
  300.6 4.3 fusion.2
  304.9 2.2 collective-permute-start.16
  307.2 28.9 %shard_map.113 = (f32[1024,2048]{1,0:T(8,128)}, bf16[3696,2048]{1,0:T(8,128)(2,1)}, bf16[3696,2048]{1,0:T(8,128)(2,1)}) custom-call(s32[2]{0:T(128)} %pad_add_fusion.k_ref.refs_0_, bf16[4,928,256]{2,1,0:T(8,128)(2,1)} %pad_maximum_fusion.1.refs_0_.refs_6_, bf16[4,928,256]{2,1,0:T(8,128)(2,1)} %shard_map.106.refs_1_.refs_7_, ...), custom_call_target="tpu_custom_call" | custom-call | flops 15569256448 | bytes 28508160 | tf_op jit(solution)/shard_map/pallas_call | solution.py:290
  336.2 14.1 %collective-permute-start.15 = (bf16[4,464,256]{2,1,0:T(8,128)(2,1)}, bf16[4,464,256]{2,1,0:T(8,128)(2,1)}, u32[]{:S(2)}, u32[]{:S(2)}) collective-permute-start(bf16[4,464,256]{2,1,0:T(8,128)(2,1)} %shard_map.116), channel_id=1, source_target_pairs={{8,0},{16,24},{9,1},{17,25},{10,2},{18,26},{11,3},{19,27},{12,4},{... | collective-permute-start | bytes 2850824 | tf_op jit(solution)/shard_map/ppermute | solution.py:29
  350.3 29.6 %shard_map.117 = (f32[1024,2048]{1,0:T(8,128)}, bf16[3696,2048]{1,0:T(8,128)(2,1)}, bf16[3696,2048]{1,0:T(8,128)(2,1)}) custom-call(s32[2]{0:T(128)} %pad_add_fusion.k_ref.refs_0_, bf16[4,928,256]{2,1,0:T(8,128)(2,1)} %pad_maximum_fusion.1.refs_0_.refs_6_, ...), custom_call_target="tpu_custom_call", output_to_operand_aliasing={{0}: (20, {}), {1}: (21, {}), {2}: (22, {})} | custom-call | flops 15569256448 | bytes 28508160 | tf_op jit(solution)/shard_map/pallas_call | solution.py:290
  379.9 4.4 fusion.10
  387.8 18.1 %shard_map.118 = (f32[1024,2048]{1,0:T(8,128)}, bf16[3696,2048]{1,0:T(8,128)(2,1)}, bf16[3696,2048]{1,0:T(8,128)(2,1)}) custom-call(s32[2]{0:T(128)} %pad_add_fusion.k_ref.refs_0_, bf16[4,928,256]{2,1,0:T(8,128)(2,1)} %pad_maximum_fusion.refs_0_.refs_6_, ...), custom_call_target="tpu_custom_call", output_to_operand_aliasing={{0}: (20, {}), {1}: (21, {}), {2}: (22, {})} | custom-call | flops 7784628224 | bytes 14254080 | tf_op jit(solution)/shard_map/pallas_call | solution.py:290
  406.0 18.1 %shard_map.119 = (f32[1024,2048]{1,0:T(8,128)}, bf16[3696,2048]{1,0:T(8,128)(2,1)}, bf16[3696,2048]{1,0:T(8,128)(2,1)}) custom-call(s32[2]{0:T(128)} %pad_add_fusion.k_ref.refs_0_, bf16[4,928,256]{2,1,0:T(8,128)(2,1)} %pad_maximum_fusion.refs_0_.refs_6_, ...), custom_call_target="tpu_custom_call", output_to_operand_aliasing={{0}: (20, {}), {1}: (21, {}), {2}: (22, {})} | custom-call | flops 7784628224 | bytes 14254080 | tf_op jit(solution)/shard_map/pallas_call | solution.py:290
  424.1 13.3 %shard_map.122 = (bf16[2,928,256]{2,1,0:T(8,128)(2,1)}, bf16[2,928,256]{2,1,0:T(8,128)(2,1)}, f32[2,256,2048]{2,1,0:T(8,128)}, bf16[2,256,2048]{2,1,0:T(8,128)(2,1)}) custom-call(s32[2]{0:T(128)} %pad_add_fusion.k_ref.refs_0_, f32[2,2,928,256]{3,2,1,0:T(8,128)} %bitcast.79, f32[2,2,928,256]{3,2,1,0:T(8,128)} %bitcast.81, f32[2,2,928,256]{3,2,1,0:T(8,128)} %bitcast.77, ...), custom_call_target="tpu_custom_call" | custom-call | flops 3892314112 | bytes 18055168 | tf_op jit(solution)/shard_map/pallas_call | solution.py:335
  439.6 13.4 %shard_map.120 = (bf16[2,928,256]{2,1,0:T(8,128)(2,1)}, bf16[2,928,256]{2,1,0:T(8,128)(2,1)}, f32[2,256,2048]{2,1,0:T(8,128)}, bf16[2,256,2048]{2,1,0:T(8,128)(2,1)}) custom-call(s32[2]{0:T(128)} %pad_add_fusion.k_ref.refs_0_, f32[2,2,928,256]{3,2,1,0:T(8,128)} %bitcast.80, f32[2,2,928,256]{3,2,1,0:T(8,128)} %bitcast.82, f32[2,2,928,256]{3,2,1,0:T(8,128)} %bitcast.78, ...), custom_call_target="tpu_custom_call" | custom-call | flops 3892314112 | bytes 18055168 | tf_op jit(solution)/shard_map/pallas_call | solution.py:335
  453.0 6.7 %collective-permute-start.20 = (bf16[2,256,2048]{2,1,0:T(8,128)(2,1)}, bf16[2,256,2048]{2,1,0:T(8,128)(2,1)S(1)}, u32[]{:S(2)}, u32[]{:S(2)}) collective-permute-start(bf16[2,256,2048]{2,1,0:T(8,128)(2,1)} %get-tuple-element.42), channel_id=1, source_target_pairs={{2,0},{3,1},{6,4},{7,5},{10,8},{11,9},{14,12},{15,13},{18,16},{19,... | collective-permute-start | bytes 6291464 | tf_op jit(solution)/shard_map/ppermute | solution.py:553
  459.8 3.3 fusion.6
  468.5 7.9 %shard_map.123.refs_1_ = bf16[3696,2048]{1,0:T(8,128)(2,1)} custom-call(bf16[2,928,256]{2,1,0:T(8,128)(2,1)} %get-tuple-element.44.refs_0_, bf16[2,928,256]{2,1,0:T(8,128)(2,1)} %get-tuple-element.45.refs_1_, bf16[1024,2048]{1,0:T(8,128)(2,1)} %all-gather.5.cloned.1.call-done.refs_16_.refs_2_, ...), custom_call_target="tpu_custom_call", output_to_operand_aliasing={{}: (3, {})} | custom-call | flops 3892314112 | bytes 5701632 | tf_op jit(solution)/shard_map/pallas_call | solution.py:380
  476.4 2.8 collective-permute-done.23.refs_0_
  479.2 2.5 fusion.8
  481.7 3.1 collective-permute-start.25
  484.8 2.5 fusion.9
  488.8 7.9 %shard_map.126 = bf16[3696,2048]{1,0:T(8,128)(2,1)} custom-call(bf16[2,928,256]{2,1,0:T(8,128)(2,1)} %get-tuple-element.47.refs_0_, bf16[2,928,256]{2,1,0:T(8,128)(2,1)} %get-tuple-element.48.refs_1_, bf16[1024,2048]{1,0:T(8,128)(2,1)} %all-gather.5.cloned.1.call-done.refs_16_.refs_2_, ...), custom_call_target="tpu_custom_call", output_to_operand_aliasing={{}: (3, {})} | custom-call | flops 3892314112 | bytes 5701632 | tf_op jit(solution)/shard_map/pallas_call | solution.py:380
  496.7 3.6 fusion.7
  (79 shorter events, 35.2 us)
Async XLA Ops:
  7.2 2.0 copy-start.7
  7.2 40.7 %all-gather.3.cloned.1.call-start = ((), (), s32[]{:S(2)}) async-start(), calls=%async_computation | async-start | bytes 4718592 | tf_op jit(solution)/shard_map/all_gather | solution.py:479
  7.9 299.3 %all-gather.5.cloned.1.call-start = ((), (), s32[]{:S(2)}) async-start(), calls=%async_computation.1 | async-start | bytes 4718592 | tf_op jit(solution)/shard_map/all_gather | solution.py:478
  10.8 45.5 %collective-permute-start.5 = (bf16[4,928,256]{2,1,0:T(8,128)(2,1)}, bf16[4,928,256]{2,1,0:T(8,128)(2,1)}, u32[]{:S(2)}, u32[]{:S(2)}) collective-permute-start(bf16[4,928,256]{2,1,0:T(8,128)(2,1)} %pad_maximum_fusion.1.refs_0_.refs_6_), channel_id=1, source_target_pairs={{0,8},{8,0},{16,24},{24,16},{1,9},{9,1},{17,25},{25,17},{2,10},{10... | collective-permute-start | bytes 5701640 | tf_op jit(solution)/shard_map/ppermute | solution.py:29
  12.1 46.4 %collective-permute-start.6 = (bf16[4,928,256]{2,1,0:T(8,128)(2,1)}, bf16[4,928,256]{2,1,0:T(8,128)(2,1)}, u32[]{:S(2)}, u32[]{:S(2)}) collective-permute-start(bf16[4,928,256]{2,1,0:T(8,128)(2,1)} %pad_maximum_fusion.1.refs_0_.refs_6_), channel_id=1, source_target_pairs={{8,16},{16,8},{9,17},{17,9},{10,18},{18,10},{11,19},{19,11},{12,20... | collective-permute-start | bytes 5701640 | tf_op jit(solution)/shard_map/ppermute | solution.py:29
  16.9 77.2 %collective-permute-start = (bf16[4,928,256]{2,1,0:T(8,128)(2,1)}, bf16[4,928,256]{2,1,0:T(8,128)(2,1)}, u32[]{:S(2)}, u32[]{:S(2)}) collective-permute-start(bf16[4,928,256]{2,1,0:T(8,128)(2,1)} %pad_maximum_fusion.refs_0_.refs_6_), channel_id=1, source_target_pairs={{0,8},{8,0},{16,24},{24,16},{1,9},{9,1},{17,25},{25,17},{2,10},{10... | collective-permute-start | bytes 5701640 | tf_op jit(solution)/shard_map/ppermute | solution.py:29
  17.1 79.9 %collective-permute-start.1 = (bf16[4,928,256]{2,1,0:T(8,128)(2,1)}, bf16[4,928,256]{2,1,0:T(8,128)(2,1)}, u32[]{:S(2)}, u32[]{:S(2)}) collective-permute-start(bf16[4,928,256]{2,1,0:T(8,128)(2,1)} %pad_maximum_fusion.refs_0_.refs_6_), channel_id=1, source_target_pairs={{8,16},{16,8},{9,17},{17,9},{10,18},{18,10},{11,19},{19,11},{12,20... | collective-permute-start | bytes 5701640 | tf_op jit(solution)/shard_map/ppermute | solution.py:29
  56.3 81.4 %collective-permute-start.8 = (bf16[4,928,256]{2,1,0:T(8,128)(2,1)}, bf16[4,928,256]{2,1,0:T(8,128)(2,1)}, u32[]{:S(2)}, u32[]{:S(2)}) collective-permute-start(bf16[4,928,256]{2,1,0:T(8,128)(2,1)} %shard_map.106.refs_1_.refs_7_), channel_id=1, source_target_pairs={{8,16},{16,8},{9,17},{17,9},{10,18},{18,10},{11,19},{19,11},{12,20... | collective-permute-start | bytes 5701640 | tf_op jit(solution)/shard_map/ppermute | solution.py:29
  62.6 79.4 %collective-permute-start.7 = (bf16[4,928,256]{2,1,0:T(8,128)(2,1)}, bf16[4,928,256]{2,1,0:T(8,128)(2,1)}, u32[]{:S(2)}, u32[]{:S(2)}) collective-permute-start(bf16[4,928,256]{2,1,0:T(8,128)(2,1)} %convert_select_fusion.1), channel_id=1, source_target_pairs={{0,8},{8,0},{16,24},{24,16},{1,9},{9,1},{17,25},{25,17},{2,10},{10... | collective-permute-start | bytes 5701640 | tf_op jit(solution)/shard_map/ppermute | solution.py:29
  94.1 84.3 %collective-permute-start.3 = (bf16[4,928,256]{2,1,0:T(8,128)(2,1)}, bf16[4,928,256]{2,1,0:T(8,128)(2,1)}, u32[]{:S(2)}, u32[]{:S(2)}) collective-permute-start(bf16[4,928,256]{2,1,0:T(8,128)(2,1)} %shard_map.103.refs_1_.refs_7_), channel_id=1, source_target_pairs={{8,16},{16,8},{9,17},{17,9},{10,18},{18,10},{11,19},{19,11},{12,20... | collective-permute-start | bytes 5701640 | tf_op jit(solution)/shard_map/ppermute | solution.py:29
  101.1 81.6 %collective-permute-start.2 = (bf16[4,928,256]{2,1,0:T(8,128)(2,1)}, bf16[4,928,256]{2,1,0:T(8,128)(2,1)}, u32[]{:S(2)}, u32[]{:S(2)}) collective-permute-start(bf16[4,928,256]{2,1,0:T(8,128)(2,1)} %convert_select_fusion.3), channel_id=1, source_target_pairs={{0,8},{8,0},{16,24},{24,16},{1,9},{9,1},{17,25},{25,17},{2,10},{10... | collective-permute-start | bytes 5701640 | tf_op jit(solution)/shard_map/ppermute | solution.py:29
  137.7 4.3 copy-start.3
  142.0 74.3 %collective-permute-start.9 = (bf16[4,928,256]{2,1,0:T(8,128)(2,1)}, bf16[4,928,256]{2,1,0:T(8,128)(2,1)}, u32[]{:S(2)}, u32[]{:S(2)}) collective-permute-start(bf16[4,928,256]{2,1,0:T(8,128)(2,1)} %convert_select_fusion), channel_id=1, source_target_pairs={{0,8},{8,0},{16,24},{24,16},{1,9},{9,1},{17,25},{25,17},{2,10},{10... | collective-permute-start | bytes 5701640 | tf_op jit(solution)/shard_map/ppermute | solution.py:29
  145.2 76.9 %collective-permute-start.11 = (bf16[4,928,256]{2,1,0:T(8,128)(2,1)}, bf16[4,928,256]{2,1,0:T(8,128)(2,1)}, u32[]{:S(2)}, u32[]{:S(2)}) collective-permute-start(bf16[4,928,256]{2,1,0:T(8,128)(2,1)} %add_convert_fusion.4), channel_id=1, source_target_pairs={{8,16},{16,8},{9,17},{17,9},{10,18},{18,10},{11,19},{19,11},{12,20... | collective-permute-start | bytes 5701640 | tf_op jit(solution)/shard_map/ppermute | solution.py:29
  178.4 4.3 copy-start.1
  182.7 74.3 %collective-permute-start.4 = (bf16[4,928,256]{2,1,0:T(8,128)(2,1)}, bf16[4,928,256]{2,1,0:T(8,128)(2,1)}, u32[]{:S(2)}, u32[]{:S(2)}) collective-permute-start(bf16[4,928,256]{2,1,0:T(8,128)(2,1)} %convert_select_fusion.2), channel_id=1, source_target_pairs={{0,8},{8,0},{16,24},{24,16},{1,9},{9,1},{17,25},{25,17},{2,10},{10... | collective-permute-start | bytes 5701640 | tf_op jit(solution)/shard_map/ppermute | solution.py:29
  182.7 33.6 %copy-start = (f32[4,928,256]{2,1,0:T(8,128)S(1)}, f32[4,928,256]{2,1,0:T(8,128)}, u32[]{:S(2)}) copy-start(f32[4,928,256]{2,1,0:T(8,128)} %shard_map.107.refs_12_) | copy-start | bytes 11403268
  186.1 77.5 %collective-permute-start.17 = (bf16[4,928,256]{2,1,0:T(8,128)(2,1)}, bf16[4,928,256]{2,1,0:T(8,128)(2,1)}, u32[]{:S(2)}, u32[]{:S(2)}) collective-permute-start(bf16[4,928,256]{2,1,0:T(8,128)(2,1)} %add_convert_fusion.1), channel_id=1, source_target_pairs={{8,16},{16,8},{9,17},{17,9},{10,18},{18,10},{11,19},{19,11},{12,20... | collective-permute-start | bytes 5701640 | tf_op jit(solution)/shard_map/ppermute | solution.py:29
  216.3 5.8 %copy-start.4 = (f32[4,928,256]{2,1,0:T(8,128)S(1)}, f32[4,928,256]{2,1,0:T(8,128)}, u32[]{:S(2)}) copy-start(f32[4,928,256]{2,1,0:T(8,128)} %shard_map.105.refs_1_.refs_12_) | copy-start | bytes 11403268
  219.7 80.9 %collective-permute-start.14 = (bf16[4,928,256]{2,1,0:T(8,128)(2,1)}, bf16[4,928,256]{2,1,0:T(8,128)(2,1)}, u32[]{:S(2)}, u32[]{:S(2)}) collective-permute-start(bf16[4,928,256]{2,1,0:T(8,128)(2,1)} %add_convert_fusion.2), channel_id=1, source_target_pairs={{8,16},{16,8},{9,17},{17,9},{10,18},{18,10},{11,19},{19,11},{12,20... | collective-permute-start | bytes 5701640 | tf_op jit(solution)/shard_map/ppermute | solution.py:29
  225.4 81.8 %collective-permute-start.12 = (bf16[4,928,256]{2,1,0:T(8,128)(2,1)}, bf16[4,928,256]{2,1,0:T(8,128)(2,1)}, u32[]{:S(2)}, u32[]{:S(2)}) collective-permute-start(bf16[4,928,256]{2,1,0:T(8,128)(2,1)} %add_convert_fusion.3), channel_id=1, source_target_pairs={{8,0},{16,24},{9,1},{17,25},{10,2},{18,26},{11,3},{19,27},{12,4},{... | collective-permute-start | bytes 5701640 | tf_op jit(solution)/shard_map/ppermute | solution.py:29
  257.0 6.6 %copy-start.2 = (f32[4,928,256]{2,1,0:T(8,128)S(1)}, f32[4,928,256]{2,1,0:T(8,128)}, u32[]{:S(2)}) copy-start(f32[4,928,256]{2,1,0:T(8,128)} %shard_map.102.refs_1_.refs_12_) | copy-start | bytes 11403268
  261.6 88.8 %collective-permute-start.10 = (bf16[4,928,256]{2,1,0:T(8,128)(2,1)}, bf16[4,928,256]{2,1,0:T(8,128)(2,1)}, u32[]{:S(2)}, u32[]{:S(2)}) collective-permute-start(bf16[4,928,256]{2,1,0:T(8,128)(2,1)} %add_convert_fusion.5), channel_id=1, source_target_pairs={{8,16},{16,8},{9,17},{17,9},{10,18},{18,10},{11,19},{19,11},{12,20... | collective-permute-start | bytes 5701640 | tf_op jit(solution)/shard_map/ppermute | solution.py:29
  266.9 83.4 %collective-permute-start.18 = (bf16[4,928,256]{2,1,0:T(8,128)(2,1)}, bf16[4,928,256]{2,1,0:T(8,128)(2,1)}, u32[]{:S(2)}, u32[]{:S(2)}) collective-permute-start(bf16[4,928,256]{2,1,0:T(8,128)(2,1)} %add_convert_fusion), channel_id=1, source_target_pairs={{8,0},{16,24},{9,1},{17,25},{10,2},{18,26},{11,3},{19,27},{12,4},{... | collective-permute-start | bytes 5701640 | tf_op jit(solution)/shard_map/ppermute | solution.py:29
  304.9 82.9 %collective-permute-start.16 = (bf16[4,464,256]{2,1,0:T(8,128)(2,1)}, bf16[4,464,256]{2,1,0:T(8,128)(2,1)}, u32[]{:S(2)}, u32[]{:S(2)}) collective-permute-start(bf16[4,464,256]{2,1,0:T(8,128)(2,1)} %get-tuple-element.52), channel_id=1, source_target_pairs={{8,0},{16,24},{9,1},{17,25},{10,2},{18,26},{11,3},{19,27},{12,4},{... | collective-permute-start | bytes 2850824 | tf_op jit(solution)/shard_map/ppermute | solution.py:29
  336.2 69.8 %collective-permute-start.15 = (bf16[4,464,256]{2,1,0:T(8,128)(2,1)}, bf16[4,464,256]{2,1,0:T(8,128)(2,1)}, u32[]{:S(2)}, u32[]{:S(2)}) collective-permute-start(bf16[4,464,256]{2,1,0:T(8,128)(2,1)} %shard_map.116), channel_id=1, source_target_pairs={{8,0},{16,24},{9,1},{17,25},{10,2},{18,26},{11,3},{19,27},{12,4},{... | collective-permute-start | bytes 2850824 | tf_op jit(solution)/shard_map/ppermute | solution.py:29
  384.3 39.8 %collective-permute-start.19 = (bf16[2,928,256]{2,1,0:T(8,128)(2,1)}, bf16[2,928,256]{2,1,0:T(8,128)(2,1)}, u32[]{:S(2)}, u32[]{:S(2)}) collective-permute-start(bf16[2,928,256]{2,1,0:T(8,128)(2,1)} %shard_map.121), channel_id=1, source_target_pairs={{8,0},{16,24},{9,1},{17,25},{10,2},{18,26},{11,3},{19,27},{12,4},{... | collective-permute-start | bytes 2850824 | tf_op jit(solution)/shard_map/ppermute | solution.py:29
  386.5 52.2 %collective-permute-start.13 = (bf16[2,928,256]{2,1,0:T(8,128)(2,1)}, bf16[2,928,256]{2,1,0:T(8,128)(2,1)S(1)}, u32[]{:S(2)}, u32[]{:S(2)}) collective-permute-start(bf16[2,928,256]{2,1,0:T(8,128)(2,1)} %get-tuple-element.50), channel_id=1, source_target_pairs={{8,0},{16,24},{9,1},{17,25},{10,2},{18,26},{11,3},{19,27},{12,4},{... | collective-permute-start | bytes 2850824 | tf_op jit(solution)/shard_map/ppermute | solution.py:29
  437.4 22.4 %collective-permute-start.21 = (bf16[2,256,2048]{2,1,0:T(8,128)(2,1)}, bf16[2,256,2048]{2,1,0:T(8,128)(2,1)}, u32[]{:S(2)}, u32[]{:S(2)}) collective-permute-start(bf16[2,256,2048]{2,1,0:T(8,128)(2,1)} %get-tuple-element.43), channel_id=1, source_target_pairs={{0,2},{1,3},{4,6},{5,7},{8,10},{9,11},{12,14},{13,15},{16,18},{17,... | collective-permute-start | bytes 6291464 | tf_op jit(solution)/shard_map/ppermute | solution.py:553
  438.7 0.9 copy-start.8
  453.0 12.2 %collective-permute-start.20 = (bf16[2,256,2048]{2,1,0:T(8,128)(2,1)}, bf16[2,256,2048]{2,1,0:T(8,128)(2,1)S(1)}, u32[]{:S(2)}, u32[]{:S(2)}) collective-permute-start(bf16[2,256,2048]{2,1,0:T(8,128)(2,1)} %get-tuple-element.42), channel_id=1, source_target_pairs={{2,0},{3,1},{6,4},{7,5},{10,8},{11,9},{14,12},{15,13},{18,16},{19,... | collective-permute-start | bytes 6291464 | tf_op jit(solution)/shard_map/ppermute | solution.py:553
  459.8 5.4 %copy-start.6 = (f32[2,256,2048]{2,1,0:T(8,128)S(1)}, f32[2,256,2048]{2,1,0:T(8,128)}, u32[]{:S(2)}) copy-start(f32[2,256,2048]{2,1,0:T(8,128)} %get-tuple-element.40) | copy-start | bytes 12582916
  463.1 16.1 %collective-permute-start.23 = (bf16[2,1,128,2048]{3,2,1,0:T(8,128)(2,1)}, bf16[2,1,128,2048]{3,2,1,0:T(8,128)(2,1)}, u32[]{:S(2)}, u32[]{:S(2)}) collective-permute-start(bf16[2,1,128,2048]{3,2,1,0:T(8,128)(2,1)} %fusion.6), channel_id=1, source_target_pairs={{2,3},{3,2},{6,7},{7,6},{10,11},{11,10},{14,15},{15,14},{18,19},{1... | collective-permute-start | bytes 3145736 | tf_op jit(solution)/shard_map/ppermute | solution.py:417
  465.2 1.6 copy-start.5
  466.8 18.0 %collective-permute-start.22 = (bf16[1,2,128,2048]{3,2,1,0:T(8,128)(2,1)}, bf16[1,2,128,2048]{3,2,1,0:T(8,128)(2,1)}, u32[]{:S(2)}, u32[]{:S(2)}) collective-permute-start(bf16[1,2,128,2048]{3,2,1,0:T(8,128)(2,1)} %fusion.5), channel_id=1, source_target_pairs={{0,4},{1,5},{4,0},{5,1},{8,12},{9,13},{12,8},{13,9},{16,20},{17,21... | collective-permute-start | bytes 3145736 | tf_op jit(solution)/shard_map/ppermute | solution.py:417
  481.7 15.0 %collective-permute-start.25 = (bf16[1,1,128,2048]{3,2,1,0:T(8,128)(2,1)}, bf16[1,1,128,2048]{3,2,1,0:T(8,128)(2,1)S(1)}, u32[]{:S(2)}, u32[]{:S(2)}) collective-permute-start(bf16[1,1,128,2048]{3,2,1,0:T(8,128)(2,1)} %fusion.8), channel_id=1, source_target_pairs={{2,6},{3,7},{6,2},{7,3},{10,14},{11,15},{14,10},{15,11},{18,22},{1... | collective-permute-start | bytes 1572872 | tf_op jit(solution)/shard_map/ppermute | solution.py:417
  487.3 9.4 %collective-permute-start.24 = (bf16[1,1,128,2048]{3,2,1,0:T(8,128)(2,1)}, bf16[1,1,128,2048]{3,2,1,0:T(8,128)(2,1)}, u32[]{:S(2)}, u32[]{:S(2)}) collective-permute-start(bf16[1,1,128,2048]{3,2,1,0:T(8,128)(2,1)} %fusion.9), channel_id=1, source_target_pairs={{0,1},{1,0},{4,5},{5,4},{8,9},{9,8},{12,13},{13,12},{16,17},{17,16... | collective-permute-start | bytes 1572872 | tf_op jit(solution)/shard_map/ppermute | solution.py:417
Sparse Core Ops, SparseCore 0:
  9.9 37.9 all-gather.2
  49.8 36.7 all-gather.4
